TPU v7x, 128 devices: a whole 4x4x4 slice. The times are simulated.
128 devices in a mesh: head: 4 (over z), blk: 32 (over y, x, core).
Axes of the slice: x: 4, y: 4, z: 4, core: 2. Of those that a mesh axis runs over, the one named last changes fastest.
Arguments:
- tokens: bfloat16 [32, 512, 2048], P('blk', 'head'), may hold values from -6 to 6
- segments: int32 [32, 512], replicated, may hold values from 0 to 15, as said below
- w_query: bfloat16 [2048, 2048], P('blk', 'head'), may hold values from -0.125 to 0.125
- key_projection: bfloat16 [2048, 256], P('blk', 'head'), may hold values from -0.125 to 0.125
- value_projection: bfloat16 [2048, 256], P('blk', 'head'), may hold values from -0.125 to 0.125
- w_out: bfloat16 [2048, 2048], P('head', 'blk'), may hold values from -1.5 to 1.5
- w_gate: bfloat16 [2048, 5632], P('blk', 'head'), may hold values from -0.125 to 0.125
- w_up: bfloat16 [2048, 5632], P('blk', 'head'), may hold values from -0.125 to 0.125
- w_down: bfloat16 [5632, 2048], P('head', 'blk'), may hold values from -0.078125 to 0.078125
- norm_attn: bfloat16 [2048], replicated, may hold values from 0.099609375 to 1.8984375
- norm_ffn: bfloat16 [2048], replicated, may hold values from 0.099609375 to 1.8984375
- cotangent: bfloat16 [32, 512, 2048], P('blk', 'head'), may hold values from -6 to 6
Outputs:
- output: bfloat16 [32, 512, 2048], P('blk', 'head')
- grad_tokens: bfloat16 [32, 512, 2048], P('blk', 'head')
- grad_w_query: float32 [2048, 2048], P('blk', 'head')
- grad_w_key: float32 [2048, 256], P('blk', 'head')
- grad_w_value: float32 [2048, 256], P('blk', 'head')
- grad_w_out: float32 [2048, 2048], P('head', 'blk')
- grad_w_gate: float32 [2048, 5632], P('blk', 'head')
- grad_w_up: float32 [2048, 5632], P('blk', 'head')
- grad_w_down: float32 [5632, 2048], P('head', 'blk')
- grad_norm_attn: float32 [2048], replicated
- grad_norm_ffn: float32 [2048], replicated
Inputs may be any that keep to these rules, and one draw needn't show every extreme that they name: `segments`: read in order of blocks and rows, the document numbers never fall; they begin at 0 and end at 15.
All inputs are finite; a program needn't handle non-finite values.
Results may differ from a plain program's by a relative error of at most 0.025.
Values may be sent and summed in bfloat16 or wider, within the bound.
No kernel may reach another device: no remote copies, remote signals or barrier semaphores. Data moves between devices by JAX's collectives and lax.ppermute only.
A program may use at most 192 MiB of HBM per device.

v0:
```python
import functools

import jax
import jax.numpy as jnp
from jax import lax
from jax.experimental import pallas as pl
from jax.experimental.pallas import tpu as pltpu
from jax.sharding import Mesh
from jax.sharding import PartitionSpec as P

HEAD_SIZE = 64
WINDOW = 1024
HIDDEN = 1408
EPSILON = 1e-05
BF16 = jnp.bfloat16
F32 = jnp.float32
BLK = ("y", "x", "core")
CORE_FIRST = ("core", "y", "x")
VMEM_LIMIT = 63 * 1024 * 1024


def dot_nn(a, b):
    return jnp.dot(a, b, preferred_element_type=F32)


def dot_nt(a, b):
    return lax.dot_general(a, b, (((1,), (1,)), ((), ())), preferred_element_type=F32)


def dot_tn(a, b):
    return lax.dot_general(a, b, (((0,), (0,)), ((), ())), preferred_element_type=F32)


def shift(value, axis, distance):
    size = lax.axis_size(axis)
    return lax.ppermute(value, axis, [(i, (i + distance) % size) for i in range(size)])


def add_low(a, b):
    return (a.astype(F32) + b.astype(F32)).astype(BF16)


def gather_pieces(rows):
    return shift(rows, "head", -1), shift(rows, "head", 2), shift(rows, "head", 1)


def near_pieces(rows):
    return shift(rows, "head", -1), shift(rows, "head", 1)


def far_pieces(ahead, behind):
    half = ahead.shape[0] // 2
    return shift(behind[:half], "head", 1), shift(ahead[half:], "head", -1)


def scatter_pieces(own, ahead, far, behind):
    return own, shift(ahead, "head", 1), shift(behind, "head", -1), shift(far, "head", 2)


def gather_axis(value, axis):
    return value, shift(value, axis, -1), shift(value, axis, 2), shift(value, axis, 1)


def exchange(pieces, axis):
    return pieces[0], shift(pieces[1], axis, 1), shift(pieces[2], axis, 2), shift(pieces[3], axis, -1)


def from_block(value, distance):
    route = [(i, i + distance) for i in range(32) if 0 <= i + distance < 32]
    return lax.ppermute(value, BLK, route)


def scale_of(values):
    return lax.rsqrt(jnp.mean(values * values, -1, keepdims=True) + EPSILON)


def x_of(code):
    return lax.shift_right_logical(code[0], 5)


def y_of(code):
    return lax.shift_right_logical(code[0], 3) & 3


def core_of(code):
    return lax.shift_right_logical(code[0], 2) & 1


def place_of(code):
    return code[0] & 3


def lane_is_low(shape, period):
    return lax.broadcasted_iota(jnp.int32, shape, len(shape) - 1) % period < period // 2


def turn(values, cosine, sine):
    swapped = jnp.where(
        lane_is_low(values.shape, 64), pltpu.roll(values, 96, 1), pltpu.roll(values, 32, 1)
    )
    return values * cosine + swapped * sine


def core_major_tiles(tiles):
    low = lane_is_low(tiles[0].shape, 128)
    rolled = [pltpu.roll(tile, 64, 1) for tile in tiles]
    first = [jnp.where(low, tiles[2 * k], rolled[2 * k + 1]) for k in range(8)]
    second = [jnp.where(low, rolled[2 * k], tiles[2 * k + 1]) for k in range(8)]
    return first + second


def block_major_tiles(tiles):
    low = lane_is_low(tiles[0].shape, 128)
    rolled = [pltpu.roll(tile, 64, 1) for tile in tiles]
    result = []
    for k in range(8):
        result.append(jnp.where(low, tiles[k], rolled[8 + k]))
        result.append(jnp.where(low, rolled[k], tiles[8 + k]))
    return result


def in_tiles(value):
    return [value[:, 128 * k : 128 * k + 128] for k in range(16)]


def prepare_kernel(x_ref, dy_ref, gain_ref, x_out, dy_out, normed_out, gain_out):
    def convert(ref):
        return jnp.concatenate(core_major_tiles(in_tiles(ref[...].astype(F32))), 1)

    x, gains = convert(x_ref), convert(gain_ref)
    gain_out[...] = gains
    x_out[...] = x
    dy_out[...] = convert(dy_ref).astype(BF16)
    normed_out[...] = (x * scale_of(x) * gains[:1]).astype(BF16)


def prepare(x, dy, gains):
    rows, width = x.shape
    return pl.pallas_call(
        prepare_kernel,
        out_shape=(
            jax.ShapeDtypeStruct((rows, width), F32),
            jax.ShapeDtypeStruct((rows, width), BF16),
            jax.ShapeDtypeStruct((rows, width), BF16),
            jax.ShapeDtypeStruct(gains.shape, F32),
        ),
        compiler_params=pltpu.CompilerParams(vmem_limit_bytes=VMEM_LIMIT),
        cost_estimate=pl.CostEstimate(
            flops=10 * rows * width, bytes_accessed=10 * rows * width, transcendentals=rows
        ),
    )(x, dy, gains)


def to_blocks(value):
    return jnp.concatenate(block_major_tiles(in_tiles(value)), 1)


def assemble_kernel(core_ref, own_ref, ahead_ref, far_ref, behind_ref, out_ref, swap_ref):
    out_ref[:128] = own_ref[...]
    start = 128
    for ref in (ahead_ref, far_ref, behind_ref):
        size = ref.shape[0]
        out_ref[start : start + size] = jnp.concatenate(
            core_major_tiles(in_tiles(ref[...].astype(F32))), 1
        ).astype(BF16)
        start += size
    swap_ref[...] = jnp.where(core_of(core_ref) == 0, out_ref[:, 1024:], out_ref[:, :1024])


def assemble(core, own, ahead, far, behind):
    vmem = pl.BlockSpec(memory_space=pltpu.VMEM)
    return pl.pallas_call(
        assemble_kernel,
        out_shape=(jax.ShapeDtypeStruct((512, 2048), BF16), jax.ShapeDtypeStruct((512, 1024), BF16)),
        in_specs=[pl.BlockSpec(memory_space=pltpu.SMEM)] + [vmem] * 4,
        out_specs=(vmem, vmem),
        compiler_params=pltpu.CompilerParams(vmem_limit_bytes=VMEM_LIMIT),
        cost_estimate=pl.CostEstimate(
            flops=4 * 512 * 2048, bytes_accessed=5 * 1024 * 1024, transcendentals=0
        ),
    )(core, own, ahead, far, behind)


def small_call(kernel, out_shape, *operands):
    return pl.pallas_call(
        kernel,
        out_shape=tuple(jax.ShapeDtypeStruct(shape, dtype) for shape, dtype in out_shape),
        compiler_params=pltpu.CompilerParams(vmem_limit_bytes=VMEM_LIMIT),
        cost_estimate=pl.CostEstimate(
            flops=sum(x.size for x in operands),
            bytes_accessed=2 * sum(x.size * x.dtype.itemsize for x in operands),
            transcendentals=0,
        ),
    )(*operands)


def total_of(refs):
    values = [ref[...].astype(F32) for ref in refs]
    while len(values) > 1:
        values = [values[0] + values[1]] + values[2:]
    return values[0]


def join_kernel(x_ref, gain_ref, a_ref, b_ref, c_ref, d_ref, h_out, top_out, bottom_out):
    h = x_ref[...] + total_of((a_ref, b_ref, c_ref, d_ref))
    h_out[...] = h
    normed = (h * scale_of(h) * gain_ref[1:2]).astype(BF16)
    half = h.shape[0] // 2
    top_out[...], bottom_out[...] = normed[:half], normed[half:]


def join(x, gain, pieces):
    half = x.shape[0] // 2, x.shape[1]
    return small_call(join_kernel, ((x.shape, F32), (half, BF16), (half, BF16)), x, gain, *pieces)


def norm_backward(values, gain, grad):
    scale = scale_of(values)
    weighted = grad * gain
    inner = jnp.mean(weighted * values, -1, keepdims=True)
    return scale * weighted - values * (scale * scale * scale * inner), scale


def join_back_kernel(h_ref, dy_ref, gain_ref, a_ref, b_ref, c_ref, d_ref, dh_out, low_out, grad_out):
    h, grad = h_ref[...], total_of((a_ref, b_ref, c_ref, d_ref))
    back, scale = norm_backward(h, gain_ref[1:2], grad)
    dh = dy_ref[...].astype(F32) + back
    dh_out[...] = dh
    low_out[...] = dh.astype(BF16)
    grad_out[...] = to_blocks(jnp.broadcast_to(jnp.sum(grad * h * scale, 0, keepdims=True), (8, h.shape[1])))


def join_back(h, dy, gain, pieces):
    shapes = (h.shape, F32), (h.shape, BF16), ((8, h.shape[1]), F32)
    return small_call(join_back_kernel, shapes, h, dy, gain, *pieces)


def output_kernel(h_ref, a_ref, b_ref, c_ref, d_ref, out_ref):
    out_ref[...] = to_blocks(h_ref[...] + total_of((a_ref, b_ref, c_ref, d_ref))).astype(BF16)


def input_grad_kernel(dh_ref, x_ref, gain_ref, grad_ref, out_ref):
    back, _ = norm_backward(x_ref[...], gain_ref[:1], grad_ref[...].astype(F32))
    out_ref[...] = to_blocks(dh_ref[...] + back).astype(BF16)


GAIN_ROWS, GAIN_COLUMNS = 16, 256


def gain_rows(vector):
    return jnp.concatenate([vector[:, 256 * k : 256 * k + 256] for k in range(8)], 0)


def put_piece(ref, rows, gains):
    count = rows.shape[0]
    ref[:count] = rows
    ref[count:, GAIN_COLUMNS:] = jnp.zeros((GAIN_ROWS, ref.shape[1] - GAIN_COLUMNS), BF16)
    ref[count:, :GAIN_COLUMNS] = gains.astype(BF16)


def first_pieces_kernel(
    at_ref, q_ref, q2_ref, kv_ref, kv2_ref, o_ref, o2_ref, *refs
):
    gain_refs, out_refs = refs[:4], refs[4:]
    query = add_low(q_ref[...], q2_ref[...]).reshape(256, 512)
    narrow = add_low(kv_ref[...], kv2_ref[...]).reshape(256, 128)
    rows = jnp.concatenate([query, narrow], 1)
    out_rows = add_low(o_ref[...], o2_ref[...]).reshape(256, 512)
    gains = total_of(gain_refs)
    gains = gains[:GAIN_ROWS] + gains[GAIN_ROWS:]
    for number in range(4):

        @pl.when(pl.program_id(0) == number)
        def _():
            put_piece(out_refs[number], rows, gains)
            out_refs[4 + number][...] = out_rows


def first_pieces(at, wide, wide2, narrow, narrow2, gains):
    pick_x = lambda column: lambda d, s: (0, lax.rem(x_of(s) + d, 4), 0, column)
    pick_y = lambda d, s: (lax.rem(y_of(s) + d, 4), 0, 0, 0)
    whole = lambda d, s: (0, 0)
    shaped = lambda value: value.reshape(4, 4, 64, value.shape[1])
    shapes = [(256 + GAIN_ROWS, 640)] * 4 + [(256, 512)] * 4
    grid = pltpu.PrefetchScalarGridSpec(
        num_scalar_prefetch=1,
        grid=(4,),
        in_specs=[pl.BlockSpec((4, 1, 64, 512), pick_x(1))] * 2
        + [pl.BlockSpec((4, 1, 64, 128), pick_x(0))] * 2
        + [pl.BlockSpec((1, 4, 64, 512), pick_y)] * 2
        + [pl.BlockSpec((2 * GAIN_ROWS, GAIN_COLUMNS), whole)] * 4,
        out_specs=tuple(pl.BlockSpec(shape, whole) for shape in shapes),
    )
    wide, wide2 = shaped(wide), shaped(wide2)
    result = pl.pallas_call(
        first_pieces_kernel,
        grid_spec=grid,
        out_shape=tuple(jax.ShapeDtypeStruct(shape, BF16) for shape in shapes),
        compiler_params=pltpu.CompilerParams(vmem_limit_bytes=VMEM_LIMIT),
        cost_estimate=pl.CostEstimate(
            flops=2 * 1024 * 1152, bytes_accessed=6 * 1024 * 1152, transcendentals=0
        ),
    )(at, wide, wide2, shaped(narrow), shaped(narrow2), wide, wide2, *gains)
    return result[:4], result[4:]


def second_pieces_kernel(at_ref, *refs):
    qkv, out, (held, out_held) = refs[:4], refs[4:8], refs[16:]
    held[...] = total_of(qkv)
    out_held[...] = total_of(out).astype(BF16)
    for number in range(4):
        y = pl.multiple_of(lax.rem(y_of(at_ref) + number, 4) * 64, 64)
        put_piece(refs[8 + number], held[pl.ds(y, 64), :].astype(BF16), held[256:, :GAIN_COLUMNS])
        x = pl.multiple_of(lax.rem(x_of(at_ref) + number, 4) * 64, 64)
        refs[12 + number][...] = out_held[pl.ds(x, 64), :]


def second_pieces(at, qkv, out):
    vmem = pl.BlockSpec(memory_space=pltpu.VMEM)
    shapes = [(64 + GAIN_ROWS, 640)] * 4 + [(64, 512)] * 4
    result = pl.pallas_call(
        second_pieces_kernel,
        out_shape=tuple(jax.ShapeDtypeStruct(shape, BF16) for shape in shapes),
        in_specs=[pl.BlockSpec(memory_space=pltpu.SMEM)] + [vmem] * 8,
        out_specs=(vmem,) * 8,
        scratch_shapes=[pltpu.VMEM((256 + GAIN_ROWS, 640), F32), pltpu.VMEM((256, 512), BF16)],
        compiler_params=pltpu.CompilerParams(vmem_limit_bytes=VMEM_LIMIT),
        cost_estimate=pl.CostEstimate(
            flops=4 * 272 * 1152, bytes_accessed=10 * 272 * 1152, transcendentals=0
        ),
    )(at, *qkv, *out)
    return result[:4], result[4:]


def attention_grads_kernel(*refs):
    out_ref, q_ref, k_ref, v_ref, one_ref, two_ref = refs[8:]
    total = total_of(refs[:4])
    out_ref[...] = total_of(refs[4:8])
    q_ref[...] = total[:64, :512]
    k_ref[...] = total[:64, 512:576]
    v_ref[...] = total[:64, 576:]
    gains = total[64:, :GAIN_COLUMNS]
    one_ref[...] = jnp.concatenate([gains[k : k + 1] for k in range(8)], 1)
    two_ref[...] = jnp.concatenate([gains[k : k + 1] for k in range(8, 16)], 1)


def put_in_order(at_ref, own_ref, other_ref, columns, to_ref, sems):
    x, y, core = x_of(at_ref), y_of(at_ref), core_of(at_ref)
    copies = []
    for number in range(32):
        ref = (own_ref, other_ref)[number // 16]
        to_x, to_y = lax.rem(x + number % 4, 4), lax.rem(y + number // 4 % 4, 4)
        to_core = core if number < 16 else 1 - core
        row = pl.multiple_of(((to_core * 4 + to_y) * 4 + to_x) * 64, 64)
        copy = pltpu.make_async_copy(
            ref.at[pl.ds(number % 16 * 64, 64), columns], to_ref.at[pl.ds(row, 64)], sems.at[number]
        )
        copy.start()
        copies.append(copy)
    return copies


def project_kv_kernel(at_ref, x_ref, own_ref, other_ref, cos_ref, sin_ref, kv_ref, held, sems):
    for copy in put_in_order(at_ref, own_ref, other_ref, pl.ds(512, 128), held, sems):
        copy.wait()
    flat = dot_nn(x_ref[...], held[...])
    turned = turn(flat, cos_ref[...], sin_ref[...])
    kv_ref[...] = jnp.where(lane_is_low(flat.shape, 128), turned, flat).astype(BF16)


def project_q_kernel(at_ref, x_ref, own_ref, other_ref, cos_ref, sin_ref, q_ref, w_ref, held, sems, sem):
    for copy in put_in_order(at_ref, own_ref, other_ref, pl.ds(0, 640), held, sems):
        copy.wait()
    whole = pltpu.make_async_copy(held, w_ref, sem)
    whole.start()
    cosine, sine, x = cos_ref[...], sin_ref[...], x_ref[...]
    for start in (0, 256):
        wide = dot_nn(x, held[:, start : start + 256])
        for part in (0, 128):
            turned = turn(wide[:, part : part + 128], cosine, sine)
            q_ref[:, start + part : start + part + 128] = (turned * HEAD_SIZE**-0.5).astype(BF16)
    whole.wait()


def project(kernel, at, normed, weights, cosine, sine, columns, held_columns, hand_out):
    rows, width = normed.shape
    vmem, anywhere = pl.BlockSpec(memory_space=pltpu.VMEM), pl.BlockSpec(memory_space=pl.ANY)
    out_shape = [jax.ShapeDtypeStruct((rows, columns), BF16)]
    out_specs = [vmem]
    scratch = [pltpu.VMEM((width, held_columns), BF16), pltpu.SemaphoreType.DMA((32,))]
    if hand_out:
        out_shape.append(jax.ShapeDtypeStruct((width, held_columns), BF16))
        out_specs.append(anywhere)
        scratch.append(pltpu.SemaphoreType.DMA)
    return pl.pallas_call(
        kernel,
        out_shape=tuple(out_shape),
        in_specs=[pl.BlockSpec(memory_space=pltpu.SMEM), vmem, anywhere, anywhere, vmem, vmem],
        out_specs=tuple(out_specs),
        scratch_shapes=scratch,
        compiler_params=pltpu.CompilerParams(vmem_limit_bytes=VMEM_LIMIT),
        cost_estimate=pl.CostEstimate(
            flops=2 * rows * width * columns,
            bytes_accessed=2 * (rows * width + width * columns + rows * columns),
            transcendentals=0,
        ),
    )(at, normed, *weights, cosine, sine)


KEYS = 1152
PAIRS = 4


def set_up_kernel(place_ref, kv0_ref, kv1_ref, kv2_ref, kk_ref, vv_ref, kvt_ref):
    place = place_of(place_ref)
    low = lane_is_low((128, 128), 128)
    for block, ref in enumerate((kv0_ref, kv1_ref, kv2_ref)):
        for group in range(4):
            at = pl.multiple_of(lax.rem(group - place + 4, 4) * 128, 128)
            piece = ref[pl.ds(at, 128), :].astype(F32)
            rolled = pltpu.roll(piece, 64, 1)
            to = block * 512 + group * 128
            kk_ref[to : to + 128, :] = jnp.where(low, piece, rolled).astype(BF16)
            vv_ref[to : to + 128, :] = jnp.where(low, rolled, piece).astype(BF16)
            kvt_ref[:, to : to + 128] = piece.T.astype(BF16)


def set_up(place, kv):
    vmem = pl.BlockSpec(memory_space=pltpu.VMEM)
    return pl.pallas_call(
        set_up_kernel,
        out_shape=(
            jax.ShapeDtypeStruct((1536, 128), BF16),
            jax.ShapeDtypeStruct((1536, 128), BF16),
            jax.ShapeDtypeStruct((128, 1536), BF16),
        ),
        in_specs=[pl.BlockSpec(memory_space=pltpu.SMEM), vmem, vmem, vmem],
        out_specs=(vmem, vmem, vmem),
        compiler_params=pltpu.CompilerParams(vmem_limit_bytes=VMEM_LIMIT),
        cost_estimate=pl.CostEstimate(flops=1536 * 128 * 8, bytes_accessed=2 * 1024 * 1024, transcendentals=0),
    )(place, *kv)


def both_heads(pair):
    low = lane_is_low(pair.shape, 128)
    nothing = jnp.zeros_like(pair)
    return jnp.concatenate([jnp.where(low, pair, nothing), jnp.where(low, nothing, pair)], 0)


def side_by_side(transposed):
    return jnp.concatenate([transposed[:, :128], transposed[:, 128:]], 0).T


def mask_of(at, low_ref):
    key = lax.broadcasted_iota(jnp.int32, (KEYS, 128), 0)
    query = lax.broadcasted_iota(jnp.int32, (KEYS, 128), 1)
    seen = (key >= low_ref[:, pl.ds(at, 128)] - at) & (key <= query + WINDOW)
    bias = jnp.where(seen, 0.0, -jnp.inf)
    return jnp.concatenate([bias, bias], 1)


def attend_kernel(
    first, step, place_ref, q_ref, kk_ref, kvt_ref, low_ref, w_ref, o_ref, lse_ref, *refs
):
    part_refs, (bias, held, w_held, sem) = refs[:-4], refs[-4:]
    group = lax.rem(place_of(place_ref) + first + step * pl.program_id(0), 4)
    at = pl.multiple_of(group * 128, 128)

    load = pltpu.make_async_copy(w_ref.at[:, pl.ds(HIDDEN, 512)], w_held, sem)

    @pl.when((pl.program_id(0) == 0) & (pl.program_id(1) == 0))
    def _():
        load.start()

    @pl.when(pl.program_id(1) == 0)
    def _():
        bias[...] = mask_of(at, low_ref)

    keys = pl.ds(at, KEYS)
    for number in range(PAIRS):
        columns = slice(128 * number, 128 * number + 128)
        scores = dot_nt(kk_ref[keys, :], both_heads(q_ref[:, columns])) + bias[...]
        top = jnp.max(scores, 0, keepdims=True)
        weights = jnp.exp(scores - top)
        total = jnp.sum(weights, 0, keepdims=True)
        result = dot_nn(kvt_ref[64:128, keys], weights.astype(BF16)) / total
        lse_ref[0, number] = top + jnp.log(total)
        result = side_by_side(result).astype(BF16)
        o_ref[:, columns] = result
        held[PAIRS * pl.program_id(1) + number] = result

    @pl.when(pl.program_id(1) == 4 // PAIRS - 1)
    def _():
        @pl.when(pl.program_id(0) == 0)
        def _():
            load.wait()

        rows = jnp.concatenate([held[k] for k in range(4)], 1)
        part = dot_nt(rows, w_held[...]).astype(BF16)
        for number, ref in enumerate(part_refs):

            @pl.when(pl.program_id(0) == number)
            def _():
                ref[...] = part


def attend(first, step, count, place, queries, kk, kvt, low, weights):
    whole = lambda g, p, s: (0, 0)
    width = 128 * PAIRS
    grid = pltpu.PrefetchScalarGridSpec(
        num_scalar_prefetch=1,
        grid=(count, 4 // PAIRS),
        in_specs=[
            pl.BlockSpec((128, width), lambda g, p, s: (first + step * g, p)),
            pl.BlockSpec((1536, 128), whole),
            pl.BlockSpec((128, 1536), whole),
            pl.BlockSpec((1, 512), whole),
            pl.BlockSpec(memory_space=pl.ANY),
        ],
        out_specs=(
            pl.BlockSpec((128, width), lambda g, p, s: (g, p)),
            pl.BlockSpec((1, PAIRS, 1, 256), lambda g, p, s: (g, p, 0, 0)),
        )
        + (pl.BlockSpec((128, 2048), whole),) * count,
        scratch_shapes=[
            pltpu.VMEM((KEYS, 256), F32),
            pltpu.VMEM((4, 128, 128), BF16),
            pltpu.VMEM((2048, 512), BF16),
            pltpu.SemaphoreType.DMA,
        ],
    )
    return pl.pallas_call(
        functools.partial(attend_kernel, first, step),
        grid_spec=grid,
        out_shape=(
            jax.ShapeDtypeStruct((128 * count, 512), BF16),
            jax.ShapeDtypeStruct((count, 4, 1, 256), F32),
        )
        + (jax.ShapeDtypeStruct((128, 2048), BF16),) * count,
        compiler_params=pltpu.CompilerParams(vmem_limit_bytes=VMEM_LIMIT),
        cost_estimate=pl.CostEstimate(
            flops=count * 4 * KEYS * 256 * 256 * 2,
            bytes_accessed=3 * 1024 * 1024,
            transcendentals=count * 4 * KEYS * 256,
        ),
    )(place, queries, kk, kvt, low, weights)


def attend_back_kernel(first, step, count, *refs):
    last = first == 2
    place_ref, q_ref, w_ref, lse_ref, kk_ref, vv_ref, kvt_ref, low_ref, cos_ref, sin_ref = refs[:10]
    o_ref = refs[10]
    dh_refs, refs = refs[11 : 11 + count], refs[11 + count :]
    dk_in = dv_in = None
    if first > 0:
        dk_in, dv_in, refs = refs[0], refs[1], refs[2:]
    bias, do_held, dk, dv, w_held, sem = refs[-6:]
    dq_ref, outs = refs[0], refs[1:-6]
    number, pair = pl.program_id(0), pl.program_id(1)
    place = place_of(place_ref)
    at = pl.multiple_of(lax.rem(place + first + step * number, 4) * 128, 128)

    load = pltpu.make_async_copy(w_ref.at[:, pl.ds(HIDDEN, 512)], w_held, sem)

    @pl.when((number == 0) & (pair == 0))
    def _():
        load.start()
        dk[...] = jnp.zeros_like(dk) if dk_in is None else dk_in[...]
        dv[...] = jnp.zeros_like(dv) if dv_in is None else dv_in[...]

    @pl.when(pair == 0)
    def _():
        bias[...] = mask_of(at, low_ref)

        @pl.when(number == 0)
        def _():
            load.wait()

        for k, ref in enumerate(dh_refs):

            @pl.when(number == k)
            def _():
                do_rows = dot_nn(ref[...], w_held[...]).astype(BF16)
                for p in range(4):
                    do_held[p] = do_rows[:, 128 * p : 128 * p + 128]

    keys = pl.ds(at, KEYS)
    queries, grads, all_weights, all_grad_scores = [], [], [], []
    for k in range(PAIRS):
        columns = slice(128 * k, 128 * k + 128)
        do_pair = do_held[PAIRS * pair + k]
        query, grad = both_heads(q_ref[:, columns]), both_heads(do_pair)
        scores = dot_nt(kk_ref[keys, :], query) + bias[...]
        weights = jnp.exp(scores - lse_ref[0, k])
        grad_weights = dot_nt(vv_ref[keys, :], grad)
        product = (o_ref[:, columns].astype(F32) * do_pair.astype(F32)).T
        inner = jnp.concatenate(
            [jnp.sum(product[:64], 0, keepdims=True), jnp.sum(product[64:], 0, keepdims=True)], 1
        )
        grad_scores = (weights * (grad_weights - inner)).astype(BF16)
        grad_query = side_by_side(dot_nn(kvt_ref[0:64, keys], grad_scores)) * HEAD_SIZE**-0.5
        dq_ref[:, columns] = turn(grad_query, cos_ref[...], -sin_ref[...]).astype(BF16)
        queries.append(query)
        grads.append(grad)
        all_weights.append(weights.astype(BF16))
        all_grad_scores.append(grad_scores)
    join = lambda values, axis: values[0] if PAIRS == 1 else jnp.concatenate(values, axis)
    dv[keys, :] += dot_nn(join(all_weights, 1), join(grads, 0))
    dk[keys, :] += dot_nn(join(all_grad_scores, 1), join(queries, 0))

    @pl.when((number == pl.num_programs(0) - 1) & (pair == 4 // PAIRS - 1))
    def _():
        if not last:
            outs[0][...], outs[1][...] = dk[...], dv[...]
            return
        half = lane_is_low((128, 128), 128)
        for block in range(3):
            for group in range(4):
                to = pl.multiple_of(lax.rem(group - place + 4, 4) * 128, 128)
                frm = slice(block * 512 + group * 128, block * 512 + group * 128 + 128)
                key, value = dk[frm, :], dv[frm, :]
                key = key + pltpu.roll(key, 64, 1)
                value = value + pltpu.roll(value, 64, 1)
                both = jnp.where(half, key, value)
                outs[block][pl.ds(to, 128), :] = both.astype(outs[block].dtype)


def attend_back(first, step, count, place, queries, o, dh, weights, lse, kk, vv, kvt, low, cosine, sine, held):
    last = first == 2
    whole = lambda g, p, s: (0, 0)
    specs = [
        pl.BlockSpec((128, 128 * PAIRS), lambda g, p, s: (first + step * g, p)),
        pl.BlockSpec(memory_space=pl.ANY),
        pl.BlockSpec((1, PAIRS, 1, 256), lambda g, p, s: (g, p, 0, 0)),
        pl.BlockSpec((1536, 128), whole),
        pl.BlockSpec((1536, 128), whole),
        pl.BlockSpec((128, 1536), whole),
        pl.BlockSpec((1, 512), whole),
        pl.BlockSpec((128, 128), lambda g, p, s: (first + step * g, 0)),
        pl.BlockSpec((128, 128), lambda g, p, s: (first + step * g, 0)),
    ]
    specs += [pl.BlockSpec((128, 128 * PAIRS), lambda g, p, s: (g, p))]
    specs += [pl.BlockSpec((128, 2048), whole)] * count + [pl.BlockSpec((1536, 128), whole)] * len(held)
    if last:
        out_specs = (pl.BlockSpec((512, 128), whole),) * 3
        out_shape = tuple(jax.ShapeDtypeStruct((512, 128), dtype) for dtype in (BF16, BF16, F32))
    else:
        out_specs = (pl.BlockSpec((1536, 128), whole),) * 2
        out_shape = (jax.ShapeDtypeStruct((1536, 128), F32),) * 2
    grid = pltpu.PrefetchScalarGridSpec(
        num_scalar_prefetch=1,
        grid=(count, 4 // PAIRS),
        in_specs=specs,
        out_specs=(pl.BlockSpec((128, 128 * PAIRS), lambda g, p, s: (g, p)),) + out_specs,
        scratch_shapes=[
            pltpu.VMEM((KEYS, 256), F32),
            pltpu.VMEM((4, 128, 128), BF16),
            pltpu.VMEM((1536, 128), F32),
            pltpu.VMEM((1536, 128), F32),
            pltpu.VMEM((2048, 512), BF16),
            pltpu.SemaphoreType.DMA,
        ],
    )
    return pl.pallas_call(
        functools.partial(attend_back_kernel, first, step, count),
        grid_spec=grid,
        out_shape=(jax.ShapeDtypeStruct((128 * count, 512), BF16),) + out_shape,
        compiler_params=pltpu.CompilerParams(vmem_limit_bytes=VMEM_LIMIT),
        cost_estimate=pl.CostEstimate(
            flops=count * 4 * KEYS * 256 * 640 * 2,
            bytes_accessed=6 * 1024 * 1024,
            transcendentals=count * 4 * KEYS * 256,
        ),
    )(place, queries, weights, lse, kk, vv, kvt, low, cosine, sine, o, *dh, *held)


GROUPS = [(0, 128), (128, 256), (384, 512), (896, 512)]


def columns_times_kernel(left_ref, right_ref, out_ref, left, right, out, sems, out_sems):
    load = pltpu.make_async_copy(left_ref, left, sems.at[len(GROUPS)])
    load.start()
    copies, results = [], []
    for number, (start, width) in enumerate(GROUPS):
        columns = pl.ds(start, width)
        copy = pltpu.make_async_copy(right_ref.at[:, columns], right.at[:, columns], sems.at[number])
        copy.start()
        copies.append(copy)
    load.wait()
    value = left[...]
    for number, (start, width) in enumerate(GROUPS):
        copies[number].wait()
        out[:, start : start + width] = dot_nn(value, right[:, start : start + width])
        columns = pl.ds(start, width)
        copy = pltpu.make_async_copy(out.at[:, columns], out_ref.at[:, columns], out_sems.at[number])
        copy.start()
        results.append(copy)
    for copy in results:
        copy.wait()


def columns_times(left, right):
    rows, width = left.shape
    anywhere = pl.BlockSpec(memory_space=pl.ANY)
    return pl.pallas_call(
        columns_times_kernel,
        out_shape=jax.ShapeDtypeStruct((rows, HIDDEN), F32),
        in_specs=[anywhere, anywhere],
        out_specs=anywhere,
        scratch_shapes=[
            pltpu.VMEM((rows, width), BF16),
            pltpu.VMEM((width, HIDDEN), BF16),
            pltpu.VMEM((rows, HIDDEN), F32),
            pltpu.SemaphoreType.DMA((len(GROUPS) + 1,)),
            pltpu.SemaphoreType.DMA((len(GROUPS),)),
        ],
        compiler_params=pltpu.CompilerParams(vmem_limit_bytes=VMEM_LIMIT),
        cost_estimate=pl.CostEstimate(
            flops=2 * rows * width * HIDDEN, bytes_accessed=11 * 1024 * 1024, transcendentals=0
        ),
    )(left, right)


PIECES = [(0, 128), (128, 128), (256, 128), (384, 128)]


def ffn_kernel(*refs):
    core_ref, x_refs, dact_ref, w_ref = refs[0], refs[1:9], refs[9], refs[10]
    gua_ref, whole_ref, swap_ref, dx_refs = refs[11], refs[12], refs[13], refs[14:18]
    x_held, dact_held, w_held, gua, dx, sems, out_sems = refs[18:]
    x_copies = []
    for number in range(8):
        copy = pltpu.make_async_copy(
            x_refs[number], x_held.at[pl.ds(64 * number, 64)], sems.at[12 + number]
        )
        copy.start()
        x_copies.append(copy)
    copies = []
    for number, (start, width) in enumerate(GROUPS):
        for part in range(3):
            if part < 2:
                columns = pl.ds(part * HIDDEN + start, width)
                copy = pltpu.make_async_copy(
                    w_ref.at[:, columns], w_held.at[:, columns], sems.at[3 * number + part]
                )
            else:
                columns = pl.ds(start, width)
                copy = pltpu.make_async_copy(
                    dact_ref.at[:, columns], dact_held.at[:, columns], sems.at[3 * number + part]
                )
            copy.start()
            copies.append(copy)
    for copy in x_copies:
        copy.wait()
    half = pl.multiple_of((1 - core_of(core_ref)) * 1024, 1024)
    results = [
        pltpu.make_async_copy(x_held, whole_ref, out_sems.at[5]),
        pltpu.make_async_copy(x_held.at[:, pl.ds(half, 1024)], swap_ref, out_sems.at[6]),
    ]
    for copy in results:
        copy.start()
    x = x_held[...]
    for number, (start, width) in enumerate(GROUPS):
        for part in range(3):
            copies[3 * number + part].wait()
        gate = dot_nn(x, w_held[:, start : start + width])
        up = dot_nn(x, w_held[:, HIDDEN + start : HIDDEN + start + width])
        dact = dact_held[:, start : start + width]
        sig = jax.nn.sigmoid(gate)
        silu = gate * sig
        dgate = dact * up * (sig * (1.0 + gate * (1.0 - sig)))
        gua[:, start : start + width] = dgate.astype(BF16)
        gua[:, HIDDEN + start : HIDDEN + start + width] = (dact * silu).astype(BF16)
        gua[:, 2 * HIDDEN + start : 2 * HIDDEN + start + width] = (silu * up).astype(BF16)
    copy = pltpu.make_async_copy(gua, gua_ref, out_sems.at[4])
    copy.start()
    results.append(copy)
    dgu = gua[:, : 2 * HIDDEN]
    for number in range(4):
        columns = slice(512 * number, 512 * number + 512)
        dx[:, columns] = dot_nt(dgu, w_held[columns, : 2 * HIDDEN]).astype(BF16)
    for number, (start, size) in enumerate(PIECES):
        copy = pltpu.make_async_copy(dx.at[pl.ds(start, size)], dx_refs[number], out_sems.at[number])
        copy.start()
        results.append(copy)
    for copy in results:
        copy.wait()


def ffn(core, pieces, dact, weights):
    rows, width = dact.shape[0], weights.shape[0]
    anywhere = pl.BlockSpec(memory_space=pl.ANY)
    result = pl.pallas_call(
        ffn_kernel,
        out_shape=(
            jax.ShapeDtypeStruct((rows, 3 * HIDDEN), BF16),
            jax.ShapeDtypeStruct((rows, width), BF16),
            jax.ShapeDtypeStruct((rows, width // 2), BF16),
            *(jax.ShapeDtypeStruct((size, width), BF16) for _, size in PIECES),
        ),
        in_specs=[pl.BlockSpec(memory_space=pltpu.SMEM)] + [anywhere] * 10,
        out_specs=(anywhere,) * 7,
        scratch_shapes=[
            pltpu.VMEM((rows, width), BF16),
            pltpu.VMEM((rows, HIDDEN), F32),
            pltpu.VMEM((width, 2 * HIDDEN), BF16),
            pltpu.VMEM((rows, 3 * HIDDEN), BF16),
            pltpu.VMEM((rows, width), BF16),
            pltpu.SemaphoreType.DMA((20,)),
            pltpu.SemaphoreType.DMA((7,)),
        ],
        compiler_params=pltpu.CompilerParams(vmem_limit_bytes=VMEM_LIMIT),
        cost_estimate=pl.CostEstimate(
            flops=8 * rows * width * HIDDEN,
            bytes_accessed=25 * 1024 * 1024,
            transcendentals=rows * HIDDEN,
        ),
    )(core, *pieces, dact, weights)
    return result[0], result[1], result[2], result[3:]


def weight_grads_kernel(core_ref, x_ref, x2_ref, dy_ref, dy2_ref, right_ref, right2_ref, out_ref):
    part = pl.program_id(0)

    @pl.when(part < 2)
    def _():
        total = dot_tn(x_ref[...], right_ref[...]) + dot_tn(x2_ref[...], right2_ref[...])
        out_ref[...] = total.astype(BF16)

    @pl.when(part == 2)
    def _():
        total = dot_tn(dy_ref[...], right_ref[...]) + dot_tn(dy2_ref[...], right2_ref[...])
        out_ref[...] = total.astype(BF16)


def weight_grads(core, x, x2, dy, dy2, right, right2):
    rows = x.shape[0]
    tile = 1024
    half = x2.shape[1]
    tiles = half // tile
    own = lambda j, i, c: (0, core_of(c) * tiles + i)
    other = lambda j, i, c: (0, i)
    side = lambda j, i, c: (0, j)
    grid = pltpu.PrefetchScalarGridSpec(
        num_scalar_prefetch=1,
        grid=(3, tiles),
        in_specs=[
            pl.BlockSpec((rows, tile), own),
            pl.BlockSpec((rows, tile), other),
            pl.BlockSpec((rows, tile), own),
            pl.BlockSpec((rows, tile), other),
            pl.BlockSpec((rows, HIDDEN), side),
            pl.BlockSpec((rows, HIDDEN), side),
        ],
        out_specs=pl.BlockSpec((tile, HIDDEN), lambda j, i, c: (i, j)),
    )
    return pl.pallas_call(
        weight_grads_kernel,
        grid_spec=grid,
        out_shape=jax.ShapeDtypeStruct((half, 3 * HIDDEN), BF16),
        compiler_params=pltpu.CompilerParams(vmem_limit_bytes=VMEM_LIMIT),
        cost_estimate=pl.CostEstimate(
            flops=2 * 3 * 2 * rows * half * HIDDEN, bytes_accessed=24 * 1024 * 1024, transcendentals=0
        ),
    )(core, x, x2, dy, dy2, right, right2)


def rows_times_kernel(left_ref, right_ref, *out_refs):
    result = dot_nt(left_ref[...], right_ref[...]).astype(BF16)
    for number, ref in enumerate(out_refs):
        ref[...] = result[128 * number : 128 * number + 128]


def rows_times(left, left_part, right, part):
    rows, depth = left.shape[0], HIDDEN
    width = right.shape[0]
    tile = 512
    return pl.pallas_call(
        rows_times_kernel,
        out_shape=(jax.ShapeDtypeStruct((128, width), BF16),) * 4,
        grid=(width // tile,),
        in_specs=[
            pl.BlockSpec((rows, depth), lambda i: (0, left_part)),
            pl.BlockSpec((tile, depth), lambda i: (i, part)),
        ],
        out_specs=(pl.BlockSpec((128, tile), lambda i: (0, i)),) * 4,
        compiler_params=pltpu.CompilerParams(vmem_limit_bytes=VMEM_LIMIT),
        cost_estimate=pl.CostEstimate(
            flops=2 * rows * depth * width,
            bytes_accessed=2 * (rows * depth + width * depth + rows * width),
            transcendentals=0,
        ),
    )(left, right)


def ring_rows(own, near, far):
    return jnp.concatenate([own, near[:128], far, near[128:]], 0)


def put_half(number, value, other_ref, own_ref):
    @pl.when(number < 2)
    def _():
        other_ref[...] = value

    @pl.when(number >= 2)
    def _():
        own_ref[...] = value


def tile_at(i, c):
    return lax.rem(i + 2 * (1 - core_of(c)), 4)


def half_specs(tile, columns):
    return (
        pl.BlockSpec((tile, columns), lambda i, c: (jnp.minimum(i, 1), 0)),
        pl.BlockSpec((tile, columns), lambda i, c: (jnp.maximum(i - 2, 0), 0)),
    )


def wide_grads_kernel(
    core_ref, x_ref, dh0, dh1, dh2, dh3, o0, o1, o2, dq0, dq1, dq2, other_ref, own_ref, o_held, dq_held
):
    number = pl.program_id(0)

    @pl.when(number == 0)
    def _():
        o_held[...] = ring_rows(o0[...], o1[...], o2[...])
        dq_held[...] = ring_rows(dq0[...], dq1[...], dq2[...])

    dh = jnp.concatenate([ref[...] for ref in (dh0, dh1, dh2, dh3)], 0)
    out = dot_tn(dh, o_held[...])
    query = dot_tn(x_ref[...], dq_held[...])
    put_half(number, jnp.concatenate([out, query], 1).astype(BF16), other_ref, own_ref)


def wide_grads(core, normed, dh, o, dq):
    rows, width = normed.shape
    tile = 512
    whole = lambda i, c: (0, 0)
    column = lambda i, c: (0, tile_at(i, c))
    small = [pl.BlockSpec((size, 512), whole) for size in (128, 256, 128)]
    grid = pltpu.PrefetchScalarGridSpec(
        num_scalar_prefetch=1,
        grid=(4,),
        in_specs=[pl.BlockSpec((rows, tile), column)]
        + [pl.BlockSpec((128, tile), column)] * 4
        + small
        + small,
        out_specs=half_specs(tile, 1024),
        scratch_shapes=[pltpu.VMEM((rows, 512), BF16), pltpu.VMEM((rows, 512), BF16)],
    )
    return pl.pallas_call(
        wide_grads_kernel,
        grid_spec=grid,
        out_shape=(jax.ShapeDtypeStruct((width // 2, 1024), BF16),) * 2,
        compiler_params=pltpu.CompilerParams(vmem_limit_bytes=VMEM_LIMIT),
        cost_estimate=pl.CostEstimate(
            flops=2 * rows * width * 1024, bytes_accessed=10 * 1024 * 1024, transcendentals=0
        ),
    )(core, normed, *dh, *o, *dq)


def finish_kernel(
    core_ref,
    x_ref,
    w_ref,
    dq0_ref,
    dq1_ref,
    dq2_ref,
    own_ref,
    one_ref,
    two_ref,
    cos_ref,
    sin_ref,
    norm_ref,
    second_ref,
    other_grad_ref,
    own_grad_ref,
    dx_ref,
    gain_ref,
    dqkv,
    sums,
):
    number = pl.program_id(0)

    @pl.when(number == 0)
    def _():
        dqkv[:, :512] = ring_rows(dq0_ref[...], dq1_ref[...], dq2_ref[...])
        dkv = own_ref[...] + one_ref[...].astype(F32) + two_ref[...].astype(F32)
        turned = turn(dkv, cos_ref[...], -sin_ref[...])
        dqkv[:, 512:] = jnp.where(lane_is_low(dkv.shape, 128), turned, dkv).astype(BF16)

    x = x_ref[...]
    put_half(number, dot_tn(x, dqkv[:, 512:]).astype(BF16), other_grad_ref, own_grad_ref)
    dx = dot_nt(dqkv[...], w_ref[...])
    for piece in range(4):
        row = pl.multiple_of(lax.rem(place_of(core_ref) + piece, 4) * 128, 128)
        dx_ref[pl.ds(row, 128), :] = dx[128 * piece : 128 * piece + 128].astype(BF16)
    columns = pl.ds(pl.multiple_of(tile_at(number, core_ref) * 512, 512), 512)
    sums[:, columns] = jnp.broadcast_to(
        jnp.sum(dx * x.astype(F32), 0, keepdims=True) / norm_ref[:1], (8, 512)
    )

    @pl.when(number == 3)
    def _():
        gain_ref[:8] = gain_rows(to_blocks(sums[...])[:1])
        gain_ref[8:] = gain_rows(second_ref[:1])


def finish(core, normed, weights, dq, own, one, two, cosine, sine, gain, second):
    rows, width = normed.shape
    tile = 512
    whole = lambda i, c: (0, 0)
    column = lambda i, c: (0, tile_at(i, c))
    narrow = pl.BlockSpec((rows, 128), whole)
    grid = pltpu.PrefetchScalarGridSpec(
        num_scalar_prefetch=1,
        grid=(4,),
        in_specs=[
            pl.BlockSpec((rows, tile), column),
            pl.BlockSpec((tile, 640), lambda i, c: (tile_at(i, c), 0)),
            pl.BlockSpec((128, 512), whole),
            pl.BlockSpec((256, 512), whole),
            pl.BlockSpec((128, 512), whole),
            narrow,
            narrow,
            narrow,
            narrow,
            narrow,
            pl.BlockSpec((2, tile), column),
            pl.BlockSpec((8, width), whole),
        ],
        out_specs=half_specs(tile, 128)
        + (pl.BlockSpec((rows, tile), column),)
        + (pl.BlockSpec((GAIN_ROWS, GAIN_COLUMNS), whole),),
        scratch_shapes=[pltpu.VMEM((rows, 640), BF16), pltpu.VMEM((8, width), F32)],
    )
    result = pl.pallas_call(
        finish_kernel,
        grid_spec=grid,
        out_shape=(jax.ShapeDtypeStruct((width // 2, 128), BF16),) * 2
        + (jax.ShapeDtypeStruct((rows, width), BF16),)
        + (jax.ShapeDtypeStruct((GAIN_ROWS, GAIN_COLUMNS), F32),),
        compiler_params=pltpu.CompilerParams(vmem_limit_bytes=VMEM_LIMIT),
        cost_estimate=pl.CostEstimate(
            flops=2 * rows * width * 768, bytes_accessed=10 * 1024 * 1024, transcendentals=0
        ),
    )(core, normed, weights, *dq, own, one, two, cosine, sine, gain, second)
    return result


def per_device(
    tokens,
    segments,
    w_query,
    key_projection,
    value_projection,
    w_out,
    w_gate,
    w_up,
    w_down,
    norm_attn,
    norm_ffn,
    cotangent,
):
    place, core = lax.axis_index("head"), lax.axis_index("core")
    block = (lax.axis_index("y") * 4 + lax.axis_index("x")) * 2 + core
    code = (((lax.axis_index("x") * 4 + lax.axis_index("y")) * 2 + core) * 4 + place).astype(jnp.int32)
    code = code.reshape(1)
    keep = lax.optimization_barrier


    out_weights = lax.all_gather(
        jnp.concatenate([w_down.T, w_out.T], 1), CORE_FIRST, axis=0, tiled=True
    )
    ffn_weights = lax.all_gather(jnp.concatenate([w_gate, w_up], 1), CORE_FIRST, axis=0, tiled=True)

    x_rows, dy_rows, normed_rows, gains = prepare(
        tokens[0], cotangent[0], jnp.stack([norm_attn, norm_ffn]).astype(F32)
    )
    normed_rows, w_query = keep((normed_rows, w_query))
    ahead, behind = near_pieces(normed_rows)
    qkv_own = gather_axis(jnp.concatenate([w_query, key_projection, value_projection], 1), "x")
    qkv_own = gather_axis(jnp.concatenate(qkv_own, 0), "y")
    far = far_pieces(ahead, behind)
    qkv_own, far = keep((qkv_own, far))
    qkv_own = jnp.concatenate(qkv_own, 0)
    qkv_pieces = qkv_own, shift(qkv_own, "core", 1)
    normed_one = jnp.concatenate([normed_rows, ahead, *far, behind], 0)
    dy_raw, far = keep((cotangent[0], far))
    dy_pieces = gather_pieces(dy_raw)

    row = jnp.arange(512, dtype=jnp.int32)
    positions = block * 512 + ((row // 128 + place) % 4) * 128 + row % 128
    frequency = 10000.0 ** (-jnp.arange(32, dtype=F32) * 2.0 / HEAD_SIZE)
    angles = positions.astype(F32)[:, None] * frequency[None, :]
    cosine, sine = jnp.cos(angles), jnp.sin(angles)
    cosine = jnp.concatenate([cosine] * 4, 1)
    sine = jnp.concatenate([-sine, sine, -sine, sine], 1)

    (kv_own,) = project(
        project_kv_kernel, code, normed_one, qkv_pieces, cosine, sine, 128, 128, False
    )
    normed_late, kv_own = keep((normed_one, kv_own))
    kv = (from_block(kv_own, 2), from_block(kv_own, 1), kv_own)
    queries, qkv_weights = project(
        project_q_kernel, code, normed_late, qkv_pieces, cosine, sine, 512, 640, True
    )

    flat = segments.reshape(-1)
    padded = jnp.concatenate([jnp.full((1024,), -1, jnp.int32), flat])
    own = lax.dynamic_slice_in_dim(flat, block * 512, 512, 0)
    window = lax.dynamic_slice_in_dim(padded, block * 512, 1536, 0)
    start = jnp.sum((window[None, :] < own[:, None]).astype(jnp.int32), 1)
    low = jnp.maximum(start, row + 1).reshape(1, 512)

    kk, vv, kvt = set_up(code, kv)
    seen = code, queries, kk, kvt, low, out_weights
    o_far, lse_far, part_far = attend(2, 1, 1, *seen)
    queries, part_far, dy_pieces = keep((queries, part_far, dy_pieces))
    part_far = shift(part_far, "head", 2)
    seen = code, queries, kk, kvt, low, out_weights
    o_near, lse_near, part_ahead, part_behind = attend(1, 2, 2, *seen)
    queries, part_far, part_ahead, part_behind = keep((queries, part_far, part_ahead, part_behind))
    seen = code, queries, kk, kvt, low, out_weights
    o_own, lse_own, part_own = attend(0, 1, 1, *seen)
    dy, dy_swap = assemble(code, dy_rows, *dy_pieces)
    dy_other = shift(dy_swap, "core", 1)
    attention_sum = part_own, shift(part_ahead, "head", 1), shift(part_behind, "head", -1), part_far
    h1, top, bottom = join(x_rows, gains, attention_sum)
    behind_top, ahead_bottom = shift(top, "head", 1), shift(bottom, "head", -1)
    ahead_top, behind_bottom = shift(top, "head", -1), shift(bottom, "head", 1)
    behind_top, ahead_bottom, dy = keep((behind_top, ahead_bottom, dy))
    far_top, far_bottom = shift(behind_top, "head", 1), shift(ahead_bottom, "head", -1)
    rows_two = top, bottom, ahead_top, ahead_bottom, far_top, far_bottom, behind_top, behind_bottom
    dact = columns_times(dy, out_weights)
    dact, dy_other = keep((dact, dy_other))

    gua, normed_two, normed_two_swap, dnormed_two = ffn(
        code, rows_two, dact, ffn_weights
    )
    dnormed_two = scatter_pieces(*dnormed_two)
    gua_other = shift(gua, "core", 1)
    normed_two_other = shift(normed_two_swap, "core", 1)
    out_pieces = rows_times(gua, 2, out_weights, 0)
    gua_other, normed_two_other, out_pieces = keep((gua_other, normed_two_other, out_pieces))
    held = weight_grads(code, normed_two, normed_two_other, dy, dy_other, gua, gua_other)
    held, dnormed_two = keep((held, dnormed_two))
    grads = lax.psum_scatter(held, ("y", "x"), scatter_dimension=0, tiled=True)

    dh1, dh1_low, grad_gain_two = join_back(h1, dy_rows, gains, dnormed_two)
    back = kk, vv, kvt, low, cosine, sine
    dq_own, dk, dv = attend_back(0, 1, 1, code, queries, o_own, (dh1_low,), out_weights, lse_own, *back, ())
    ahead, behind = shift(dh1_low, "head", -1), shift(dh1_low, "head", 1)
    ahead, behind, dk, dv, dh1_late, out_pieces = keep((ahead, behind, dk, dv, dh1_low, out_pieces))
    far = shift(dh1_late, "head", 2)
    dq_near, dk, dv = attend_back(
        1, 2, 2, code, queries, o_near, (ahead, behind), out_weights, lse_near, *back, (dk, dv)
    )
    far, dk, dv, out_pieces = keep((far, dk, dv, out_pieces))
    out_pieces = scatter_pieces(*out_pieces)
    dq_far, dkv_first, dkv_second, dkv_own = attend_back(
        2, 1, 1, code, queries, o_far, (far,), out_weights, lse_far, *back, (dk, dv)
    )
    dq = dq_own, dq_near, dq_far
    dkv_one = from_block(dkv_second, -1)
    dkv_two = from_block(dkv_first, -2)
    wide_other, wide_own = wide_grads(
        code, normed_one, (dh1_low, ahead, far, behind), (o_own, o_near, o_far), dq
    )
    dkv_one, dkv_two, wide_other, out_pieces = keep((dkv_one, dkv_two, wide_other, out_pieces))
    wide_other = shift(wide_other, "core", 1)

    narrow_other, narrow_own, dnormed_one, gain_grads = finish(
        code,
        normed_one,
        qkv_weights,
        dq,
        dkv_own,
        dkv_one,
        dkv_two,
        cosine,
        sine,
        gains,
        grad_gain_two,
    )
    dnormed_one = lax.psum_scatter(dnormed_one, "head", scatter_dimension=0, tiled=True)
    gain_grads = jnp.concatenate([gain_grads, shift(gain_grads, "core", 1)], 0)
    gain_grads = exchange([gain_grads] * 4, "head")
    rows = [(x_rows.shape, BF16)]
    (output,) = small_call(output_kernel, rows, h1, *out_pieces)
    gain_grads, output = keep((gain_grads, output))
    pieces, out_sums = first_pieces(
        code, wide_own, wide_other, narrow_own, shift(narrow_other, "core", 1), gain_grads
    )
    grads = (
        grads[:, :HIDDEN].astype(F32),
        grads[:, HIDDEN : 2 * HIDDEN].astype(F32),
        grads[:, 2 * HIDDEN :].T.astype(F32),
    )
    pieces, out_sums, grads = keep((exchange(pieces, "x"), exchange(out_sums, "y"), grads))
    pieces, out_sums = second_pieces(code, pieces, out_sums)
    (grad_inputs,) = small_call(input_grad_kernel, rows, dh1, x_rows, gains, dnormed_one)
    pieces, out_sums, grad_inputs = keep((exchange(pieces, "y"), exchange(out_sums, "x"), grad_inputs))
    columns = (64, 512), (64, 512), (64, 64), (64, 64), (1, 2048), (1, 2048)
    grad_out, grad_query, grad_key, grad_value, grad_gain_one, grad_gain_two = small_call(
        attention_grads_kernel,
        [(shape, F32) for shape in columns],
        *pieces,
        *out_sums,
    )

    return (
        output[None],
        grad_inputs[None],
        grad_query,
        grad_key,
        grad_value,
        grad_out.T,
        *grads,
        grad_gain_one.reshape(2048),
        grad_gain_two.reshape(2048),
    )


def solution(mesh):
    grid = Mesh(mesh.devices.reshape(4, 4, 4, 2), ("head", "y", "x", "core"))
    rows, up, down = P(BLK, "head", None), P(BLK, "head"), P("head", BLK)
    return jax.shard_map(
        per_device,
        mesh=grid,
        in_specs=(rows, P(), up, up, up, down, up, up, down, P(), P(), rows),
        out_specs=(rows, rows, up, up, up, down, up, up, down, P(), P()),
        check_vma=False,
    )
```

profile of v0, /device:TPU:0, one launch (start us, length us, event | category | flops | bytes accessed | tf_op | source)
XLA Modules:
  0.0 342.6 jit_solution(11943505241537703228)
XLA Ops:
  41.7 7.2 %collective-permute-done.5 = bf16[256,640]{1,0:T(8,128)(2,1)S(1)} collective-permute-done((bf16[256,640]{1,0:T(8,128)(2,1)S(1)}, bf16[256,640]{1,0:T(8,128)(2,1)S(1)}, u32[]{:S(2)}, u32[]{:S(2)}) %collective-permute-start.5) | collective-permute-done | bytes 327712 | tf_op jit(solution)/shard_map/ppermute | solution.py:36
  68.2 4.5 %shard_map.204.kv2_ref = bf16[512,128]{1,0:T(8,128)(2,1)} custom-call(s32[1]{0:T(128)} %bitcast.at_ref.place_ref.core_ref.refs_0_, bf16[512,2048]{1,0:T(8,128)(2,1)} %constant_dynamic-update-slice_fusion.x_ref, bf16[1024,640]{1,0:T(8,128)(2,1)} %copy-done, bf16[1024,640]{1,0:T(8,128)(2,1)} %copy-done.1, f32[512,128]{1,0:T(8,128)} %get-tuple-element.337.cos_ref.refs_8_, ...), custom_call_target="tpu_custom_call" | custom-call | flops 268435456 | bytes 2752512 | tf_op jit(solution)/shard_map/pallas_call | solution.py:395
  77.0 6.3 %shard_map.205 = (bf16[512,512]{1,0:T(8,128)(2,1)}, bf16[2048,640]{1,0:T(8,128)(2,1)}) custom-call(s32[1]{0:T(128)} %bitcast.at_ref.place_ref.core_ref.refs_0_, bf16[512,2048]{1,0:T(8,128)(2,1)} %constant_dynamic-update-slice_fusion.x_ref, bf16[1024,640]{1,0:T(8,128)(2,1)} %copy-done, bf16[1024,640]{1,0:T(8,128)(2,1)} %copy-done.1, ...), custom_call_target="tpu_custom_call" | custom-call | flops 1073741824 | bytes 4718592 | tf_op jit(solution)/shard_map/pallas_call | solution.py:395
  86.9 6.0 %shard_map.207 = (bf16[128,512]{1,0:T(8,128)(2,1)}, f32[1,4,1,256]{3,2,1,0:T(1,128)}, bf16[128,2048]{1,0:T(8,128)(2,1)}) custom-call(s32[1]{0:T(128)} %bitcast.at_ref.place_ref.core_ref.refs_0_, bf16[512,512]{1,0:T(8,128)(2,1)} %get-tuple-element.192.q_ref.refs_1_, bf16[1536,128]{1,0:T(8,128)(2,1)} %get-tuple-element.184.kk_ref.refs_4_, ...), custom_call_target="tpu_custom_call" | custom-call | flops 603979776 | bytes 3145728 | tf_op jit(solution)/shard_map/pallas_call | solution.py:532
  95.1 10.3 %shard_map.208 = (bf16[256,512]{1,0:T(8,128)(2,1)}, f32[2,4,1,256]{3,2,1,0:T(1,128)}, bf16[128,2048]{1,0:T(8,128)(2,1)}, bf16[128,2048]{1,0:T(8,128)(2,1)}) custom-call(s32[1]{0:T(128)} %bitcast.at_ref.place_ref.core_ref.refs_0_, bf16[512,512]{1,0:T(8,128)(2,1)} %get-tuple-element.192.q_ref.refs_1_, bf16[1536,128]{1,0:T(8,128)(2,1)} %get-tuple-element.184.kk_ref.refs_4_, ...), custom_call_target="tpu_custom_call" | custom-call | flops 1207959552 | bytes 3145728 | tf_op jit(solution)/shard_map/pallas_call | solution.py:532
  105.4 4.0 %collective-permute-done.16.d_ref = bf16[128,2048]{1,0:T(8,128)(2,1)S(1)} collective-permute-done((bf16[128,2048]{1,0:T(8,128)(2,1)}, bf16[128,2048]{1,0:T(8,128)(2,1)S(1)}, u32[]{:S(2)}, u32[]{:S(2)}) %collective-permute-start.16) | collective-permute-done | bytes 524320 | tf_op jit(solution)/shard_map/ppermute | solution.py:36
  112.6 4.1 %shard_map.211 = (bf16[512,2048]{1,0:T(8,128)(2,1)}, bf16[512,1024]{1,0:T(8,128)(2,1)}) custom-call(s32[1]{0:T(128)} %bitcast.at_ref.place_ref.core_ref.refs_0_, bf16[128,2048]{1,0:T(8,128)(2,1)} %get-tuple-element.203.own_ref.dy_ref, bf16[128,2048]{1,0:T(8,128)(2,1)} %collective-permute-done.13.ahead_ref, ...), custom_call_target="tpu_custom_call" | custom-call | flops 4194304 | bytes 5242880 | tf_op jit(solution)/shard_map/pallas_call | solution.py:172
  116.7 6.1 %shard_map.209 = (bf16[128,512]{1,0:T(8,128)(2,1)}, f32[1,4,1,256]{3,2,1,0:T(1,128)}, bf16[128,2048]{1,0:T(8,128)(2,1)}) custom-call(s32[1]{0:T(128)} %bitcast.at_ref.place_ref.core_ref.refs_0_, bf16[512,512]{1,0:T(8,128)(2,1)} %get-tuple-element.192.q_ref.refs_1_, bf16[1536,128]{1,0:T(8,128)(2,1)} %get-tuple-element.184.kk_ref.refs_4_, ...), custom_call_target="tpu_custom_call" | custom-call | flops 603979776 | bytes 3145728 | tf_op jit(solution)/shard_map/pallas_call | solution.py:532
  124.7 3.6 %shard_map.210 = (f32[128,2048]{1,0:T(8,128)}, bf16[64,2048]{1,0:T(8,128)(2,1)}, bf16[64,2048]{1,0:T(8,128)(2,1)}) custom-call(f32[128,2048]{1,0:T(8,128)} %get-tuple-element.196.x_ref, f32[2,2048]{1,0:T(2,128)} %get-tuple-element.197.gain_ref.norm_ref, bf16[128,2048]{1,0:T(8,128)(2,1)} %get-tuple-element.198.a_ref, ...), custom_call_target="tpu_custom_call" | custom-call | flops 1314816 | bytes 6324224 | tf_op jit(solution)/shard_map/pallas_call | solution.py:185
  133.6 5.3 %collective-permute-done.20.refs_7_ = bf16[64,2048]{1,0:T(8,128)(2,1)S(1)} collective-permute-done((bf16[64,2048]{1,0:T(8,128)(2,1)}, bf16[64,2048]{1,0:T(8,128)(2,1)S(1)}, u32[]{:S(2)}, u32[]{:S(2)}) %collective-permute-start.20) | collective-permute-done | bytes 262176 | tf_op jit(solution)/shard_map/ppermute | solution.py:36
  142.2 8.6 %collective-permute-start.22 = (bf16[64,2048]{1,0:T(8,128)(2,1)S(1)}, bf16[64,2048]{1,0:T(8,128)(2,1)}, u32[]{:S(2)}, u32[]{:S(2)}) collective-permute-start(bf16[64,2048]{1,0:T(8,128)(2,1)S(1)} %collective-permute-done.20.refs_7_), channel_id=1, source_target_pairs={{0,32},{32,64},{64,96},{96,0},{1,33},{33,65},{65,97},{97,1},{2,34}... | collective-permute-start | bytes 786440 | tf_op jit(solution)/shard_map/ppermute | solution.py:36
  150.8 7.8 %shard_map.212.refs_9_ = f32[512,1408]{1,0:T(8,128)} custom-call(bf16[512,2048]{1,0:T(8,128)(2,1)} %get-tuple-element.212.left_ref.dy_ref, bf16[2048,1920]{1,0:T(8,128)(2,1)} %all-gather.3.cloned.1.call-done.w_ref.right_ref.refs_2_), custom_call_target="tpu_custom_call" | custom-call | flops 2952790016 | bytes 11534336 | tf_op jit(solution)/shard_map/pallas_call | solution.py:705
  159.3 17.9 %shard_map.213 = (bf16[512,4224]{1,0:T(8,128)(2,1)}, bf16[512,2048]{1,0:T(8,128)(2,1)}, bf16[512,1024]{1,0:T(8,128)(2,1)}, bf16[128,2048]{1,0:T(8,128)(2,1)}, bf...) custom-call(s32[1]{0:T(128)} %bitcast.at_ref.place_ref.core_ref.refs_0_, ...), custom_call_target="tpu_custom_call" | custom-call | flops 11811160064 | bytes 26214400 | tf_op jit(solution)/shard_map/pallas_call | solution.py:793
  177.8 3.6 %collective-permute-start.29 = (bf16[128,2048]{1,0:T(8,128)(2,1)}, bf16[128,2048]{1,0:T(8,128)(2,1)}, u32[]{:S(2)}, u32[]{:S(2)}) collective-permute-start(bf16[128,2048]{1,0:T(8,128)(2,1)} %get-tuple-element.227), channel_id=1, source_target_pairs={{0,96},{32,0},{64,32},{96,64},{1,97},{33,1},{65,33},{97,65},{2,98}... | collective-permute-start | bytes 1572872 | tf_op jit(solution)/shard_map/ppermute | solution.py:36
  182.9 7.2 %shard_map.214 = (bf16[128,2048]{1,0:T(8,128)(2,1)}, bf16[128,2048]{1,0:T(8,128)(2,1)}, bf16[128,2048]{1,0:T(8,128)(2,1)}, bf16[128,2048]{1,0:T(8,128)(2,1)}) custom-call(bf16[512,4224]{1,0:T(8,128)(2,1)} %get-tuple-element.216.left_ref.right_ref, bf16[2048,1920]{1,0:T(8,128)(2,1)} %all-gather.3.cloned.1.call-done.w_ref.right_ref.refs_2_), custom_call_target="tpu_custom_call" | custom-call | flops 2952790016 | bytes 9306112 | tf_op jit(solution)/shard_map/pallas_call | solution.py:878
  190.2 15.2 %shard_map.215 = bf16[1024,4224]{1,0:T(8,128)(2,1)} custom-call(s32[1]{0:T(128)} %bitcast.at_ref.place_ref.core_ref.refs_0_, bf16[512,2048]{1,0:T(8,128)(2,1)} %get-tuple-element.215.x_ref, bf16[512,1024]{1,0:T(8,128)(2,1)} %collective-permute-done.27.x2_ref, bf16[512,2048]{1,0:T(8,128)(2,1)} %get-tuple-element.212.left_ref.dy_ref, ...), custom_call_target="tpu_custom_call" | custom-call | flops 8858370048 | bytes 25165824 | tf_op jit(solution)/shard_map/pallas_call | solution.py:857
  206.2 4.2 %shard_map.216 = (f32[128,2048]{1,0:T(8,128)}, bf16[128,2048]{1,0:T(8,128)(2,1)}, f32[8,2048]{1,0:T(8,128)}) custom-call(f32[128,2048]{1,0:T(8,128)} %get-tuple-element.202.h_ref, bf16[128,2048]{1,0:T(8,128)(2,1)} %get-tuple-element.203.own_ref.dy_ref, f32[2,2048]{1,0:T(2,128)} %get-tuple-element.197.gain_ref.norm_ref, ...), custom_call_target="tpu_custom_call" | custom-call | flops 1576960 | bytes 7372800 | tf_op jit(solution)/shard_map/pallas_call | solution.py:185
  213.7 8.6 %shard_map.217 = (bf16[128,512]{1,0:T(8,128)(2,1)}, f32[1536,128]{1,0:T(8,128)}, f32[1536,128]{1,0:T(8,128)}) custom-call(s32[1]{0:T(128)} %bitcast.at_ref.place_ref.core_ref.refs_0_, bf16[512,512]{1,0:T(8,128)(2,1)} %get-tuple-element.192.q_ref.refs_1_, bf16[2048,1920]{1,0:T(8,128)(2,1)} %all-gather.3.cloned.1.call-done.w_ref.right_ref.refs_2_, ...), custom_call_target="tpu_custom_call" | custom-call | flops 1509949440 | bytes 6291456 | tf_op jit(solution)/shard_map/pallas_call | solution.py:664
  227.2 13.3 %shard_map.218 = (bf16[256,512]{1,0:T(8,128)(2,1)}, f32[1536,128]{1,0:T(8,128)}, f32[1536,128]{1,0:T(8,128)}) custom-call(s32[1]{0:T(128)} %bitcast.at_ref.place_ref.core_ref.refs_0_, bf16[512,512]{1,0:T(8,128)(2,1)} %get-tuple-element.192.q_ref.refs_1_, bf16[2048,1920]{1,0:T(8,128)(2,1)} %all-gather.3.cloned.1.call-done.w_ref.right_ref.refs_2_, ...), custom_call_target="tpu_custom_call" | custom-call | flops 3019898880 | bytes 6291456 | tf_op jit(solution)/shard_map/pallas_call | solution.py:664
  245.2 8.7 %shard_map.219 = (bf16[128,512]{1,0:T(8,128)(2,1)}, bf16[512,128]{1,0:T(8,128)(2,1)}, bf16[512,128]{1,0:T(8,128)(2,1)}, f32[512,128]{1,0:T(8,128)}) custom-call(s32[1]{0:T(128)} %bitcast.at_ref.place_ref.core_ref.refs_0_, bf16[512,512]{1,0:T(8,128)(2,1)} %get-tuple-element.192.q_ref.refs_1_, ...), custom_call_target="tpu_custom_call" | custom-call | flops 1509949440 | bytes 6291456 | tf_op jit(solution)/shard_map/pallas_call | solution.py:664
  256.5 7.6 %shard_map.220 = (bf16[1024,1024]{1,0:T(8,128)(2,1)}, bf16[1024,1024]{1,0:T(8,128)(2,1)}) custom-call(s32[1]{0:T(128)} %bitcast.at_ref.place_ref.core_ref.refs_0_, bf16[512,2048]{1,0:T(8,128)(2,1)} %constant_dynamic-update-slice_fusion.x_ref, bf16[128,2048]{1,0:T(8,128)(2,1)} %get-tuple-element.250.refs_11_.dh0, ...), custom_call_target="tpu_custom_call" | custom-call | flops 2147483648 | bytes 10485760 | tf_op jit(solution)/shard_map/pallas_call | solution.py:953
  266.8 7.8 %shard_map.221 = (bf16[1024,128]{1,0:T(8,128)(2,1)}, bf16[1024,128]{1,0:T(8,128)(2,1)}, bf16[512,2048]{1,0:T(8,128)(2,1)}, f32[16,256]{1,0:T(8,128)}) custom-call(s32[1]{0:T(128)} %bitcast.at_ref.place_ref.core_ref.refs_0_, bf16[512,2048]{1,0:T(8,128)(2,1)} %constant_dynamic-update-slice_fusion.x_ref, bf16[2048,640]{1,0:T(8,128)(2,1)} %get-tuple-element.181.w_ref, ...), custom_call_target="tpu_custom_call" | custom-call | flops 1610612736 | bytes 10485760 | tf_op jit(solution)/shard_map/pallas_call | solution.py:1039
  288.2 5.2 %shard_map.223 = (bf16[272,640]{1,0:T(8,128)(2,1)}, bf16[272,640]{1,0:T(8,128)(2,1)}, bf16[272,640]{1,0:T(8,128)(2,1)}, bf16[272,640]{1,0:T(8,128)(2,1)}, bf16[2...) custom-call(s32[1]{0:T(128)} %bitcast.at_ref.place_ref.core_ref.refs_0_, ...), custom_call_target="tpu_custom_call" | custom-call | flops 2359296 | bytes 7077888 | tf_op jit(solution)/shard_map/pallas_call | solution.py:295
  309.7 8.0 %collective-permute-done.45.refs_1_ = bf16[272,640]{1,0:T(8,128)(2,1)S(1)} collective-permute-done((bf16[272,640]{1,0:T(8,128)(2,1)}, bf16[272,640]{1,0:T(8,128)(2,1)S(1)}, u32[]{:S(2)}, u32[]{:S(2)}) %collective-permute-start.45) | collective-permute-done | bytes 348192 | tf_op jit(solution)/shard_map/ppermute | solution.py:36
  (238 shorter events, 147.0 us)
Async XLA Ops:
  7.2 79.7 %all-gather.3.cloned.1.call-start = ((), (), s32[]{:S(2)}) async-start(), calls=%async_computation.2 | async-start | bytes 8110080 | tf_op jit(solution)/shard_map/all_gather | solution.py:1074
  9.0 149.6 %all-gather.5.cloned.1.call-start = ((), (), s32[]{:S(2)}) async-start(), calls=%async_computation.3 | async-start | bytes 11894784 | tf_op jit(solution)/shard_map/all_gather | solution.py:1077
  10.8 295.9 %reduce-scatter.3.cloned.1.call-start = ((), (), s32[]{:S(2)}) async-start(), calls=%async_computation.4 | async-start | bytes 9191424 | tf_op jit(solution)/shard_map/reduce_scatter | solution.py:1150
  15.7 19.5 %collective-permute-start.7 = (bf16[128,2048]{1,0:T(8,128)(2,1)}, bf16[128,2048]{1,0:T(8,128)(2,1)S(1)}, u32[]{:S(2)}, u32[]{:S(2)}) collective-permute-start(bf16[128,2048]{1,0:T(8,128)(2,1)} %get-tuple-element.172), channel_id=1, source_target_pairs={{0,32},{32,64},{64,96},{96,0},{1,33},{33,65},{65,97},{97,1},{2,34}... | collective-permute-start | bytes 1572872 | tf_op jit(solution)/shard_map/ppermute | solution.py:36
  17.7 17.7 %collective-permute-start = (bf16[128,2048]{1,0:T(8,128)(2,1)}, bf16[128,2048]{1,0:T(8,128)(2,1)S(1)}, u32[]{:S(2)}, u32[]{:S(2)}) collective-permute-start(bf16[128,2048]{1,0:T(8,128)(2,1)} %get-tuple-element.172), channel_id=1, source_target_pairs={{0,96},{32,0},{64,32},{96,64},{1,97},{33,1},{65,33},{97,65},{2,98}... | collective-permute-start | bytes 1572872 | tf_op jit(solution)/shard_map/ppermute | solution.py:36
  31.0 17.8 %collective-permute-start.5 = (bf16[256,640]{1,0:T(8,128)(2,1)S(1)}, bf16[256,640]{1,0:T(8,128)(2,1)S(1)}, u32[]{:S(2)}, u32[]{:S(2)}) collective-permute-start(bf16[256,640]{1,0:T(8,128)(2,1)S(1)} %pad_maximum_fusion.1), channel_id=1, source_target_pairs={{0,16},{8,24},{16,0},{24,8},{1,17},{9,25},{17,1},{25,9},{2,18},{10... | collective-permute-start | bytes 983048 | tf_op jit(solution)/shard_map/ppermute | solution.py:36
  58.6 34.3 %collective-permute-start.15 = (bf16[128,2048]{1,0:T(8,128)(2,1)}, bf16[128,2048]{1,0:T(8,128)(2,1)}, u32[]{:S(2)}, u32[]{:S(2)}) collective-permute-start(bf16[128,2048]{1,0:T(8,128)(2,1)} %bitcast.2.dy_ref), channel_id=1, source_target_pairs={{0,32},{32,64},{64,96},{96,0},{1,33},{33,65},{65,97},{97,1},{2,34}... | collective-permute-start | bytes 1572872 | tf_op jit(solution)/shard_map/ppermute | solution.py:36
  59.6 33.3 %collective-permute-start.14 = (bf16[128,2048]{1,0:T(8,128)(2,1)}, bf16[128,2048]{1,0:T(8,128)(2,1)}, u32[]{:S(2)}, u32[]{:S(2)}) collective-permute-start(bf16[128,2048]{1,0:T(8,128)(2,1)} %bitcast.2.dy_ref), channel_id=1, source_target_pairs={{0,64},{32,96},{64,0},{96,32},{1,65},{33,97},{65,1},{97,33},{2,66}... | collective-permute-start | bytes 1572872 | tf_op jit(solution)/shard_map/ppermute | solution.py:36
  62.7 30.3 %collective-permute-start.13 = (bf16[128,2048]{1,0:T(8,128)(2,1)}, bf16[128,2048]{1,0:T(8,128)(2,1)}, u32[]{:S(2)}, u32[]{:S(2)}) collective-permute-start(bf16[128,2048]{1,0:T(8,128)(2,1)} %bitcast.2.dy_ref), channel_id=1, source_target_pairs={{0,96},{32,0},{64,32},{96,64},{1,97},{33,1},{65,33},{97,65},{2,98}... | collective-permute-start | bytes 1572872 | tf_op jit(solution)/shard_map/ppermute | solution.py:36
  92.9 16.4 %collective-permute-start.16 = (bf16[128,2048]{1,0:T(8,128)(2,1)}, bf16[128,2048]{1,0:T(8,128)(2,1)S(1)}, u32[]{:S(2)}, u32[]{:S(2)}) collective-permute-start(bf16[128,2048]{1,0:T(8,128)(2,1)} %get-tuple-element.189), channel_id=1, source_target_pairs={{0,64},{32,96},{64,0},{96,32},{1,65},{33,97},{65,1},{97,33},{2,66}... | collective-permute-start | bytes 1572872 | tf_op jit(solution)/shard_map/ppermute | solution.py:36
  116.7 41.8 %collective-permute-start.25 = (bf16[512,1024]{1,0:T(8,128)(2,1)}, bf16[512,1024]{1,0:T(8,128)(2,1)}, u32[]{:S(2)}, u32[]{:S(2)}) collective-permute-start(bf16[512,1024]{1,0:T(8,128)(2,1)} %get-tuple-element.213), channel_id=1, source_target_pairs={{0,1},{1,0},{2,3},{3,2},{4,5},{5,4},{6,7},{7,6},{8,9},{9,8},{10,11... | collective-permute-start | bytes 3145736 | tf_op jit(solution)/shard_map/ppermute | solution.py:36
  131.5 27.0 %collective-permute-start.19 = (bf16[64,2048]{1,0:T(8,128)(2,1)}, bf16[64,2048]{1,0:T(8,128)(2,1)S(1)}, u32[]{:S(2)}, u32[]{:S(2)}) collective-permute-start(bf16[64,2048]{1,0:T(8,128)(2,1)} %get-tuple-element.204.refs_1_), channel_id=1, source_target_pairs={{0,96},{32,0},{64,32},{96,64},{1,97},{33,1},{65,33},{97,65},{2,98}... | collective-permute-start | bytes 786440 | tf_op jit(solution)/shard_map/ppermute | solution.py:36
  133.3 25.3 %collective-permute-start.24 = (bf16[64,2048]{1,0:T(8,128)(2,1)}, bf16[64,2048]{1,0:T(8,128)(2,1)}, u32[]{:S(2)}, u32[]{:S(2)}) collective-permute-start(bf16[64,2048]{1,0:T(8,128)(2,1)} %get-tuple-element.205.refs_2_), channel_id=1, source_target_pairs={{0,32},{32,64},{64,96},{96,0},{1,33},{33,65},{65,97},{97,1},{2,34}... | collective-permute-start | bytes 786440 | tf_op jit(solution)/shard_map/ppermute | solution.py:36
  138.9 19.7 %collective-permute-start.23 = (bf16[64,2048]{1,0:T(8,128)(2,1)S(1)}, bf16[64,2048]{1,0:T(8,128)(2,1)}, u32[]{:S(2)}, u32[]{:S(2)}) collective-permute-start(bf16[64,2048]{1,0:T(8,128)(2,1)S(1)} %collective-permute-done.21.refs_4_), channel_id=1, source_target_pairs={{0,96},{32,0},{64,32},{96,64},{1,97},{33,1},{65,33},{97,65},{2,98}... | collective-permute-start | bytes 786440 | tf_op jit(solution)/shard_map/ppermute | solution.py:36
  142.2 16.4 %collective-permute-start.22 = (bf16[64,2048]{1,0:T(8,128)(2,1)S(1)}, bf16[64,2048]{1,0:T(8,128)(2,1)}, u32[]{:S(2)}, u32[]{:S(2)}) collective-permute-start(bf16[64,2048]{1,0:T(8,128)(2,1)S(1)} %collective-permute-done.20.refs_7_), channel_id=1, source_target_pairs={{0,32},{32,64},{64,96},{96,0},{1,33},{33,65},{65,97},{97,1},{2,34}... | collective-permute-start | bytes 786440 | tf_op jit(solution)/shard_map/ppermute | solution.py:36
  177.8 27.6 %collective-permute-start.28 = (bf16[128,2048]{1,0:T(8,128)(2,1)}, bf16[128,2048]{1,0:T(8,128)(2,1)S(1)}, u32[]{:S(2)}, u32[]{:S(2)}) collective-permute-start(bf16[128,2048]{1,0:T(8,128)(2,1)} %get-tuple-element.226), channel_id=1, source_target_pairs={{0,32},{32,64},{64,96},{96,0},{1,33},{33,65},{65,97},{97,1},{2,34}... | collective-permute-start | bytes 1572872 | tf_op jit(solution)/shard_map/ppermute | solution.py:36
  177.8 27.6 %collective-permute-start.29 = (bf16[128,2048]{1,0:T(8,128)(2,1)}, bf16[128,2048]{1,0:T(8,128)(2,1)}, u32[]{:S(2)}, u32[]{:S(2)}) collective-permute-start(bf16[128,2048]{1,0:T(8,128)(2,1)} %get-tuple-element.227), channel_id=1, source_target_pairs={{0,96},{32,0},{64,32},{96,64},{1,97},{33,1},{65,33},{97,65},{2,98}... | collective-permute-start | bytes 1572872 | tf_op jit(solution)/shard_map/ppermute | solution.py:36
  181.4 24.5 %collective-permute-start.30 = (bf16[128,2048]{1,0:T(8,128)(2,1)}, bf16[128,2048]{1,0:T(8,128)(2,1)}, u32[]{:S(2)}, u32[]{:S(2)}) collective-permute-start(bf16[128,2048]{1,0:T(8,128)(2,1)} %get-tuple-element.228), channel_id=1, source_target_pairs={{0,64},{32,96},{64,0},{96,32},{1,65},{33,97},{65,1},{97,33},{2,66}... | collective-permute-start | bytes 1572872 | tf_op jit(solution)/shard_map/ppermute | solution.py:36
  206.2 122.5 %reduce-scatter.5.cloned.1.call-start = ((), (), s32[]{:S(2)}) async-start(), calls=%async_computation.5 | async-start | bytes 2621440 | tf_op jit(solution)/shard_map/reduce_scatter | solution.py:1188
  240.5 25.7 %collective-permute-start.36 = (bf16[128,2048]{1,0:T(8,128)(2,1)}, bf16[128,2048]{1,0:T(8,128)(2,1)S(1)}, u32[]{:S(2)}, u32[]{:S(2)}) collective-permute-start(bf16[128,2048]{1,0:T(8,128)(2,1)} %get-tuple-element.266), channel_id=1, source_target_pairs={{0,32},{32,64},{64,96},{96,0},{1,33},{33,65},{65,97},{97,1},{2,34}... | collective-permute-start | bytes 1572872 | tf_op jit(solution)/shard_map/ppermute | solution.py:36
  243.0 23.2 %collective-permute-start.37 = (bf16[128,2048]{1,0:T(8,128)(2,1)}, bf16[128,2048]{1,0:T(8,128)(2,1)}, u32[]{:S(2)}, u32[]{:S(2)}) collective-permute-start(bf16[128,2048]{1,0:T(8,128)(2,1)} %get-tuple-element.267), channel_id=1, source_target_pairs={{0,96},{32,0},{64,32},{96,64},{1,97},{33,1},{65,33},{97,65},{2,98}... | collective-permute-start | bytes 1572872 | tf_op jit(solution)/shard_map/ppermute | solution.py:36
  243.8 22.4 %collective-permute-start.38 = (bf16[128,2048]{1,0:T(8,128)(2,1)}, bf16[128,2048]{1,0:T(8,128)(2,1)}, u32[]{:S(2)}, u32[]{:S(2)}) collective-permute-start(bf16[128,2048]{1,0:T(8,128)(2,1)} %get-tuple-element.268), channel_id=1, source_target_pairs={{0,64},{32,96},{64,0},{96,32},{1,65},{33,97},{65,1},{97,33},{2,66}... | collective-permute-start | bytes 1572872 | tf_op jit(solution)/shard_map/ppermute | solution.py:36
  300.5 17.1 %collective-permute-start.45 = (bf16[272,640]{1,0:T(8,128)(2,1)}, bf16[272,640]{1,0:T(8,128)(2,1)S(1)}, u32[]{:S(2)}, u32[]{:S(2)}) collective-permute-start(bf16[272,640]{1,0:T(8,128)(2,1)} %get-tuple-element.287), channel_id=1, source_target_pairs={{0,2},{2,4},{4,6},{6,0},{1,3},{3,5},{5,7},{7,1},{8,10},{10,12},{12... | collective-permute-start | bytes 1044488 | tf_op jit(solution)/shard_map/ppermute | solution.py:36
  300.5 17.1 %collective-permute-start.46 = (bf16[272,640]{1,0:T(8,128)(2,1)}, bf16[272,640]{1,0:T(8,128)(2,1)S(1)}, u32[]{:S(2)}, u32[]{:S(2)}) collective-permute-start(bf16[272,640]{1,0:T(8,128)(2,1)} %get-tuple-element.288), channel_id=1, source_target_pairs={{0,4},{2,6},{4,0},{6,2},{1,5},{3,7},{5,1},{7,3},{8,12},{10,14},{12... | collective-permute-start | bytes 1044488 | tf_op jit(solution)/shard_map/ppermute | solution.py:36
  (78 other events, 636.0 us)
Sparse Core Ops, SparseCore 0:
  10.3 60.5 all-gather.2
  73.8 59.8 all-gather.4
  206.1 87.4 reduce-scatter.2
  295.9 29.2 reduce-scatter.4
where the time goes:
time: 346 us; the launch traced here: 343 us
  Pallas kernels  161 us (47%)
  starting transfers between devices  93.2 us (27%)
  waiting for transfers between devices  43.9 us (13%)
  local copies, waits for them, and re-layouts  18.2 us (5%)
  between operations  14.6 us (4%)
  other arithmetic  12 us (3%)
    ppermute x53, starting transfers between devices, shift(): lax.ppermute(value, axis, [(i, (i + distance) % size) for i in range(size)])  86.8 us
    ppermute x53, waiting for transfers between devices, shift(): lax.ppermute(value, axis, [(i, (i + distance) % size) for i in range(size)])  41.8 us
    pallas_call x3, Pallas kernels, attend_back(): pl.pallas_call(functools.partial(attend_back_kernel, first, step, count),...  30.6 us
    pallas_call x3, Pallas kernels, attend(): pl.pallas_call(functools.partial(attend_kernel, first, step), grid_spec=g...  22.4 us
    pallas_call x1, Pallas kernels, ffn(): pl.pallas_call(ffn_kernel, out_shape=(jax.ShapeDtypeStruct((rows, 3 * HID...  17.9 us
    pallas_call x5, Pallas kernels, small_call(): pl.pallas_call(kernel, out_shape=tuple((jax.ShapeDtypeStruct(shape, dtype...  15.9 us
    pallas_call x1, Pallas kernels, weight_grads(): pl.pallas_call(weight_grads_kernel, grid_spec=grid, out_shape=jax.ShapeDt...  15.2 us
    unnamed x91, local copies, waits for them, and re-layouts  15 us
  transfers between devices with their start and end apart: 61, of which 19 were waited for; matrix products, arithmetic and copies ran while one was open for 6% of the time, Pallas kernels for 41%

commit v1 on v0

--- a/solution.py
+++ b/solution.py
@@ -344,32 +344,69 @@
     two_ref[...] = jnp.concatenate([gains[k : k + 1] for k in range(8, 16)], 1)
 
 
-def put_in_order(at_ref, own_ref, other_ref, columns, to_ref, sems):
+def put_in_order(at_ref, piece_refs, columns, to_ref, sems):
     x, y, core = x_of(at_ref), y_of(at_ref), core_of(at_ref)
     copies = []
     for number in range(32):
-        ref = (own_ref, other_ref)[number // 16]
         to_x, to_y = lax.rem(x + number % 4, 4), lax.rem(y + number // 4 % 4, 4)
         to_core = core if number < 16 else 1 - core
         row = pl.multiple_of(((to_core * 4 + to_y) * 4 + to_x) * 64, 64)
         copy = pltpu.make_async_copy(
-            ref.at[pl.ds(number % 16 * 64, 64), columns], to_ref.at[pl.ds(row, 64)], sems.at[number]
+            piece_refs[number // 4].at[pl.ds(number % 4 * 64, 64), columns],
+            to_ref.at[pl.ds(row, 64)],
+            sems.at[number],
         )
         copy.start()
         copies.append(copy)
     return copies
 
 
-def project_kv_kernel(at_ref, x_ref, own_ref, other_ref, cos_ref, sin_ref, kv_ref, held, sems):
-    for copy in put_in_order(at_ref, own_ref, other_ref, pl.ds(512, 128), held, sems):
+RING_PIECES = [(0, 128), (128, 128), (256, 64), (320, 64), (384, 128)]
+
+
+def project_kv_kernel(at_ref, *refs):
+    x_refs, piece_refs, (cos_ref, sin_ref, kv_ref, whole_ref) = refs[:5], refs[5:13], refs[13:17]
+    x_held, held, sems, x_sems = refs[17:]
+    copies = []
+    for number, (start, size) in enumerate(RING_PIECES):
+        copy = pltpu.make_async_copy(x_refs[number], x_held.at[pl.ds(start, size)], x_sems.at[number])
+        copy.start()
+        copies.append(copy)
+    copies += put_in_order(at_ref, piece_refs, pl.ds(512, 128), held, sems)
+    for copy in copies:
         copy.wait()
-    flat = dot_nn(x_ref[...], held[...])
+    whole = pltpu.make_async_copy(x_held, whole_ref, x_sems.at[len(RING_PIECES)])
+    whole.start()
+    flat = dot_nn(x_held[...], held[...])
     turned = turn(flat, cos_ref[...], sin_ref[...])
     kv_ref[...] = jnp.where(lane_is_low(flat.shape, 128), turned, flat).astype(BF16)
-
-
-def project_q_kernel(at_ref, x_ref, own_ref, other_ref, cos_ref, sin_ref, q_ref, w_ref, held, sems, sem):
-    for copy in put_in_order(at_ref, own_ref, other_ref, pl.ds(0, 640), held, sems):
+    whole.wait()
+
+
+def project_kv(at, x_pieces, weights, cosine, sine):
+    rows, width = 512, x_pieces[0].shape[1]
+    vmem, anywhere = pl.BlockSpec(memory_space=pltpu.VMEM), pl.BlockSpec(memory_space=pl.ANY)
+    return pl.pallas_call(
+        project_kv_kernel,
+        out_shape=(jax.ShapeDtypeStruct((rows, 128), BF16), jax.ShapeDtypeStruct((rows, width), BF16)),
+        in_specs=[pl.BlockSpec(memory_space=pltpu.SMEM)] + [anywhere] * 13 + [vmem, vmem],
+        out_specs=(vmem, anywhere),
+        scratch_shapes=[
+            pltpu.VMEM((rows, width), BF16),
+            pltpu.VMEM((width, 128), BF16),
+            pltpu.SemaphoreType.DMA((32,)),
+            pltpu.SemaphoreType.DMA((len(RING_PIECES) + 1,)),
+        ],
+        compiler_params=pltpu.CompilerParams(vmem_limit_bytes=VMEM_LIMIT),
+        cost_estimate=pl.CostEstimate(
+            flops=2 * rows * width * 128, bytes_accessed=5 * 1024 * 1024, transcendentals=0
+        ),
+    )(at, *x_pieces, *weights, cosine, sine)
+
+
+def project_q_kernel(at_ref, x_ref, *refs):
+    piece_refs, (cos_ref, sin_ref, q_ref, w_ref, held, sems, sem) = refs[:8], refs[8:]
+    for copy in put_in_order(at_ref, piece_refs, pl.ds(0, 640), held, sems):
         copy.wait()
     whole = pltpu.make_async_copy(held, w_ref, sem)
     whole.start()
@@ -382,27 +419,22 @@
     whole.wait()
 
 
-def project(kernel, at, normed, weights, cosine, sine, columns, held_columns, hand_out):
+def project_q(at, normed, weights, cosine, sine):
     rows, width = normed.shape
     vmem, anywhere = pl.BlockSpec(memory_space=pltpu.VMEM), pl.BlockSpec(memory_space=pl.ANY)
-    out_shape = [jax.ShapeDtypeStruct((rows, columns), BF16)]
-    out_specs = [vmem]
-    scratch = [pltpu.VMEM((width, held_columns), BF16), pltpu.SemaphoreType.DMA((32,))]
-    if hand_out:
-        out_shape.append(jax.ShapeDtypeStruct((width, held_columns), BF16))
-        out_specs.append(anywhere)
-        scratch.append(pltpu.SemaphoreType.DMA)
     return pl.pallas_call(
-        kernel,
-        out_shape=tuple(out_shape),
-        in_specs=[pl.BlockSpec(memory_space=pltpu.SMEM), vmem, anywhere, anywhere, vmem, vmem],
-        out_specs=tuple(out_specs),
-        scratch_shapes=scratch,
-        compiler_params=pltpu.CompilerParams(vmem_limit_bytes=VMEM_LIMIT),
-        cost_estimate=pl.CostEstimate(
-            flops=2 * rows * width * columns,
-            bytes_accessed=2 * (rows * width + width * columns + rows * columns),
-            transcendentals=0,
+        project_q_kernel,
+        out_shape=(jax.ShapeDtypeStruct((rows, 512), BF16), jax.ShapeDtypeStruct((width, 640), BF16)),
+        in_specs=[pl.BlockSpec(memory_space=pltpu.SMEM), vmem] + [anywhere] * 8 + [vmem, vmem],
+        out_specs=(vmem, anywhere),
+        scratch_shapes=[
+            pltpu.VMEM((width, 640), BF16),
+            pltpu.SemaphoreType.DMA((32,)),
+            pltpu.SemaphoreType.DMA,
+        ],
+        compiler_params=pltpu.CompilerParams(vmem_limit_bytes=VMEM_LIMIT),
+        cost_estimate=pl.CostEstimate(
+            flops=2 * rows * width * 512, bytes_accessed=7 * 1024 * 1024, transcendentals=0
         ),
     )(at, normed, *weights, cosine, sine)
 
@@ -1079,18 +1111,6 @@
     x_rows, dy_rows, normed_rows, gains = prepare(
         tokens[0], cotangent[0], jnp.stack([norm_attn, norm_ffn]).astype(F32)
     )
-    normed_rows, w_query = keep((normed_rows, w_query))
-    ahead, behind = near_pieces(normed_rows)
-    qkv_own = gather_axis(jnp.concatenate([w_query, key_projection, value_projection], 1), "x")
-    qkv_own = gather_axis(jnp.concatenate(qkv_own, 0), "y")
-    far = far_pieces(ahead, behind)
-    qkv_own, far = keep((qkv_own, far))
-    qkv_own = jnp.concatenate(qkv_own, 0)
-    qkv_pieces = qkv_own, shift(qkv_own, "core", 1)
-    normed_one = jnp.concatenate([normed_rows, ahead, *far, behind], 0)
-    dy_raw, far = keep((cotangent[0], far))
-    dy_pieces = gather_pieces(dy_raw)
-
     row = jnp.arange(512, dtype=jnp.int32)
     positions = block * 512 + ((row // 128 + place) % 4) * 128 + row % 128
     frequency = 10000.0 ** (-jnp.arange(32, dtype=F32) * 2.0 / HEAD_SIZE)
@@ -1099,21 +1119,25 @@
     cosine = jnp.concatenate([cosine] * 4, 1)
     sine = jnp.concatenate([-sine, sine, -sine, sine], 1)
 
-    (kv_own,) = project(
-        project_kv_kernel, code, normed_one, qkv_pieces, cosine, sine, 128, 128, False
-    )
-    normed_late, kv_own = keep((normed_one, kv_own))
-    kv = (from_block(kv_own, 2), from_block(kv_own, 1), kv_own)
-    queries, qkv_weights = project(
-        project_q_kernel, code, normed_late, qkv_pieces, cosine, sine, 512, 640, True
-    )
-
     flat = segments.reshape(-1)
     padded = jnp.concatenate([jnp.full((1024,), -1, jnp.int32), flat])
     own = lax.dynamic_slice_in_dim(flat, block * 512, 512, 0)
     window = lax.dynamic_slice_in_dim(padded, block * 512, 1536, 0)
     start = jnp.sum((window[None, :] < own[:, None]).astype(jnp.int32), 1)
     low = jnp.maximum(start, row + 1).reshape(1, 512)
+
+    normed_rows, w_query = keep((normed_rows, w_query))
+    ahead, behind = near_pieces(normed_rows)
+    qkv_own = gather_axis(jnp.concatenate([w_query, key_projection, value_projection], 1), "x")
+    qkv_own = gather_axis(jnp.concatenate(qkv_own, 0), "y")
+    far = far_pieces(ahead, behind)
+    qkv_own, far, cosine, sine, low = keep((qkv_own, far, cosine, sine, low))
+    qkv_pieces = *qkv_own, *(shift(piece, "core", 1) for piece in qkv_own)
+    kv_own, normed_one = project_kv(code, (normed_rows, ahead, *far, behind), qkv_pieces, cosine, sine)
+    normed_late, kv_own, dy_raw = keep((normed_one, kv_own, cotangent[0]))
+    dy_pieces = gather_pieces(dy_raw)
+    kv = (from_block(kv_own, 2), from_block(kv_own, 1), kv_own)
+    queries, qkv_weights = project_q(code, normed_late, qkv_pieces, cosine, sine)
 
     kk, vv, kvt = set_up(code, kv)
     seen = code, queries, kk, kvt, low, out_weights

time: 346 us -> 337 us (0.974)
  local copies, waits for them, and re-layouts: 18.2 us -> 8.69 us
  starting transfers between devices: 93.2 us -> 99.2 us
  waiting for transfers between devices: 43.9 us -> 39.6 us
    unnamed x91 -> x90, local copies, waits for them, and re-layouts: 15 us -> 7.1 us
    ppermute x53 -> x56, starting transfers between devices: 86.8 us -> 92.4 us  [shift(): lax.ppermute(value, axis, [(i, (i + distance) % size) for i in range(size)])]
    ppermute x53 -> x56, waiting for transfers between devices: 41.8 us -> 37.7 us  [shift(): lax.ppermute(value, axis, [(i, (i + distance) % size) for i in range(size)])]
  transfers between devices with their start and end apart: 61 -> 64, of which waited for: 19 -> 22; matrix products, arithmetic and copies ran while one was open for 6% -> 3% of each run, Pallas kernels for 41% -> 42%
where the time goes in v1:
time: 337 us; the launch traced here: 333 us
  Pallas kernels  161 us (48%)
  starting transfers between devices  99.2 us (29%)
  waiting for transfers between devices  39.6 us (12%)
  between operations  14.6 us (4%)
  other arithmetic  9.73 us (3%)
  local copies, waits for them, and re-layouts  8.69 us (3%)
    ppermute x56, starting transfers between devices, shift(): lax.ppermute(value, axis, [(i, (i + distance) % size) for i in range(size)])  92.4 us
    ppermute x56, waiting for transfers between devices, shift(): lax.ppermute(value, axis, [(i, (i + distance) % size) for i in range(size)])  37.7 us
    pallas_call x3, Pallas kernels, attend_back(): pl.pallas_call(functools.partial(attend_back_kernel, first, step, count),...  30.6 us
    pallas_call x3, Pallas kernels, attend(): pl.pallas_call(functools.partial(attend_kernel, first, step), grid_spec=g...  22.3 us
    pallas_call x1, Pallas kernels, ffn(): pl.pallas_call(ffn_kernel, out_shape=(jax.ShapeDtypeStruct((rows, 3 * HID...  17.9 us
    pallas_call x5, Pallas kernels, small_call(): pl.pallas_call(kernel, out_shape=tuple((jax.ShapeDtypeStruct(shape, dtype...  15.7 us
    pallas_call x1, Pallas kernels, weight_grads(): pl.pallas_call(weight_grads_kernel, grid_spec=grid, out_shape=jax.ShapeDt...  15.3 us
    pallas_call x1, Pallas kernels, finish(): pl.pallas_call(finish_kernel, grid_spec=grid, out_shape=(jax.ShapeDtypeSt...  7.82 us
  transfers between devices with their start and end apart: 64, of which 22 were waited for; matrix products, arithmetic and copies ran while one was open for 3% of the time, Pallas kernels for 42%

profile of v1, /device:TPU:0, one launch (start us, length us, event | category | flops | bytes accessed | tf_op | source)
XLA Modules:
  0.0 333.1 jit_solution(16800324897633237424)
XLA Ops:
  42.2 5.4 %collective-permute-done.5.refs_7_.refs_2_ = bf16[256,640]{1,0:T(8,128)(2,1)S(1)} collective-permute-done((bf16[256,640]{1,0:T(8,128)(2,1)S(1)}, bf16[256,640]{1,0:T(8,128)(2,1)S(1)}, u32[]{:S(2)}, u32[]{:S(2)}) %collective-permute-start.5) | collective-permute-done | bytes 327712 | tf_op jit(solution)/shard_map/ppermute | solution.py:36
  51.8 5.3 %shard_map.204 = (bf16[512,128]{1,0:T(8,128)(2,1)}, bf16[512,2048]{1,0:T(8,128)(2,1)}) custom-call(s32[1]{0:T(128)} %bitcast.at_ref.place_ref.core_ref.refs_0_, bf16[128,2048]{1,0:T(8,128)(2,1)} %get-tuple-element.177.refs_0_, bf16[128,2048]{1,0:T(8,128)(2,1)} %copy-done.9, bf16[64,2048]{1,0:T(8,128)(2,1)} %copy-done.22, bf16[64,2048]{1,0:T(8,128)(2,1)} %copy-done.23, ...), custom_call_target="tpu_custom_call" | custom-call | flops 268435456 | bytes 5242880 | tf_op jit(solution)/shard_map/pallas_call | solution.py:389
  57.5 3.7 %collective-permute-start.17 = (bf16[128,2048]{1,0:T(8,128)(2,1)}, bf16[128,2048]{1,0:T(8,128)(2,1)}, u32[]{:S(2)}, u32[]{:S(2)}) collective-permute-start(bf16[128,2048]{1,0:T(8,128)(2,1)} %bitcast.25), channel_id=1, source_target_pairs={{0,64},{32,96},{64,0},{96,32},{1,65},{33,97},{65,1},{97,33},{2,66}... | collective-permute-start | bytes 1572872 | tf_op jit(solution)/shard_map/ppermute | solution.py:36
  66.3 6.4 %shard_map.205 = (bf16[512,512]{1,0:T(8,128)(2,1)}, bf16[2048,640]{1,0:T(8,128)(2,1)}) custom-call(s32[1]{0:T(128)} %bitcast.at_ref.place_ref.core_ref.refs_0_, bf16[512,2048]{1,0:T(8,128)(2,1)} %get-tuple-element.189.x_ref, bf16[256,640]{1,0:T(8,128)(2,1)} %copy-done, bf16[256,640]{1,0:T(8,128)(2,1)} %copy-done.3, bf16[256,640]{1,0:T(8,128)(2,1)} %copy-done.2, ...), custom_call_target="tpu_custom_call" | custom-call | flops 1073741824 | bytes 7340032 | tf_op jit(solution)/shard_map/pallas_call | solution.py:425
  76.5 6.0 %shard_map.207 = (bf16[128,512]{1,0:T(8,128)(2,1)}, f32[1,4,1,256]{3,2,1,0:T(1,128)}, bf16[128,2048]{1,0:T(8,128)(2,1)}) custom-call(s32[1]{0:T(128)} %bitcast.at_ref.place_ref.core_ref.refs_0_, bf16[512,512]{1,0:T(8,128)(2,1)} %get-tuple-element.202.q_ref.refs_1_, bf16[1536,128]{1,0:T(8,128)(2,1)} %get-tuple-element.193.kk_ref.refs_4_, ...), custom_call_target="tpu_custom_call" | custom-call | flops 603979776 | bytes 3145728 | tf_op jit(solution)/shard_map/pallas_call | solution.py:564
  86.8 10.3 %shard_map.208 = (bf16[256,512]{1,0:T(8,128)(2,1)}, f32[2,4,1,256]{3,2,1,0:T(1,128)}, bf16[128,2048]{1,0:T(8,128)(2,1)}, bf16[128,2048]{1,0:T(8,128)(2,1)}) custom-call(s32[1]{0:T(128)} %bitcast.at_ref.place_ref.core_ref.refs_0_, bf16[512,512]{1,0:T(8,128)(2,1)} %get-tuple-element.202.q_ref.refs_1_, bf16[1536,128]{1,0:T(8,128)(2,1)} %get-tuple-element.193.kk_ref.refs_4_, ...), custom_call_target="tpu_custom_call" | custom-call | flops 1207959552 | bytes 3145728 | tf_op jit(solution)/shard_map/pallas_call | solution.py:564
  102.9 4.0 %shard_map.211 = (bf16[512,2048]{1,0:T(8,128)(2,1)}, bf16[512,1024]{1,0:T(8,128)(2,1)}) custom-call(s32[1]{0:T(128)} %bitcast.at_ref.place_ref.core_ref.refs_0_, bf16[128,2048]{1,0:T(8,128)(2,1)} %get-tuple-element.213.own_ref.dy_ref, bf16[128,2048]{1,0:T(8,128)(2,1)} %collective-permute-done.16.ahead_ref, ...), custom_call_target="tpu_custom_call" | custom-call | flops 4194304 | bytes 5242880 | tf_op jit(solution)/shard_map/pallas_call | solution.py:172
  106.9 6.0 %shard_map.209 = (bf16[128,512]{1,0:T(8,128)(2,1)}, f32[1,4,1,256]{3,2,1,0:T(1,128)}, bf16[128,2048]{1,0:T(8,128)(2,1)}) custom-call(s32[1]{0:T(128)} %bitcast.at_ref.place_ref.core_ref.refs_0_, bf16[512,512]{1,0:T(8,128)(2,1)} %get-tuple-element.202.q_ref.refs_1_, bf16[1536,128]{1,0:T(8,128)(2,1)} %get-tuple-element.193.kk_ref.refs_4_, ...), custom_call_target="tpu_custom_call" | custom-call | flops 603979776 | bytes 3145728 | tf_op jit(solution)/shard_map/pallas_call | solution.py:564
  123.8 5.4 %collective-permute-done.23.refs_7_ = bf16[64,2048]{1,0:T(8,128)(2,1)S(1)} collective-permute-done((bf16[64,2048]{1,0:T(8,128)(2,1)}, bf16[64,2048]{1,0:T(8,128)(2,1)S(1)}, u32[]{:S(2)}, u32[]{:S(2)}) %collective-permute-start.23) | collective-permute-done | bytes 262176 | tf_op jit(solution)/shard_map/ppermute | solution.py:36
  132.4 8.6 %collective-permute-start.25 = (bf16[64,2048]{1,0:T(8,128)(2,1)S(1)}, bf16[64,2048]{1,0:T(8,128)(2,1)}, u32[]{:S(2)}, u32[]{:S(2)}) collective-permute-start(bf16[64,2048]{1,0:T(8,128)(2,1)S(1)} %collective-permute-done.23.refs_7_), channel_id=1, source_target_pairs={{0,32},{32,64},{64,96},{96,0},{1,33},{33,65},{65,97},{97,1},{2,34}... | collective-permute-start | bytes 786440 | tf_op jit(solution)/shard_map/ppermute | solution.py:36
  141.0 7.8 %shard_map.212.refs_9_ = f32[512,1408]{1,0:T(8,128)} custom-call(bf16[512,2048]{1,0:T(8,128)(2,1)} %get-tuple-element.222.left_ref.dy_ref, bf16[2048,1920]{1,0:T(8,128)(2,1)} %all-gather.3.cloned.1.call-done.w_ref.right_ref.refs_2_), custom_call_target="tpu_custom_call" | custom-call | flops 2952790016 | bytes 11534336 | tf_op jit(solution)/shard_map/pallas_call | solution.py:737
  149.5 17.9 %shard_map.213 = (bf16[512,4224]{1,0:T(8,128)(2,1)}, bf16[512,2048]{1,0:T(8,128)(2,1)}, bf16[512,1024]{1,0:T(8,128)(2,1)}, bf16[128,2048]{1,0:T(8,128)(2,1)}, bf...) custom-call(s32[1]{0:T(128)} %bitcast.at_ref.place_ref.core_ref.refs_0_, ...), custom_call_target="tpu_custom_call" | custom-call | flops 11811160064 | bytes 26214400 | tf_op jit(solution)/shard_map/pallas_call | solution.py:825
  168.1 3.6 %collective-permute-start.32 = (bf16[128,2048]{1,0:T(8,128)(2,1)}, bf16[128,2048]{1,0:T(8,128)(2,1)}, u32[]{:S(2)}, u32[]{:S(2)}) collective-permute-start(bf16[128,2048]{1,0:T(8,128)(2,1)} %get-tuple-element.237), channel_id=1, source_target_pairs={{0,96},{32,0},{64,32},{96,64},{1,97},{33,1},{65,33},{97,65},{2,98}... | collective-permute-start | bytes 1572872 | tf_op jit(solution)/shard_map/ppermute | solution.py:36
  173.2 7.2 %shard_map.214 = (bf16[128,2048]{1,0:T(8,128)(2,1)}, bf16[128,2048]{1,0:T(8,128)(2,1)}, bf16[128,2048]{1,0:T(8,128)(2,1)}, bf16[128,2048]{1,0:T(8,128)(2,1)}) custom-call(bf16[512,4224]{1,0:T(8,128)(2,1)} %get-tuple-element.226.left_ref.right_ref, bf16[2048,1920]{1,0:T(8,128)(2,1)} %all-gather.3.cloned.1.call-done.w_ref.right_ref.refs_2_), custom_call_target="tpu_custom_call" | custom-call | flops 2952790016 | bytes 9306112 | tf_op jit(solution)/shard_map/pallas_call | solution.py:910
  180.4 15.3 %shard_map.215 = bf16[1024,4224]{1,0:T(8,128)(2,1)} custom-call(s32[1]{0:T(128)} %bitcast.at_ref.place_ref.core_ref.refs_0_, bf16[512,2048]{1,0:T(8,128)(2,1)} %get-tuple-element.225.x_ref, bf16[512,1024]{1,0:T(8,128)(2,1)} %collective-permute-done.30.x2_ref, bf16[512,2048]{1,0:T(8,128)(2,1)} %get-tuple-element.222.left_ref.dy_ref, ...), custom_call_target="tpu_custom_call" | custom-call | flops 8858370048 | bytes 25165824 | tf_op jit(solution)/shard_map/pallas_call | solution.py:889
  196.5 4.2 %shard_map.216 = (f32[128,2048]{1,0:T(8,128)}, bf16[128,2048]{1,0:T(8,128)(2,1)}, f32[8,2048]{1,0:T(8,128)}) custom-call(f32[128,2048]{1,0:T(8,128)} %get-tuple-element.212.h_ref, bf16[128,2048]{1,0:T(8,128)(2,1)} %get-tuple-element.213.own_ref.dy_ref, f32[2,2048]{1,0:T(2,128)} %get-tuple-element.207.gain_ref.norm_ref, ...), custom_call_target="tpu_custom_call" | custom-call | flops 1576960 | bytes 7372800 | tf_op jit(solution)/shard_map/pallas_call | solution.py:185
  204.0 8.5 %shard_map.217 = (bf16[128,512]{1,0:T(8,128)(2,1)}, f32[1536,128]{1,0:T(8,128)}, f32[1536,128]{1,0:T(8,128)}) custom-call(s32[1]{0:T(128)} %bitcast.at_ref.place_ref.core_ref.refs_0_, bf16[512,512]{1,0:T(8,128)(2,1)} %get-tuple-element.202.q_ref.refs_1_, bf16[2048,1920]{1,0:T(8,128)(2,1)} %all-gather.3.cloned.1.call-done.w_ref.right_ref.refs_2_, ...), custom_call_target="tpu_custom_call" | custom-call | flops 1509949440 | bytes 6291456 | tf_op jit(solution)/shard_map/pallas_call | solution.py:696
  217.4 13.4 %shard_map.218 = (bf16[256,512]{1,0:T(8,128)(2,1)}, f32[1536,128]{1,0:T(8,128)}, f32[1536,128]{1,0:T(8,128)}) custom-call(s32[1]{0:T(128)} %bitcast.at_ref.place_ref.core_ref.refs_0_, bf16[512,512]{1,0:T(8,128)(2,1)} %get-tuple-element.202.q_ref.refs_1_, bf16[2048,1920]{1,0:T(8,128)(2,1)} %all-gather.3.cloned.1.call-done.w_ref.right_ref.refs_2_, ...), custom_call_target="tpu_custom_call" | custom-call | flops 3019898880 | bytes 6291456 | tf_op jit(solution)/shard_map/pallas_call | solution.py:696
  235.5 8.7 %shard_map.219 = (bf16[128,512]{1,0:T(8,128)(2,1)}, bf16[512,128]{1,0:T(8,128)(2,1)}, bf16[512,128]{1,0:T(8,128)(2,1)}, f32[512,128]{1,0:T(8,128)}) custom-call(s32[1]{0:T(128)} %bitcast.at_ref.place_ref.core_ref.refs_0_, bf16[512,512]{1,0:T(8,128)(2,1)} %get-tuple-element.202.q_ref.refs_1_, ...), custom_call_target="tpu_custom_call" | custom-call | flops 1509949440 | bytes 6291456 | tf_op jit(solution)/shard_map/pallas_call | solution.py:696
  246.8 7.5 %shard_map.220 = (bf16[1024,1024]{1,0:T(8,128)(2,1)}, bf16[1024,1024]{1,0:T(8,128)(2,1)}) custom-call(s32[1]{0:T(128)} %bitcast.at_ref.place_ref.core_ref.refs_0_, bf16[512,2048]{1,0:T(8,128)(2,1)} %get-tuple-element.189.x_ref, bf16[128,2048]{1,0:T(8,128)(2,1)} %get-tuple-element.260.refs_11_.dh0, bf16[128,2048]{1,0:T(8,128)(2,1)} %collective-permute-done.34.refs_11_.dh1, ...), custom_call_target="tpu_custom_call" | custom-call | flops 2147483648 | bytes 10485760 | tf_op jit(solution)/shard_map/pallas_call | solution.py:985
  256.8 7.8 %shard_map.221 = (bf16[1024,128]{1,0:T(8,128)(2,1)}, bf16[1024,128]{1,0:T(8,128)(2,1)}, bf16[512,2048]{1,0:T(8,128)(2,1)}, f32[16,256]{1,0:T(8,128)}) custom-call(s32[1]{0:T(128)} %bitcast.at_ref.place_ref.core_ref.refs_0_, bf16[512,2048]{1,0:T(8,128)(2,1)} %get-tuple-element.189.x_ref, bf16[2048,640]{1,0:T(8,128)(2,1)} %get-tuple-element.190.w_ref, ...), custom_call_target="tpu_custom_call" | custom-call | flops 1610612736 | bytes 10485760 | tf_op jit(solution)/shard_map/pallas_call | solution.py:1071
  278.7 5.2 %shard_map.223 = (bf16[272,640]{1,0:T(8,128)(2,1)}, bf16[272,640]{1,0:T(8,128)(2,1)}, bf16[272,640]{1,0:T(8,128)(2,1)}, bf16[272,640]{1,0:T(8,128)(2,1)}, bf16[2...) custom-call(s32[1]{0:T(128)} %bitcast.at_ref.place_ref.core_ref.refs_0_, ...), custom_call_target="tpu_custom_call" | custom-call | flops 2359296 | bytes 7077888 | tf_op jit(solution)/shard_map/pallas_call | solution.py:295
  295.0 6.6 %collective-permute-start.50 = (bf16[272,640]{1,0:T(8,128)(2,1)}, bf16[272,640]{1,0:T(8,128)(2,1)}, u32[]{:S(2)}, u32[]{:S(2)}) collective-permute-start(bf16[272,640]{1,0:T(8,128)(2,1)} %get-tuple-element.299), channel_id=1, source_target_pairs={{0,6},{2,0},{4,2},{6,4},{1,7},{3,1},{5,3},{7,5},{8,14},{10,8},{12,... | collective-permute-start | bytes 1044488 | tf_op jit(solution)/shard_map/ppermute | solution.py:36
  303.7 4.3 %collective-permute-done.49.refs_2_ = bf16[272,640]{1,0:T(8,128)(2,1)S(1)} collective-permute-done((bf16[272,640]{1,0:T(8,128)(2,1)}, bf16[272,640]{1,0:T(8,128)(2,1)S(1)}, u32[]{:S(2)}, u32[]{:S(2)}) %collective-permute-start.49) | collective-permute-done | bytes 348192 | tf_op jit(solution)/shard_map/ppermute | solution.py:36
  (241 shorter events, 139.3 us)
Async XLA Ops:
  7.2 69.2 %all-gather.3.cloned.1.call-start = ((), (), s32[]{:S(2)}) async-start(), calls=%async_computation.2 | async-start | bytes 8110080 | tf_op jit(solution)/shard_map/all_gather | solution.py:1106
  9.0 139.9 %all-gather.5.cloned.1.call-start = ((), (), s32[]{:S(2)}) async-start(), calls=%async_computation.3 | async-start | bytes 11894784 | tf_op jit(solution)/shard_map/all_gather | solution.py:1109
  10.8 290.8 %reduce-scatter.3.cloned.1.call-start = ((), (), s32[]{:S(2)}) async-start(), calls=%async_computation.4 | async-start | bytes 9191424 | tf_op jit(solution)/shard_map/reduce_scatter | solution.py:1174
  21.6 15.3 %collective-permute-start.7 = (bf16[128,2048]{1,0:T(8,128)(2,1)}, bf16[128,2048]{1,0:T(8,128)(2,1)S(1)}, u32[]{:S(2)}, u32[]{:S(2)}) collective-permute-start(bf16[128,2048]{1,0:T(8,128)(2,1)} %get-tuple-element.177.refs_0_), channel_id=1, source_target_pairs={{0,32},{32,64},{64,96},{96,0},{1,33},{33,65},{65,97},{97,1},{2,34}... | collective-permute-start | bytes 1572872 | tf_op jit(solution)/shard_map/ppermute | solution.py:36
  29.1 18.5 %collective-permute-start.5 = (bf16[256,640]{1,0:T(8,128)(2,1)S(1)}, bf16[256,640]{1,0:T(8,128)(2,1)S(1)}, u32[]{:S(2)}, u32[]{:S(2)}) collective-permute-start(bf16[256,640]{1,0:T(8,128)(2,1)S(1)} %pad_maximum_fusion.1.refs_5_.refs_0_), channel_id=1, source_target_pairs={{0,16},{8,24},{16,0},{24,8},{1,17},{9,25},{17,1},{25,9},{2,18},{10... | collective-permute-start | bytes 983048 | tf_op jit(solution)/shard_map/ppermute | solution.py:36
  32.0 15.6 %collective-permute-start.4 = (bf16[256,640]{1,0:T(8,128)(2,1)S(1)}, bf16[256,640]{1,0:T(8,128)(2,1)S(1)}, u32[]{:S(2)}, u32[]{:S(2)}) collective-permute-start(bf16[256,640]{1,0:T(8,128)(2,1)S(1)} %pad_maximum_fusion.1.refs_5_.refs_0_), channel_id=1, source_target_pairs={{0,24},{8,0},{16,8},{24,16},{1,25},{9,1},{17,9},{25,17},{2,26},{10... | collective-permute-start | bytes 983048 | tf_op jit(solution)/shard_map/ppermute | solution.py:36
  57.1 25.3 %collective-permute-start.18 = (bf16[128,2048]{1,0:T(8,128)(2,1)}, bf16[128,2048]{1,0:T(8,128)(2,1)S(1)}, u32[]{:S(2)}, u32[]{:S(2)}) collective-permute-start(bf16[128,2048]{1,0:T(8,128)(2,1)} %bitcast.24), channel_id=1, source_target_pairs={{0,32},{32,64},{64,96},{96,0},{1,33},{33,65},{65,97},{97,1},{2,34}... | collective-permute-start | bytes 1572872 | tf_op jit(solution)/shard_map/ppermute | solution.py:36
  57.5 27.2 %collective-permute-start.17 = (bf16[128,2048]{1,0:T(8,128)(2,1)}, bf16[128,2048]{1,0:T(8,128)(2,1)}, u32[]{:S(2)}, u32[]{:S(2)}) collective-permute-start(bf16[128,2048]{1,0:T(8,128)(2,1)} %bitcast.25), channel_id=1, source_target_pairs={{0,64},{32,96},{64,0},{96,32},{1,65},{33,97},{65,1},{97,33},{2,66}... | collective-permute-start | bytes 1572872 | tf_op jit(solution)/shard_map/ppermute | solution.py:36
  61.2 23.5 %collective-permute-start.16 = (bf16[128,2048]{1,0:T(8,128)(2,1)}, bf16[128,2048]{1,0:T(8,128)(2,1)}, u32[]{:S(2)}, u32[]{:S(2)}) collective-permute-start(bf16[128,2048]{1,0:T(8,128)(2,1)} %bitcast.26), channel_id=1, source_target_pairs={{0,96},{32,0},{64,32},{96,64},{1,97},{33,1},{65,33},{97,65},{2,98}... | collective-permute-start | bytes 1572872 | tf_op jit(solution)/shard_map/ppermute | solution.py:36
  106.9 41.9 %collective-permute-start.28 = (bf16[512,1024]{1,0:T(8,128)(2,1)}, bf16[512,1024]{1,0:T(8,128)(2,1)}, u32[]{:S(2)}, u32[]{:S(2)}) collective-permute-start(bf16[512,1024]{1,0:T(8,128)(2,1)} %get-tuple-element.223), channel_id=1, source_target_pairs={{0,1},{1,0},{2,3},{3,2},{4,5},{5,4},{6,7},{7,6},{8,9},{9,8},{10,11... | collective-permute-start | bytes 3145736 | tf_op jit(solution)/shard_map/ppermute | solution.py:36
  121.8 27.1 %collective-permute-start.22 = (bf16[64,2048]{1,0:T(8,128)(2,1)}, bf16[64,2048]{1,0:T(8,128)(2,1)S(1)}, u32[]{:S(2)}, u32[]{:S(2)}) collective-permute-start(bf16[64,2048]{1,0:T(8,128)(2,1)} %get-tuple-element.214.refs_1_), channel_id=1, source_target_pairs={{0,96},{32,0},{64,32},{96,64},{1,97},{33,1},{65,33},{97,65},{2,98}... | collective-permute-start | bytes 786440 | tf_op jit(solution)/shard_map/ppermute | solution.py:36
  122.8 26.0 %collective-permute-start.27 = (bf16[64,2048]{1,0:T(8,128)(2,1)}, bf16[64,2048]{1,0:T(8,128)(2,1)}, u32[]{:S(2)}, u32[]{:S(2)}) collective-permute-start(bf16[64,2048]{1,0:T(8,128)(2,1)} %get-tuple-element.215.refs_2_), channel_id=1, source_target_pairs={{0,32},{32,64},{64,96},{96,0},{1,33},{33,65},{65,97},{97,1},{2,34}... | collective-permute-start | bytes 786440 | tf_op jit(solution)/shard_map/ppermute | solution.py:36
  129.2 19.7 %collective-permute-start.26 = (bf16[64,2048]{1,0:T(8,128)(2,1)S(1)}, bf16[64,2048]{1,0:T(8,128)(2,1)}, u32[]{:S(2)}, u32[]{:S(2)}) collective-permute-start(bf16[64,2048]{1,0:T(8,128)(2,1)S(1)} %collective-permute-done.24.refs_4_), channel_id=1, source_target_pairs={{0,96},{32,0},{64,32},{96,64},{1,97},{33,1},{65,33},{97,65},{2,98}... | collective-permute-start | bytes 786440 | tf_op jit(solution)/shard_map/ppermute | solution.py:36
  132.4 16.4 %collective-permute-start.25 = (bf16[64,2048]{1,0:T(8,128)(2,1)S(1)}, bf16[64,2048]{1,0:T(8,128)(2,1)}, u32[]{:S(2)}, u32[]{:S(2)}) collective-permute-start(bf16[64,2048]{1,0:T(8,128)(2,1)S(1)} %collective-permute-done.23.refs_7_), channel_id=1, source_target_pairs={{0,32},{32,64},{64,96},{96,0},{1,33},{33,65},{65,97},{97,1},{2,34}... | collective-permute-start | bytes 786440 | tf_op jit(solution)/shard_map/ppermute | solution.py:36
  168.1 27.7 %collective-permute-start.31 = (bf16[128,2048]{1,0:T(8,128)(2,1)}, bf16[128,2048]{1,0:T(8,128)(2,1)S(1)}, u32[]{:S(2)}, u32[]{:S(2)}) collective-permute-start(bf16[128,2048]{1,0:T(8,128)(2,1)} %get-tuple-element.236), channel_id=1, source_target_pairs={{0,32},{32,64},{64,96},{96,0},{1,33},{33,65},{65,97},{97,1},{2,34}... | collective-permute-start | bytes 1572872 | tf_op jit(solution)/shard_map/ppermute | solution.py:36
  168.1 27.7 %collective-permute-start.32 = (bf16[128,2048]{1,0:T(8,128)(2,1)}, bf16[128,2048]{1,0:T(8,128)(2,1)}, u32[]{:S(2)}, u32[]{:S(2)}) collective-permute-start(bf16[128,2048]{1,0:T(8,128)(2,1)} %get-tuple-element.237), channel_id=1, source_target_pairs={{0,96},{32,0},{64,32},{96,64},{1,97},{33,1},{65,33},{97,65},{2,98}... | collective-permute-start | bytes 1572872 | tf_op jit(solution)/shard_map/ppermute | solution.py:36
  171.7 24.5 %collective-permute-start.33 = (bf16[128,2048]{1,0:T(8,128)(2,1)}, bf16[128,2048]{1,0:T(8,128)(2,1)}, u32[]{:S(2)}, u32[]{:S(2)}) collective-permute-start(bf16[128,2048]{1,0:T(8,128)(2,1)} %get-tuple-element.238), channel_id=1, source_target_pairs={{0,64},{32,96},{64,0},{96,32},{1,65},{33,97},{65,1},{97,33},{2,66}... | collective-permute-start | bytes 1572872 | tf_op jit(solution)/shard_map/ppermute | solution.py:36
  196.5 122.8 %reduce-scatter.5.cloned.1.call-start = ((), (), s32[]{:S(2)}) async-start(), calls=%async_computation.5 | async-start | bytes 2621440 | tf_op jit(solution)/shard_map/reduce_scatter | solution.py:1212
  215.6 15.2 %collective-permute-start.36 = (bf16[128,2048]{1,0:T(8,128)(2,1)S(1)}, bf16[128,2048]{1,0:T(8,128)(2,1)}, u32[]{:S(2)}, u32[]{:S(2)}) collective-permute-start(bf16[128,2048]{1,0:T(8,128)(2,1)S(1)} %copy-done.11), channel_id=1, source_target_pairs={{0,64},{32,96},{64,0},{96,32},{1,65},{33,97},{65,1},{97,33},{2,66}... | collective-permute-start | bytes 1572872 | tf_op jit(solution)/shard_map/ppermute | solution.py:36
  230.8 25.3 %collective-permute-start.39 = (bf16[128,2048]{1,0:T(8,128)(2,1)}, bf16[128,2048]{1,0:T(8,128)(2,1)S(1)}, u32[]{:S(2)}, u32[]{:S(2)}) collective-permute-start(bf16[128,2048]{1,0:T(8,128)(2,1)} %get-tuple-element.276), channel_id=1, source_target_pairs={{0,32},{32,64},{64,96},{96,0},{1,33},{33,65},{65,97},{97,1},{2,34}... | collective-permute-start | bytes 1572872 | tf_op jit(solution)/shard_map/ppermute | solution.py:36
  233.4 22.8 %collective-permute-start.40 = (bf16[128,2048]{1,0:T(8,128)(2,1)}, bf16[128,2048]{1,0:T(8,128)(2,1)}, u32[]{:S(2)}, u32[]{:S(2)}) collective-permute-start(bf16[128,2048]{1,0:T(8,128)(2,1)} %get-tuple-element.277), channel_id=1, source_target_pairs={{0,96},{32,0},{64,32},{96,64},{1,97},{33,1},{65,33},{97,65},{2,98}... | collective-permute-start | bytes 1572872 | tf_op jit(solution)/shard_map/ppermute | solution.py:36
  234.1 22.0 %collective-permute-start.41 = (bf16[128,2048]{1,0:T(8,128)(2,1)}, bf16[128,2048]{1,0:T(8,128)(2,1)}, u32[]{:S(2)}, u32[]{:S(2)}) collective-permute-start(bf16[128,2048]{1,0:T(8,128)(2,1)} %get-tuple-element.278), channel_id=1, source_target_pairs={{0,64},{32,96},{64,0},{96,32},{1,65},{33,97},{65,1},{97,33},{2,66}... | collective-permute-start | bytes 1572872 | tf_op jit(solution)/shard_map/ppermute | solution.py:36
  286.7 17.0 %collective-permute-start.52 = (bf16[256,512]{1,0:T(8,128)(2,1)}, bf16[256,512]{1,0:T(8,128)(2,1)S(1)}, u32[]{:S(2)}, u32[]{:S(2)}) collective-permute-start(bf16[256,512]{1,0:T(8,128)(2,1)} %get-tuple-element.302), channel_id=1, source_target_pairs={{0,16},{8,24},{16,0},{24,8},{1,17},{9,25},{17,1},{25,9},{2,18},{10... | collective-permute-start | bytes 786440 | tf_op jit(solution)/shard_map/ppermute | solution.py:36
  292.2 15.8 %collective-permute-start.49 = (bf16[272,640]{1,0:T(8,128)(2,1)}, bf16[272,640]{1,0:T(8,128)(2,1)S(1)}, u32[]{:S(2)}, u32[]{:S(2)}) collective-permute-start(bf16[272,640]{1,0:T(8,128)(2,1)} %get-tuple-element.298), channel_id=1, source_target_pairs={{0,4},{2,6},{4,0},{6,2},{1,5},{3,7},{5,1},{7,3},{8,12},{10,14},{12... | collective-permute-start | bytes 1044488 | tf_op jit(solution)/shard_map/ppermute | solution.py:36
  (84 other events, 633.9 us)
Sparse Core Ops, SparseCore 0:
  10.3 66.1 all-gather.2
  79.3 60.1 all-gather.4
  196.3 86.3 reduce-scatter.2
  285.1 29.2 reduce-scatter.4

commit v2 on v1

--- a/solution.py
+++ b/solution.py
@@ -304,32 +304,35 @@
     return result[:4], result[4:]
 
 
-def second_pieces_kernel(at_ref, *refs):
-    qkv, out, (held, out_held) = refs[:4], refs[4:8], refs[16:]
-    held[...] = total_of(qkv)
-    out_held[...] = total_of(out).astype(BF16)
-    for number in range(4):
-        y = pl.multiple_of(lax.rem(y_of(at_ref) + number, 4) * 64, 64)
-        put_piece(refs[8 + number], held[pl.ds(y, 64), :].astype(BF16), held[256:, :GAIN_COLUMNS])
-        x = pl.multiple_of(lax.rem(x_of(at_ref) + number, 4) * 64, 64)
-        refs[12 + number][...] = out_held[pl.ds(x, 64), :]
-
-
-def second_pieces(at, qkv, out):
+def second_qkv_kernel(at_ref, a_ref, b_ref, c_ref, d_ref, *refs):
+    held = refs[4]
+    held[...] = total_of((a_ref, b_ref, c_ref, d_ref))
+    for number, ref in enumerate(refs[:4]):
+        row = pl.multiple_of(lax.rem(y_of(at_ref) + number, 4) * 64, 64)
+        put_piece(ref, held[pl.ds(row, 64), :].astype(BF16), held[256:, :GAIN_COLUMNS])
+
+
+def second_out_kernel(at_ref, a_ref, b_ref, c_ref, d_ref, *refs):
+    held = refs[4]
+    held[...] = total_of((a_ref, b_ref, c_ref, d_ref)).astype(BF16)
+    for number, ref in enumerate(refs[:4]):
+        row = pl.multiple_of(lax.rem(x_of(at_ref) + number, 4) * 64, 64)
+        ref[...] = held[pl.ds(row, 64), :]
+
+
+def second_pieces(kernel, shape, held_type, at, pieces):
     vmem = pl.BlockSpec(memory_space=pltpu.VMEM)
-    shapes = [(64 + GAIN_ROWS, 640)] * 4 + [(64, 512)] * 4
-    result = pl.pallas_call(
-        second_pieces_kernel,
-        out_shape=tuple(jax.ShapeDtypeStruct(shape, BF16) for shape in shapes),
-        in_specs=[pl.BlockSpec(memory_space=pltpu.SMEM)] + [vmem] * 8,
-        out_specs=(vmem,) * 8,
-        scratch_shapes=[pltpu.VMEM((256 + GAIN_ROWS, 640), F32), pltpu.VMEM((256, 512), BF16)],
-        compiler_params=pltpu.CompilerParams(vmem_limit_bytes=VMEM_LIMIT),
-        cost_estimate=pl.CostEstimate(
-            flops=4 * 272 * 1152, bytes_accessed=10 * 272 * 1152, transcendentals=0
-        ),
-    )(at, *qkv, *out)
-    return result[:4], result[4:]
+    return pl.pallas_call(
+        kernel,
+        out_shape=(jax.ShapeDtypeStruct(shape, BF16),) * 4,
+        in_specs=[pl.BlockSpec(memory_space=pltpu.SMEM)] + [vmem] * 4,
+        out_specs=(vmem,) * 4,
+        scratch_shapes=[pltpu.VMEM(pieces[0].shape, held_type)],
+        compiler_params=pltpu.CompilerParams(vmem_limit_bytes=VMEM_LIMIT),
+        cost_estimate=pl.CostEstimate(
+            flops=4 * pieces[0].size, bytes_accessed=10 * pieces[0].size, transcendentals=0
+        ),
+    )(at, *pieces)
 
 
 def attention_grads_kernel(*refs):
@@ -811,10 +814,14 @@
     for number in range(4):
         columns = slice(512 * number, 512 * number + 512)
         dx[:, columns] = dot_nt(dgu, w_held[columns, : 2 * HIDDEN]).astype(BF16)
-    for number, (start, size) in enumerate(PIECES):
-        copy = pltpu.make_async_copy(dx.at[pl.ds(start, size)], dx_refs[number], out_sems.at[number])
-        copy.start()
-        results.append(copy)
+        for piece, (start, size) in enumerate(PIECES):
+            copy = pltpu.make_async_copy(
+                dx.at[pl.ds(start, size), pl.ds(512 * number, 512)],
+                dx_refs[piece].at[:, pl.ds(512 * number, 512)],
+                out_sems.at[7 + 4 * number + piece],
+            )
+            copy.start()
+            results.append(copy)
     for copy in results:
         copy.wait()
 
@@ -839,7 +846,7 @@
             pltpu.VMEM((rows, 3 * HIDDEN), BF16),
             pltpu.VMEM((rows, width), BF16),
             pltpu.SemaphoreType.DMA((20,)),
-            pltpu.SemaphoreType.DMA((7,)),
+            pltpu.SemaphoreType.DMA((23,)),
         ],
         compiler_params=pltpu.CompilerParams(vmem_limit_bytes=VMEM_LIMIT),
         cost_estimate=pl.CostEstimate(
@@ -851,8 +858,19 @@
     return result[0], result[1], result[2], result[3:]
 
 
-def weight_grads_kernel(core_ref, x_ref, x2_ref, dy_ref, dy2_ref, right_ref, right2_ref, out_ref):
+def weight_grads_kernel(core_ref, x_ref, x2_ref, dy_ref, dy2_ref, right_ref, right2_ref, out_ref, dy, dy2, sems):
     part = pl.program_id(0)
+    half = dy.shape[1]
+    start = pl.multiple_of(core_of(core_ref) * half, half)
+    loads = (
+        pltpu.make_async_copy(dy_ref.at[:, pl.ds(start, half)], dy, sems.at[0]),
+        pltpu.make_async_copy(dy2_ref, dy2, sems.at[1]),
+    )
+
+    @pl.when(part == 0)
+    def _():
+        for load in loads:
+            load.start()
 
     @pl.when(part < 2)
     def _():
@@ -861,30 +879,33 @@
 
     @pl.when(part == 2)
     def _():
-        total = dot_tn(dy_ref[...], right_ref[...]) + dot_tn(dy2_ref[...], right2_ref[...])
+        for load in loads:
+            load.wait()
+        total = dot_tn(dy[...], right_ref[...]) + dot_tn(dy2[...], right2_ref[...])
         out_ref[...] = total.astype(BF16)
 
 
 def weight_grads(core, x, x2, dy, dy2, right, right2):
-    rows = x.shape[0]
-    tile = 1024
-    half = x2.shape[1]
-    tiles = half // tile
-    own = lambda j, i, c: (0, core_of(c) * tiles + i)
-    other = lambda j, i, c: (0, i)
-    side = lambda j, i, c: (0, j)
+    rows, half = x2.shape
+    anywhere = pl.BlockSpec(memory_space=pl.ANY)
+    side = lambda j, c: (0, j)
     grid = pltpu.PrefetchScalarGridSpec(
         num_scalar_prefetch=1,
-        grid=(3, tiles),
+        grid=(3,),
         in_specs=[
-            pl.BlockSpec((rows, tile), own),
-            pl.BlockSpec((rows, tile), other),
-            pl.BlockSpec((rows, tile), own),
-            pl.BlockSpec((rows, tile), other),
+            pl.BlockSpec((rows, half), lambda j, c: (0, core_of(c))),
+            pl.BlockSpec((rows, half), lambda j, c: (0, 0)),
+            anywhere,
+            anywhere,
             pl.BlockSpec((rows, HIDDEN), side),
             pl.BlockSpec((rows, HIDDEN), side),
         ],
-        out_specs=pl.BlockSpec((tile, HIDDEN), lambda j, i, c: (i, j)),
+        out_specs=pl.BlockSpec((half, HIDDEN), side),
+        scratch_shapes=[
+            pltpu.VMEM((rows, half), BF16),
+            pltpu.VMEM((rows, half), BF16),
+            pltpu.SemaphoreType.DMA((2,)),
+        ],
     )
     return pl.pallas_call(
         weight_grads_kernel,
@@ -1223,8 +1244,10 @@
         grads[:, HIDDEN : 2 * HIDDEN].astype(F32),
         grads[:, 2 * HIDDEN :].T.astype(F32),
     )
-    pieces, out_sums, grads = keep((exchange(pieces, "x"), exchange(out_sums, "y"), grads))
-    pieces, out_sums = second_pieces(code, pieces, out_sums)
+    pieces, grads = keep((exchange(pieces, "x"), grads))
+    pieces = second_pieces(second_qkv_kernel, (64 + GAIN_ROWS, 640), F32, code, pieces)
+    out_sums, pieces = keep((exchange(out_sums, "y"), pieces))
+    out_sums = second_pieces(second_out_kernel, (64, 512), BF16, code, out_sums)
     (grad_inputs,) = small_call(input_grad_kernel, rows, dh1, x_rows, gains, dnormed_one)
     pieces, out_sums, grad_inputs = keep((exchange(pieces, "y"), exchange(out_sums, "x"), grad_inputs))
     columns = (64, 512), (64, 512), (64, 64), (64, 64), (1, 2048), (1, 2048)

time: 337 us -> 341 us (1.012)
    unnamed x90 -> x86, local copies, waits for them, and re-layouts: 7.1 us -> 6.89 us
  transfers between devices with their start and end apart: 64 -> 64, of which waited for: 22 -> 21; matrix products, arithmetic and copies ran while one was open for 3% -> 3% of each run, Pallas kernels for 42% -> 42%
where the time goes in v2:
time: 341 us; the launch traced here: 336 us
  Pallas kernels  162 us (48%)
  starting transfers between devices  98.8 us (29%)
  waiting for transfers between devices  43 us (13%)
  between operations  14.7 us (4%)
  other arithmetic  9.72 us (3%)
  local copies, waits for them, and re-layouts  8.48 us (2%)
    ppermute x56, starting transfers between devices, shift(): lax.ppermute(value, axis, [(i, (i + distance) % size) for i in range(size)])  91.9 us
    ppermute x56, waiting for transfers between devices, shift(): lax.ppermute(value, axis, [(i, (i + distance) % size) for i in range(size)])  40.9 us
    pallas_call x3, Pallas kernels, attend_back(): pl.pallas_call(functools.partial(attend_back_kernel, first, step, count),...  30.7 us
    pallas_call x3, Pallas kernels, attend(): pl.pallas_call(functools.partial(attend_kernel, first, step), grid_spec=g...  22.3 us
    pallas_call x1, Pallas kernels, ffn(): pl.pallas_call(ffn_kernel, out_shape=(jax.ShapeDtypeStruct((rows, 3 * HID...  17.6 us
    pallas_call x5, Pallas kernels, small_call(): pl.pallas_call(kernel, out_shape=tuple((jax.ShapeDtypeStruct(shape, dtype...  15.8 us
    pallas_call x1, Pallas kernels, weight_grads(): pl.pallas_call(weight_grads_kernel, grid_spec=grid, out_shape=jax.ShapeDt...  14.6 us
    pallas_call x1, Pallas kernels, finish(): pl.pallas_call(finish_kernel, grid_spec=grid, out_shape=(jax.ShapeDtypeSt...  7.76 us
  transfers between devices with their start and end apart: 64, of which 21 were waited for; matrix products, arithmetic and copies ran while one was open for 3% of the time, Pallas kernels for 42%

profile of v2, /device:TPU:0, one launch (start us, length us, event | category | flops | bytes accessed | tf_op | source)
XLA Modules:
  0.0 336.4 jit_solution(12398061629581044911)
XLA Ops:
  42.2 5.4 %collective-permute-done.5.refs_7_.refs_2_ = bf16[256,640]{1,0:T(8,128)(2,1)S(1)} collective-permute-done((bf16[256,640]{1,0:T(8,128)(2,1)S(1)}, bf16[256,640]{1,0:T(8,128)(2,1)S(1)}, u32[]{:S(2)}, u32[]{:S(2)}) %collective-permute-start.5) | collective-permute-done | bytes 327712 | tf_op jit(solution)/shard_map/ppermute | solution.py:36
  51.7 5.3 %shard_map.204 = (bf16[512,128]{1,0:T(8,128)(2,1)}, bf16[512,2048]{1,0:T(8,128)(2,1)}) custom-call(s32[1]{0:T(128)} %bitcast.at_ref.place_ref.core_ref.refs_0_, bf16[128,2048]{1,0:T(8,128)(2,1)} %get-tuple-element.181.refs_0_, bf16[128,2048]{1,0:T(8,128)(2,1)} %copy-done.9, bf16[64,2048]{1,0:T(8,128)(2,1)} %copy-done.20, bf16[64,2048]{1,0:T(8,128)(2,1)} %copy-done.21, ...), custom_call_target="tpu_custom_call" | custom-call | flops 268435456 | bytes 5242880 | tf_op jit(solution)/shard_map/pallas_call | solution.py:392
  57.5 3.7 %collective-permute-start.17 = (bf16[128,2048]{1,0:T(8,128)(2,1)}, bf16[128,2048]{1,0:T(8,128)(2,1)}, u32[]{:S(2)}, u32[]{:S(2)}) collective-permute-start(bf16[128,2048]{1,0:T(8,128)(2,1)} %bitcast.25), channel_id=1, source_target_pairs={{0,64},{32,96},{64,0},{96,32},{1,65},{33,97},{65,1},{97,33},{2,66}... | collective-permute-start | bytes 1572872 | tf_op jit(solution)/shard_map/ppermute | solution.py:36
  66.3 6.4 %shard_map.205 = (bf16[512,512]{1,0:T(8,128)(2,1)}, bf16[2048,640]{1,0:T(8,128)(2,1)}) custom-call(s32[1]{0:T(128)} %bitcast.at_ref.place_ref.core_ref.refs_0_, bf16[512,2048]{1,0:T(8,128)(2,1)} %get-tuple-element.193.x_ref, bf16[256,640]{1,0:T(8,128)(2,1)} %copy-done, bf16[256,640]{1,0:T(8,128)(2,1)} %copy-done.3, bf16[256,640]{1,0:T(8,128)(2,1)} %copy-done.2, ...), custom_call_target="tpu_custom_call" | custom-call | flops 1073741824 | bytes 7340032 | tf_op jit(solution)/shard_map/pallas_call | solution.py:428
  76.5 6.0 %shard_map.207 = (bf16[128,512]{1,0:T(8,128)(2,1)}, f32[1,4,1,256]{3,2,1,0:T(1,128)}, bf16[128,2048]{1,0:T(8,128)(2,1)}) custom-call(s32[1]{0:T(128)} %bitcast.at_ref.place_ref.core_ref.refs_0_, bf16[512,512]{1,0:T(8,128)(2,1)} %get-tuple-element.206.q_ref.refs_1_, bf16[1536,128]{1,0:T(8,128)(2,1)} %get-tuple-element.197.kk_ref.refs_4_, ...), custom_call_target="tpu_custom_call" | custom-call | flops 603979776 | bytes 3145728 | tf_op jit(solution)/shard_map/pallas_call | solution.py:567
  86.8 10.3 %shard_map.208 = (bf16[256,512]{1,0:T(8,128)(2,1)}, f32[2,4,1,256]{3,2,1,0:T(1,128)}, bf16[128,2048]{1,0:T(8,128)(2,1)}, bf16[128,2048]{1,0:T(8,128)(2,1)}) custom-call(s32[1]{0:T(128)} %bitcast.at_ref.place_ref.core_ref.refs_0_, bf16[512,512]{1,0:T(8,128)(2,1)} %get-tuple-element.206.q_ref.refs_1_, bf16[1536,128]{1,0:T(8,128)(2,1)} %get-tuple-element.197.kk_ref.refs_4_, ...), custom_call_target="tpu_custom_call" | custom-call | flops 1207959552 | bytes 3145728 | tf_op jit(solution)/shard_map/pallas_call | solution.py:567
  102.9 4.0 %shard_map.211 = (bf16[512,2048]{1,0:T(8,128)(2,1)}, bf16[512,1024]{1,0:T(8,128)(2,1)}) custom-call(s32[1]{0:T(128)} %bitcast.at_ref.place_ref.core_ref.refs_0_, bf16[128,2048]{1,0:T(8,128)(2,1)} %get-tuple-element.217.own_ref.dy_ref, bf16[128,2048]{1,0:T(8,128)(2,1)} %collective-permute-done.16.ahead_ref, ...), custom_call_target="tpu_custom_call" | custom-call | flops 4194304 | bytes 5242880 | tf_op jit(solution)/shard_map/pallas_call | solution.py:172
  106.9 6.0 %shard_map.209 = (bf16[128,512]{1,0:T(8,128)(2,1)}, f32[1,4,1,256]{3,2,1,0:T(1,128)}, bf16[128,2048]{1,0:T(8,128)(2,1)}) custom-call(s32[1]{0:T(128)} %bitcast.at_ref.place_ref.core_ref.refs_0_, bf16[512,512]{1,0:T(8,128)(2,1)} %get-tuple-element.206.q_ref.refs_1_, bf16[1536,128]{1,0:T(8,128)(2,1)} %get-tuple-element.197.kk_ref.refs_4_, ...), custom_call_target="tpu_custom_call" | custom-call | flops 603979776 | bytes 3145728 | tf_op jit(solution)/shard_map/pallas_call | solution.py:567
  123.8 5.4 %collective-permute-done.23.refs_7_ = bf16[64,2048]{1,0:T(8,128)(2,1)S(1)} collective-permute-done((bf16[64,2048]{1,0:T(8,128)(2,1)}, bf16[64,2048]{1,0:T(8,128)(2,1)S(1)}, u32[]{:S(2)}, u32[]{:S(2)}) %collective-permute-start.23) | collective-permute-done | bytes 262176 | tf_op jit(solution)/shard_map/ppermute | solution.py:36
  132.4 8.6 %collective-permute-start.25 = (bf16[64,2048]{1,0:T(8,128)(2,1)S(1)}, bf16[64,2048]{1,0:T(8,128)(2,1)}, u32[]{:S(2)}, u32[]{:S(2)}) collective-permute-start(bf16[64,2048]{1,0:T(8,128)(2,1)S(1)} %collective-permute-done.23.refs_7_), channel_id=1, source_target_pairs={{0,32},{32,64},{64,96},{96,0},{1,33},{33,65},{65,97},{97,1},{2,34}... | collective-permute-start | bytes 786440 | tf_op jit(solution)/shard_map/ppermute | solution.py:36
  141.0 7.8 %shard_map.212.refs_9_ = f32[512,1408]{1,0:T(8,128)} custom-call(bf16[512,2048]{1,0:T(8,128)(2,1)} %get-tuple-element.226.left_ref.dy_ref, bf16[2048,1920]{1,0:T(8,128)(2,1)} %all-gather.3.cloned.1.call-done.w_ref.right_ref.refs_2_), custom_call_target="tpu_custom_call" | custom-call | flops 2952790016 | bytes 11534336 | tf_op jit(solution)/shard_map/pallas_call | solution.py:740
  149.5 17.6 %shard_map.213 = (bf16[512,4224]{1,0:T(8,128)(2,1)}, bf16[512,2048]{1,0:T(8,128)(2,1)}, bf16[512,1024]{1,0:T(8,128)(2,1)}, bf16[128,2048]{1,0:T(8,128)(2,1)}, bf...) custom-call(s32[1]{0:T(128)} %bitcast.at_ref.place_ref.core_ref.refs_0_, ...), custom_call_target="tpu_custom_call" | custom-call | flops 11811160064 | bytes 26214400 | tf_op jit(solution)/shard_map/pallas_call | solution.py:832
  167.7 3.6 %collective-permute-start.32 = (bf16[128,2048]{1,0:T(8,128)(2,1)}, bf16[128,2048]{1,0:T(8,128)(2,1)}, u32[]{:S(2)}, u32[]{:S(2)}) collective-permute-start(bf16[128,2048]{1,0:T(8,128)(2,1)} %get-tuple-element.241), channel_id=1, source_target_pairs={{0,96},{32,0},{64,32},{96,64},{1,97},{33,1},{65,33},{97,65},{2,98}... | collective-permute-start | bytes 1572872 | tf_op jit(solution)/shard_map/ppermute | solution.py:36
  172.8 7.2 %shard_map.214 = (bf16[128,2048]{1,0:T(8,128)(2,1)}, bf16[128,2048]{1,0:T(8,128)(2,1)}, bf16[128,2048]{1,0:T(8,128)(2,1)}, bf16[128,2048]{1,0:T(8,128)(2,1)}) custom-call(bf16[512,4224]{1,0:T(8,128)(2,1)} %get-tuple-element.230.left_ref.right_ref, bf16[2048,1920]{1,0:T(8,128)(2,1)} %all-gather.3.cloned.1.call-done.w_ref.right_ref.refs_2_), custom_call_target="tpu_custom_call" | custom-call | flops 2952790016 | bytes 9306112 | tf_op jit(solution)/shard_map/pallas_call | solution.py:931
  180.1 14.6 %shard_map.215 = bf16[1024,4224]{1,0:T(8,128)(2,1)} custom-call(s32[1]{0:T(128)} %bitcast.at_ref.place_ref.core_ref.refs_0_, bf16[512,2048]{1,0:T(8,128)(2,1)} %get-tuple-element.229.x_ref, bf16[512,1024]{1,0:T(8,128)(2,1)} %collective-permute-done.30.x2_ref, bf16[512,2048]{1,0:T(8,128)(2,1)} %get-tuple-element.226.left_ref.dy_ref, ...), custom_call_target="tpu_custom_call" | custom-call | flops 8858370048 | bytes 25165824 | tf_op jit(solution)/shard_map/pallas_call | solution.py:910
  195.9 4.2 %shard_map.216 = (f32[128,2048]{1,0:T(8,128)}, bf16[128,2048]{1,0:T(8,128)(2,1)}, f32[8,2048]{1,0:T(8,128)}) custom-call(f32[128,2048]{1,0:T(8,128)} %get-tuple-element.216.h_ref, bf16[128,2048]{1,0:T(8,128)(2,1)} %get-tuple-element.217.own_ref.dy_ref, f32[2,2048]{1,0:T(2,128)} %get-tuple-element.211.gain_ref.norm_ref, ...), custom_call_target="tpu_custom_call" | custom-call | flops 1576960 | bytes 7372800 | tf_op jit(solution)/shard_map/pallas_call | solution.py:185
  203.4 8.5 %shard_map.217 = (bf16[128,512]{1,0:T(8,128)(2,1)}, f32[1536,128]{1,0:T(8,128)}, f32[1536,128]{1,0:T(8,128)}) custom-call(s32[1]{0:T(128)} %bitcast.at_ref.place_ref.core_ref.refs_0_, bf16[512,512]{1,0:T(8,128)(2,1)} %get-tuple-element.206.q_ref.refs_1_, bf16[2048,1920]{1,0:T(8,128)(2,1)} %all-gather.3.cloned.1.call-done.w_ref.right_ref.refs_2_, ...), custom_call_target="tpu_custom_call" | custom-call | flops 1509949440 | bytes 6291456 | tf_op jit(solution)/shard_map/pallas_call | solution.py:699
  217.1 13.4 %shard_map.218 = (bf16[256,512]{1,0:T(8,128)(2,1)}, f32[1536,128]{1,0:T(8,128)}, f32[1536,128]{1,0:T(8,128)}) custom-call(s32[1]{0:T(128)} %bitcast.at_ref.place_ref.core_ref.refs_0_, bf16[512,512]{1,0:T(8,128)(2,1)} %get-tuple-element.206.q_ref.refs_1_, bf16[2048,1920]{1,0:T(8,128)(2,1)} %all-gather.3.cloned.1.call-done.w_ref.right_ref.refs_2_, ...), custom_call_target="tpu_custom_call" | custom-call | flops 3019898880 | bytes 6291456 | tf_op jit(solution)/shard_map/pallas_call | solution.py:699
  234.5 8.7 %shard_map.219 = (bf16[128,512]{1,0:T(8,128)(2,1)}, bf16[512,128]{1,0:T(8,128)(2,1)}, bf16[512,128]{1,0:T(8,128)(2,1)}, f32[512,128]{1,0:T(8,128)}) custom-call(s32[1]{0:T(128)} %bitcast.at_ref.place_ref.core_ref.refs_0_, bf16[512,512]{1,0:T(8,128)(2,1)} %get-tuple-element.206.q_ref.refs_1_, ...), custom_call_target="tpu_custom_call" | custom-call | flops 1509949440 | bytes 6291456 | tf_op jit(solution)/shard_map/pallas_call | solution.py:699
  245.8 7.6 %shard_map.220 = (bf16[1024,1024]{1,0:T(8,128)(2,1)}, bf16[1024,1024]{1,0:T(8,128)(2,1)}) custom-call(s32[1]{0:T(128)} %bitcast.at_ref.place_ref.core_ref.refs_0_, bf16[512,2048]{1,0:T(8,128)(2,1)} %get-tuple-element.193.x_ref, bf16[128,2048]{1,0:T(8,128)(2,1)} %get-tuple-element.264.refs_11_.dh0, bf16[128,2048]{1,0:T(8,128)(2,1)} %collective-permute-done.34.refs_11_.dh1, ...), custom_call_target="tpu_custom_call" | custom-call | flops 2147483648 | bytes 10485760 | tf_op jit(solution)/shard_map/pallas_call | solution.py:1006
  256.0 7.8 %shard_map.221 = (bf16[1024,128]{1,0:T(8,128)(2,1)}, bf16[1024,128]{1,0:T(8,128)(2,1)}, bf16[512,2048]{1,0:T(8,128)(2,1)}, f32[16,256]{1,0:T(8,128)}) custom-call(s32[1]{0:T(128)} %bitcast.at_ref.place_ref.core_ref.refs_0_, bf16[512,2048]{1,0:T(8,128)(2,1)} %get-tuple-element.193.x_ref, bf16[2048,640]{1,0:T(8,128)(2,1)} %get-tuple-element.194.w_ref, ...), custom_call_target="tpu_custom_call" | custom-call | flops 1610612736 | bytes 10485760 | tf_op jit(solution)/shard_map/pallas_call | solution.py:1092
  277.9 5.2 %shard_map.223 = (bf16[272,640]{1,0:T(8,128)(2,1)}, bf16[272,640]{1,0:T(8,128)(2,1)}, bf16[272,640]{1,0:T(8,128)(2,1)}, bf16[272,640]{1,0:T(8,128)(2,1)}, bf16[2...) custom-call(s32[1]{0:T(128)} %bitcast.at_ref.place_ref.core_ref.refs_0_, ...), custom_call_target="tpu_custom_call" | custom-call | flops 2359296 | bytes 7077888 | tf_op jit(solution)/shard_map/pallas_call | solution.py:295
  302.9 4.7 %collective-permute-done.53.d_ref = bf16[272,640]{1,0:T(8,128)(2,1)} collective-permute-done((bf16[272,640]{1,0:T(8,128)(2,1)}, bf16[272,640]{1,0:T(8,128)(2,1)}, u32[]{:S(2)}, u32[]{:S(2)}) %collective-permute-start.53) | collective-permute-done | bytes 348192 | tf_op jit(solution)/shard_map/ppermute | solution.py:36
  315.4 4.4 %collective-permute-start.55 = (bf16[80,640]{1,0:T(8,128)(2,1)}, bf16[80,640]{1,0:T(8,128)(2,1)S(1)}, u32[]{:S(2)}, u32[]{:S(2)}) collective-permute-start(bf16[80,640]{1,0:T(8,128)(2,1)} %get-tuple-element.319), channel_id=1, source_target_pairs={{0,16},{8,24},{16,0},{24,8},{1,17},{9,25},{17,1},{25,9},{2,18},{10... | collective-permute-start | bytes 307208 | tf_op jit(solution)/shard_map/ppermute | solution.py:36
  (238 shorter events, 145.4 us)
Async XLA Ops:
  7.2 69.2 %all-gather.3.cloned.1.call-start = ((), (), s32[]{:S(2)}) async-start(), calls=%async_computation.2 | async-start | bytes 8110080 | tf_op jit(solution)/shard_map/all_gather | solution.py:1127
  9.0 139.9 %all-gather.5.cloned.1.call-start = ((), (), s32[]{:S(2)}) async-start(), calls=%async_computation.3 | async-start | bytes 11894784 | tf_op jit(solution)/shard_map/all_gather | solution.py:1130
  10.8 286.9 %reduce-scatter.3.cloned.1.call-start = ((), (), s32[]{:S(2)}) async-start(), calls=%async_computation.4 | async-start | bytes 9191424 | tf_op jit(solution)/shard_map/reduce_scatter | solution.py:1195
  29.1 18.5 %collective-permute-start.5 = (bf16[256,640]{1,0:T(8,128)(2,1)S(1)}, bf16[256,640]{1,0:T(8,128)(2,1)S(1)}, u32[]{:S(2)}, u32[]{:S(2)}) collective-permute-start(bf16[256,640]{1,0:T(8,128)(2,1)S(1)} %pad_maximum_fusion.1.refs_5_.refs_0_), channel_id=1, source_target_pairs={{0,16},{8,24},{16,0},{24,8},{1,17},{9,25},{17,1},{25,9},{2,18},{10... | collective-permute-start | bytes 983048 | tf_op jit(solution)/shard_map/ppermute | solution.py:36
  32.0 15.6 %collective-permute-start.4 = (bf16[256,640]{1,0:T(8,128)(2,1)S(1)}, bf16[256,640]{1,0:T(8,128)(2,1)S(1)}, u32[]{:S(2)}, u32[]{:S(2)}) collective-permute-start(bf16[256,640]{1,0:T(8,128)(2,1)S(1)} %pad_maximum_fusion.1.refs_5_.refs_0_), channel_id=1, source_target_pairs={{0,24},{8,0},{16,8},{24,16},{1,25},{9,1},{17,9},{25,17},{2,26},{10... | collective-permute-start | bytes 983048 | tf_op jit(solution)/shard_map/ppermute | solution.py:36
  57.1 25.4 %collective-permute-start.18 = (bf16[128,2048]{1,0:T(8,128)(2,1)}, bf16[128,2048]{1,0:T(8,128)(2,1)S(1)}, u32[]{:S(2)}, u32[]{:S(2)}) collective-permute-start(bf16[128,2048]{1,0:T(8,128)(2,1)} %bitcast.24), channel_id=1, source_target_pairs={{0,32},{32,64},{64,96},{96,0},{1,33},{33,65},{65,97},{97,1},{2,34}... | collective-permute-start | bytes 1572872 | tf_op jit(solution)/shard_map/ppermute | solution.py:36
  57.5 27.2 %collective-permute-start.17 = (bf16[128,2048]{1,0:T(8,128)(2,1)}, bf16[128,2048]{1,0:T(8,128)(2,1)}, u32[]{:S(2)}, u32[]{:S(2)}) collective-permute-start(bf16[128,2048]{1,0:T(8,128)(2,1)} %bitcast.25), channel_id=1, source_target_pairs={{0,64},{32,96},{64,0},{96,32},{1,65},{33,97},{65,1},{97,33},{2,66}... | collective-permute-start | bytes 1572872 | tf_op jit(solution)/shard_map/ppermute | solution.py:36
  61.2 23.5 %collective-permute-start.16 = (bf16[128,2048]{1,0:T(8,128)(2,1)}, bf16[128,2048]{1,0:T(8,128)(2,1)}, u32[]{:S(2)}, u32[]{:S(2)}) collective-permute-start(bf16[128,2048]{1,0:T(8,128)(2,1)} %bitcast.26), channel_id=1, source_target_pairs={{0,96},{32,0},{64,32},{96,64},{1,97},{33,1},{65,33},{97,65},{2,98}... | collective-permute-start | bytes 1572872 | tf_op jit(solution)/shard_map/ppermute | solution.py:36
  106.9 41.9 %collective-permute-start.28 = (bf16[512,1024]{1,0:T(8,128)(2,1)}, bf16[512,1024]{1,0:T(8,128)(2,1)}, u32[]{:S(2)}, u32[]{:S(2)}) collective-permute-start(bf16[512,1024]{1,0:T(8,128)(2,1)} %get-tuple-element.227), channel_id=1, source_target_pairs={{0,1},{1,0},{2,3},{3,2},{4,5},{5,4},{6,7},{7,6},{8,9},{9,8},{10,11... | collective-permute-start | bytes 3145736 | tf_op jit(solution)/shard_map/ppermute | solution.py:36
  121.7 27.1 %collective-permute-start.22 = (bf16[64,2048]{1,0:T(8,128)(2,1)}, bf16[64,2048]{1,0:T(8,128)(2,1)S(1)}, u32[]{:S(2)}, u32[]{:S(2)}) collective-permute-start(bf16[64,2048]{1,0:T(8,128)(2,1)} %get-tuple-element.218.refs_1_), channel_id=1, source_target_pairs={{0,96},{32,0},{64,32},{96,64},{1,97},{33,1},{65,33},{97,65},{2,98}... | collective-permute-start | bytes 786440 | tf_op jit(solution)/shard_map/ppermute | solution.py:36
  122.8 26.0 %collective-permute-start.27 = (bf16[64,2048]{1,0:T(8,128)(2,1)}, bf16[64,2048]{1,0:T(8,128)(2,1)}, u32[]{:S(2)}, u32[]{:S(2)}) collective-permute-start(bf16[64,2048]{1,0:T(8,128)(2,1)} %get-tuple-element.219.refs_2_), channel_id=1, source_target_pairs={{0,32},{32,64},{64,96},{96,0},{1,33},{33,65},{65,97},{97,1},{2,34}... | collective-permute-start | bytes 786440 | tf_op jit(solution)/shard_map/ppermute | solution.py:36
  129.2 19.7 %collective-permute-start.26 = (bf16[64,2048]{1,0:T(8,128)(2,1)S(1)}, bf16[64,2048]{1,0:T(8,128)(2,1)}, u32[]{:S(2)}, u32[]{:S(2)}) collective-permute-start(bf16[64,2048]{1,0:T(8,128)(2,1)S(1)} %collective-permute-done.24.refs_4_), channel_id=1, source_target_pairs={{0,96},{32,0},{64,32},{96,64},{1,97},{33,1},{65,33},{97,65},{2,98}... | collective-permute-start | bytes 786440 | tf_op jit(solution)/shard_map/ppermute | solution.py:36
  132.4 16.4 %collective-permute-start.25 = (bf16[64,2048]{1,0:T(8,128)(2,1)S(1)}, bf16[64,2048]{1,0:T(8,128)(2,1)}, u32[]{:S(2)}, u32[]{:S(2)}) collective-permute-start(bf16[64,2048]{1,0:T(8,128)(2,1)S(1)} %collective-permute-done.23.refs_7_), channel_id=1, source_target_pairs={{0,32},{32,64},{64,96},{96,0},{1,33},{33,65},{65,97},{97,1},{2,34}... | collective-permute-start | bytes 786440 | tf_op jit(solution)/shard_map/ppermute | solution.py:36
  167.7 27.0 %collective-permute-start.31 = (bf16[128,2048]{1,0:T(8,128)(2,1)}, bf16[128,2048]{1,0:T(8,128)(2,1)S(1)}, u32[]{:S(2)}, u32[]{:S(2)}) collective-permute-start(bf16[128,2048]{1,0:T(8,128)(2,1)} %get-tuple-element.240), channel_id=1, source_target_pairs={{0,32},{32,64},{64,96},{96,0},{1,33},{33,65},{65,97},{97,1},{2,34}... | collective-permute-start | bytes 1572872 | tf_op jit(solution)/shard_map/ppermute | solution.py:36
  167.7 27.0 %collective-permute-start.32 = (bf16[128,2048]{1,0:T(8,128)(2,1)}, bf16[128,2048]{1,0:T(8,128)(2,1)}, u32[]{:S(2)}, u32[]{:S(2)}) collective-permute-start(bf16[128,2048]{1,0:T(8,128)(2,1)} %get-tuple-element.241), channel_id=1, source_target_pairs={{0,96},{32,0},{64,32},{96,64},{1,97},{33,1},{65,33},{97,65},{2,98}... | collective-permute-start | bytes 1572872 | tf_op jit(solution)/shard_map/ppermute | solution.py:36
  171.3 24.5 %collective-permute-start.33 = (bf16[128,2048]{1,0:T(8,128)(2,1)}, bf16[128,2048]{1,0:T(8,128)(2,1)}, u32[]{:S(2)}, u32[]{:S(2)}) collective-permute-start(bf16[128,2048]{1,0:T(8,128)(2,1)} %get-tuple-element.242), channel_id=1, source_target_pairs={{0,64},{32,96},{64,0},{96,32},{1,65},{33,97},{65,1},{97,33},{2,66}... | collective-permute-start | bytes 1572872 | tf_op jit(solution)/shard_map/ppermute | solution.py:36
  195.8 127.3 %reduce-scatter.5.cloned.1.call-start = ((), (), s32[]{:S(2)}) async-start(), calls=%async_computation.5 | async-start | bytes 2621440 | tf_op jit(solution)/shard_map/reduce_scatter | solution.py:1233
  214.7 15.8 %collective-permute-start.36 = (bf16[128,2048]{1,0:T(8,128)(2,1)S(1)}, bf16[128,2048]{1,0:T(8,128)(2,1)}, u32[]{:S(2)}, u32[]{:S(2)}) collective-permute-start(bf16[128,2048]{1,0:T(8,128)(2,1)S(1)} %copy-done.11), channel_id=1, source_target_pairs={{0,64},{32,96},{64,0},{96,32},{1,65},{33,97},{65,1},{97,33},{2,66}... | collective-permute-start | bytes 1572872 | tf_op jit(solution)/shard_map/ppermute | solution.py:36
  230.5 24.9 %collective-permute-start.39 = (bf16[128,2048]{1,0:T(8,128)(2,1)}, bf16[128,2048]{1,0:T(8,128)(2,1)S(1)}, u32[]{:S(2)}, u32[]{:S(2)}) collective-permute-start(bf16[128,2048]{1,0:T(8,128)(2,1)} %get-tuple-element.280), channel_id=1, source_target_pairs={{0,32},{32,64},{64,96},{96,0},{1,33},{33,65},{65,97},{97,1},{2,34}... | collective-permute-start | bytes 1572872 | tf_op jit(solution)/shard_map/ppermute | solution.py:36
  232.4 23.0 %collective-permute-start.40 = (bf16[128,2048]{1,0:T(8,128)(2,1)}, bf16[128,2048]{1,0:T(8,128)(2,1)}, u32[]{:S(2)}, u32[]{:S(2)}) collective-permute-start(bf16[128,2048]{1,0:T(8,128)(2,1)} %get-tuple-element.281), channel_id=1, source_target_pairs={{0,96},{32,0},{64,32},{96,64},{1,97},{33,1},{65,33},{97,65},{2,98}... | collective-permute-start | bytes 1572872 | tf_op jit(solution)/shard_map/ppermute | solution.py:36
  233.8 21.6 %collective-permute-start.41 = (bf16[128,2048]{1,0:T(8,128)(2,1)}, bf16[128,2048]{1,0:T(8,128)(2,1)}, u32[]{:S(2)}, u32[]{:S(2)}) collective-permute-start(bf16[128,2048]{1,0:T(8,128)(2,1)} %get-tuple-element.282), channel_id=1, source_target_pairs={{0,64},{32,96},{64,0},{96,32},{1,65},{33,97},{65,1},{97,33},{2,66}... | collective-permute-start | bytes 1572872 | tf_op jit(solution)/shard_map/ppermute | solution.py:36
  284.4 25.6 %collective-permute-start.48 = (bf16[256,512]{1,0:T(8,128)(2,1)}, bf16[256,512]{1,0:T(8,128)(2,1)S(1)}, u32[]{:S(2)}, u32[]{:S(2)}) collective-permute-start(bf16[256,512]{1,0:T(8,128)(2,1)} %get-tuple-element.301), channel_id=1, source_target_pairs={{0,8},{8,16},{16,24},{24,0},{1,9},{9,17},{17,25},{25,1},{2,10},{10... | collective-permute-start | bytes 786440 | tf_op jit(solution)/shard_map/ppermute | solution.py:36
  287.7 22.2 %collective-permute-start.49 = (bf16[256,512]{1,0:T(8,128)(2,1)}, bf16[256,512]{1,0:T(8,128)(2,1)}, u32[]{:S(2)}, u32[]{:S(2)}) collective-permute-start(bf16[256,512]{1,0:T(8,128)(2,1)} %get-tuple-element.302), channel_id=1, source_target_pairs={{0,16},{8,24},{16,0},{24,8},{1,17},{9,25},{17,1},{25,9},{2,18},{10... | collective-permute-start | bytes 786440 | tf_op jit(solution)/shard_map/ppermute | solution.py:36
  290.5 19.5 %collective-permute-start.50 = (bf16[256,512]{1,0:T(8,128)(2,1)}, bf16[256,512]{1,0:T(8,128)(2,1)}, u32[]{:S(2)}, u32[]{:S(2)}) collective-permute-start(bf16[256,512]{1,0:T(8,128)(2,1)} %get-tuple-element.303), channel_id=1, source_target_pairs={{0,24},{8,0},{16,8},{24,16},{1,25},{9,1},{17,9},{25,17},{2,26},{10... | collective-permute-start | bytes 786440 | tf_op jit(solution)/shard_map/ppermute | solution.py:36
  (82 other events, 626.7 us)
Sparse Core Ops, SparseCore 0:
  10.3 66.1 all-gather.2
  79.3 60.1 all-gather.4
  196.0 86.6 reduce-scatter.2
  285.0 29.2 reduce-scatter.4

commit v3 on v2

--- a/solution.py
+++ b/solution.py
@@ -267,7 +267,6 @@
     rows = jnp.concatenate([query, narrow], 1)
     out_rows = add_low(o_ref[...], o2_ref[...]).reshape(256, 512)
     gains = total_of(gain_refs)
-    gains = gains[:GAIN_ROWS] + gains[GAIN_ROWS:]
     for number in range(4):
 
         @pl.when(pl.program_id(0) == number)
@@ -288,7 +287,7 @@
         in_specs=[pl.BlockSpec((4, 1, 64, 512), pick_x(1))] * 2
         + [pl.BlockSpec((4, 1, 64, 128), pick_x(0))] * 2
         + [pl.BlockSpec((1, 4, 64, 512), pick_y)] * 2
-        + [pl.BlockSpec((2 * GAIN_ROWS, GAIN_COLUMNS), whole)] * 4,
+        + [pl.BlockSpec((GAIN_ROWS, GAIN_COLUMNS), whole)] * 4,
         out_specs=tuple(pl.BlockSpec(shape, whole) for shape in shapes),
     )
     wide, wide2 = shaped(wide), shaped(wide2)
@@ -304,45 +303,47 @@
     return result[:4], result[4:]
 
 
-def second_qkv_kernel(at_ref, a_ref, b_ref, c_ref, d_ref, *refs):
-    held = refs[4]
-    held[...] = total_of((a_ref, b_ref, c_ref, d_ref))
-    for number, ref in enumerate(refs[:4]):
-        row = pl.multiple_of(lax.rem(y_of(at_ref) + number, 4) * 64, 64)
-        put_piece(ref, held[pl.ds(row, 64), :].astype(BF16), held[256:, :GAIN_COLUMNS])
-
-
-def second_out_kernel(at_ref, a_ref, b_ref, c_ref, d_ref, *refs):
-    held = refs[4]
-    held[...] = total_of((a_ref, b_ref, c_ref, d_ref)).astype(BF16)
-    for number, ref in enumerate(refs[:4]):
-        row = pl.multiple_of(lax.rem(x_of(at_ref) + number, 4) * 64, 64)
-        ref[...] = held[pl.ds(row, 64), :]
-
-
-def second_pieces(kernel, shape, held_type, at, pieces):
+def second_pieces_kernel(at_ref, *refs):
+    qkv, out, (held, out_held) = refs[:4], refs[4:8], refs[16:]
+    held[...] = total_of(qkv)
+    out_held[...] = total_of(out).astype(BF16)
+    for number in range(4):
+        y = pl.multiple_of(lax.rem(y_of(at_ref) + number, 4) * 64, 64)
+        put_piece(refs[8 + number], held[pl.ds(y, 64), :].astype(BF16), held[256:, :GAIN_COLUMNS])
+        x = pl.multiple_of(lax.rem(x_of(at_ref) + number, 4) * 64, 64)
+        refs[12 + number][...] = out_held[pl.ds(x, 64), :]
+
+
+def second_pieces(at, qkv, out):
     vmem = pl.BlockSpec(memory_space=pltpu.VMEM)
-    return pl.pallas_call(
-        kernel,
-        out_shape=(jax.ShapeDtypeStruct(shape, BF16),) * 4,
-        in_specs=[pl.BlockSpec(memory_space=pltpu.SMEM)] + [vmem] * 4,
-        out_specs=(vmem,) * 4,
-        scratch_shapes=[pltpu.VMEM(pieces[0].shape, held_type)],
-        compiler_params=pltpu.CompilerParams(vmem_limit_bytes=VMEM_LIMIT),
-        cost_estimate=pl.CostEstimate(
-            flops=4 * pieces[0].size, bytes_accessed=10 * pieces[0].size, transcendentals=0
-        ),
-    )(at, *pieces)
+    shapes = [(64 + GAIN_ROWS, 640)] * 4 + [(64, 512)] * 4
+    result = pl.pallas_call(
+        second_pieces_kernel,
+        out_shape=tuple(jax.ShapeDtypeStruct(shape, BF16) for shape in shapes),
+        in_specs=[pl.BlockSpec(memory_space=pltpu.SMEM)] + [vmem] * 8,
+        out_specs=(vmem,) * 8,
+        scratch_shapes=[pltpu.VMEM((256 + GAIN_ROWS, 640), F32), pltpu.VMEM((256, 512), BF16)],
+        compiler_params=pltpu.CompilerParams(vmem_limit_bytes=VMEM_LIMIT),
+        cost_estimate=pl.CostEstimate(
+            flops=4 * 272 * 1152, bytes_accessed=10 * 272 * 1152, transcendentals=0
+        ),
+    )(at, *qkv, *out)
+    return result[:4], result[4:]
+
+
+def gains_kernel(a_ref, b_ref, c_ref, d_ref, out_ref):
+    values = [ref[64:, :GAIN_COLUMNS].astype(F32) for ref in (a_ref, b_ref, c_ref, d_ref)]
+    out_ref[...] = (values[0] + values[1]) + (values[2] + values[3])
 
 
 def attention_grads_kernel(*refs):
-    out_ref, q_ref, k_ref, v_ref, one_ref, two_ref = refs[8:]
+    out_ref, q_ref, k_ref, v_ref, one_ref, two_ref = refs[10:]
     total = total_of(refs[:4])
     out_ref[...] = total_of(refs[4:8])
     q_ref[...] = total[:64, :512]
     k_ref[...] = total[:64, 512:576]
     v_ref[...] = total[:64, 576:]
-    gains = total[64:, :GAIN_COLUMNS]
+    gains = total_of(refs[8:10])
     one_ref[...] = jnp.concatenate([gains[k : k + 1] for k in range(8)], 1)
     two_ref[...] = jnp.concatenate([gains[k : k + 1] for k in range(8, 16)], 1)
 
@@ -1231,7 +1232,6 @@
         grad_gain_two,
     )
     dnormed_one = lax.psum_scatter(dnormed_one, "head", scatter_dimension=0, tiled=True)
-    gain_grads = jnp.concatenate([gain_grads, shift(gain_grads, "core", 1)], 0)
     gain_grads = exchange([gain_grads] * 4, "head")
     rows = [(x_rows.shape, BF16)]
     (output,) = small_call(output_kernel, rows, h1, *out_pieces)
@@ -1244,18 +1244,19 @@
         grads[:, HIDDEN : 2 * HIDDEN].astype(F32),
         grads[:, 2 * HIDDEN :].T.astype(F32),
     )
-    pieces, grads = keep((exchange(pieces, "x"), grads))
-    pieces = second_pieces(second_qkv_kernel, (64 + GAIN_ROWS, 640), F32, code, pieces)
-    out_sums, pieces = keep((exchange(out_sums, "y"), pieces))
-    out_sums = second_pieces(second_out_kernel, (64, 512), BF16, code, out_sums)
+    pieces, out_sums, grads = keep((exchange(pieces, "x"), exchange(out_sums, "y"), grads))
+    pieces, out_sums = second_pieces(code, pieces, out_sums)
     (grad_inputs,) = small_call(input_grad_kernel, rows, dh1, x_rows, gains, dnormed_one)
     pieces, out_sums, grad_inputs = keep((exchange(pieces, "y"), exchange(out_sums, "x"), grad_inputs))
+    (gain_grads,) = small_call(gains_kernel, [((GAIN_ROWS, GAIN_COLUMNS), F32)], *pieces)
     columns = (64, 512), (64, 512), (64, 64), (64, 64), (1, 2048), (1, 2048)
     grad_out, grad_query, grad_key, grad_value, grad_gain_one, grad_gain_two = small_call(
         attention_grads_kernel,
         [(shape, F32) for shape in columns],
         *pieces,
         *out_sums,
+        gain_grads,
+        shift(gain_grads, "core", 1),
     )
 
     return (

time: 341 us -> 338 us (level)
  waiting for transfers between devices: 43 us -> 37.7 us
    ppermute x56, waiting for transfers between devices: 40.9 us -> 35.5 us  [shift(): lax.ppermute(value, axis, [(i, (i + distance) % size) for i in range(size)])]
    pallas_call x5 -> x6, Pallas kernels: 15.8 us -> 17.3 us  [small_call(): pl.pallas_call(kernel, out_shape=tuple((jax.ShapeDtypeStruct(shape, dtype...]
    unnamed x86 -> x89, local copies, waits for them, and re-layouts: 6.89 us -> 6.24 us
where the time goes in v3:
time: 338 us; the launch traced here: 333 us
  Pallas kernels  162 us (48%)
  starting transfers between devices  101 us (30%)
  waiting for transfers between devices  37.7 us (11%)
  between operations  14.7 us (4%)
  other arithmetic  9.72 us (3%)
  local copies, waits for them, and re-layouts  7.82 us (2%)
    ppermute x56, starting transfers between devices, shift(): lax.ppermute(value, axis, [(i, (i + distance) % size) for i in range(size)])  93.8 us
    ppermute x56, waiting for transfers between devices, shift(): lax.ppermute(value, axis, [(i, (i + distance) % size) for i in range(size)])  35.5 us
    pallas_call x3, Pallas kernels, attend_back(): pl.pallas_call(functools.partial(attend_back_kernel, first, step, count),...  30.7 us
    pallas_call x3, Pallas kernels, attend(): pl.pallas_call(functools.partial(attend_kernel, first, step), grid_spec=g...  22.3 us
    pallas_call x1, Pallas kernels, ffn(): pl.pallas_call(ffn_kernel, out_shape=(jax.ShapeDtypeStruct((rows, 3 * HID...  17.6 us
    pallas_call x6, Pallas kernels, small_call(): pl.pallas_call(kernel, out_shape=tuple((jax.ShapeDtypeStruct(shape, dtype...  17.3 us
    pallas_call x1, Pallas kernels, weight_grads(): pl.pallas_call(weight_grads_kernel, grid_spec=grid, out_shape=jax.ShapeDt...  14.7 us
    pallas_call x1, Pallas kernels, columns_times(): pl.pallas_call(columns_times_kernel, out_shape=jax.ShapeDtypeStruct((rows...  7.79 us
  transfers between devices with their start and end apart: 64, of which 21 were waited for; matrix products, arithmetic and copies ran while one was open for 3% of the time, Pallas kernels for 42%

profile of v3, /device:TPU:0, one launch (start us, length us, event | category | flops | bytes accessed | tf_op | source)
XLA Modules:
  0.0 332.5 jit_solution(13135498382767631450)
XLA Ops:
  33.3 3.6 %collective-permute-done.7.refs_4_ = bf16[128,2048]{1,0:T(8,128)(2,1)S(1)} collective-permute-done((bf16[128,2048]{1,0:T(8,128)(2,1)}, bf16[128,2048]{1,0:T(8,128)(2,1)S(1)}, u32[]{:S(2)}, u32[]{:S(2)}) %collective-permute-start.7) | collective-permute-done | bytes 524320 | tf_op jit(solution)/shard_map/ppermute | solution.py:36
  42.2 5.4 %collective-permute-done.5.refs_7_.refs_2_ = bf16[256,640]{1,0:T(8,128)(2,1)S(1)} collective-permute-done((bf16[256,640]{1,0:T(8,128)(2,1)S(1)}, bf16[256,640]{1,0:T(8,128)(2,1)S(1)}, u32[]{:S(2)}, u32[]{:S(2)}) %collective-permute-start.5) | collective-permute-done | bytes 327712 | tf_op jit(solution)/shard_map/ppermute | solution.py:36
  51.8 5.3 %shard_map.204 = (bf16[512,128]{1,0:T(8,128)(2,1)}, bf16[512,2048]{1,0:T(8,128)(2,1)}) custom-call(s32[1]{0:T(128)} %bitcast.at_ref.place_ref.core_ref.refs_0_, bf16[128,2048]{1,0:T(8,128)(2,1)} %get-tuple-element.177.refs_0_, bf16[128,2048]{1,0:T(8,128)(2,1)} %copy-done.9, bf16[64,2048]{1,0:T(8,128)(2,1)} %copy-done.25, bf16[64,2048]{1,0:T(8,128)(2,1)} %copy-done.26, ...), custom_call_target="tpu_custom_call" | custom-call | flops 268435456 | bytes 5242880 | tf_op jit(solution)/shard_map/pallas_call | solution.py:393
  57.5 3.7 %collective-permute-start.17 = (bf16[128,2048]{1,0:T(8,128)(2,1)}, bf16[128,2048]{1,0:T(8,128)(2,1)}, u32[]{:S(2)}, u32[]{:S(2)}) collective-permute-start(bf16[128,2048]{1,0:T(8,128)(2,1)} %bitcast.25), channel_id=1, source_target_pairs={{0,64},{32,96},{64,0},{96,32},{1,65},{33,97},{65,1},{97,33},{2,66}... | collective-permute-start | bytes 1572872 | tf_op jit(solution)/shard_map/ppermute | solution.py:36
  66.3 6.4 %shard_map.205 = (bf16[512,512]{1,0:T(8,128)(2,1)}, bf16[2048,640]{1,0:T(8,128)(2,1)}) custom-call(s32[1]{0:T(128)} %bitcast.at_ref.place_ref.core_ref.refs_0_, bf16[512,2048]{1,0:T(8,128)(2,1)} %get-tuple-element.189.x_ref, bf16[256,640]{1,0:T(8,128)(2,1)} %copy-done, bf16[256,640]{1,0:T(8,128)(2,1)} %copy-done.3, bf16[256,640]{1,0:T(8,128)(2,1)} %copy-done.2, ...), custom_call_target="tpu_custom_call" | custom-call | flops 1073741824 | bytes 7340032 | tf_op jit(solution)/shard_map/pallas_call | solution.py:429
  76.5 6.0 %shard_map.207 = (bf16[128,512]{1,0:T(8,128)(2,1)}, f32[1,4,1,256]{3,2,1,0:T(1,128)}, bf16[128,2048]{1,0:T(8,128)(2,1)}) custom-call(s32[1]{0:T(128)} %bitcast.at_ref.place_ref.core_ref.refs_0_, bf16[512,512]{1,0:T(8,128)(2,1)} %get-tuple-element.202.q_ref.refs_1_, bf16[1536,128]{1,0:T(8,128)(2,1)} %get-tuple-element.193.kk_ref.refs_4_, ...), custom_call_target="tpu_custom_call" | custom-call | flops 603979776 | bytes 3145728 | tf_op jit(solution)/shard_map/pallas_call | solution.py:568
  86.8 10.3 %shard_map.208 = (bf16[256,512]{1,0:T(8,128)(2,1)}, f32[2,4,1,256]{3,2,1,0:T(1,128)}, bf16[128,2048]{1,0:T(8,128)(2,1)}, bf16[128,2048]{1,0:T(8,128)(2,1)}) custom-call(s32[1]{0:T(128)} %bitcast.at_ref.place_ref.core_ref.refs_0_, bf16[512,512]{1,0:T(8,128)(2,1)} %get-tuple-element.202.q_ref.refs_1_, bf16[1536,128]{1,0:T(8,128)(2,1)} %get-tuple-element.193.kk_ref.refs_4_, ...), custom_call_target="tpu_custom_call" | custom-call | flops 1207959552 | bytes 3145728 | tf_op jit(solution)/shard_map/pallas_call | solution.py:568
  102.9 4.0 %shard_map.211 = (bf16[512,2048]{1,0:T(8,128)(2,1)}, bf16[512,1024]{1,0:T(8,128)(2,1)}) custom-call(s32[1]{0:T(128)} %bitcast.at_ref.place_ref.core_ref.refs_0_, bf16[128,2048]{1,0:T(8,128)(2,1)} %get-tuple-element.213.own_ref.dy_ref, bf16[128,2048]{1,0:T(8,128)(2,1)} %collective-permute-done.16.ahead_ref, ...), custom_call_target="tpu_custom_call" | custom-call | flops 4194304 | bytes 5242880 | tf_op jit(solution)/shard_map/pallas_call | solution.py:172
  106.9 6.0 %shard_map.209 = (bf16[128,512]{1,0:T(8,128)(2,1)}, f32[1,4,1,256]{3,2,1,0:T(1,128)}, bf16[128,2048]{1,0:T(8,128)(2,1)}) custom-call(s32[1]{0:T(128)} %bitcast.at_ref.place_ref.core_ref.refs_0_, bf16[512,512]{1,0:T(8,128)(2,1)} %get-tuple-element.202.q_ref.refs_1_, bf16[1536,128]{1,0:T(8,128)(2,1)} %get-tuple-element.193.kk_ref.refs_4_, ...), custom_call_target="tpu_custom_call" | custom-call | flops 603979776 | bytes 3145728 | tf_op jit(solution)/shard_map/pallas_call | solution.py:568
  123.8 5.4 %collective-permute-done.23.refs_7_ = bf16[64,2048]{1,0:T(8,128)(2,1)S(1)} collective-permute-done((bf16[64,2048]{1,0:T(8,128)(2,1)}, bf16[64,2048]{1,0:T(8,128)(2,1)S(1)}, u32[]{:S(2)}, u32[]{:S(2)}) %collective-permute-start.23) | collective-permute-done | bytes 262176 | tf_op jit(solution)/shard_map/ppermute | solution.py:36
  132.4 8.6 %collective-permute-start.25 = (bf16[64,2048]{1,0:T(8,128)(2,1)S(1)}, bf16[64,2048]{1,0:T(8,128)(2,1)}, u32[]{:S(2)}, u32[]{:S(2)}) collective-permute-start(bf16[64,2048]{1,0:T(8,128)(2,1)S(1)} %collective-permute-done.23.refs_7_), channel_id=1, source_target_pairs={{0,32},{32,64},{64,96},{96,0},{1,33},{33,65},{65,97},{97,1},{2,34}... | collective-permute-start | bytes 786440 | tf_op jit(solution)/shard_map/ppermute | solution.py:36
  141.0 7.8 %shard_map.212.refs_9_ = f32[512,1408]{1,0:T(8,128)} custom-call(bf16[512,2048]{1,0:T(8,128)(2,1)} %get-tuple-element.222.left_ref.dy_ref, bf16[2048,1920]{1,0:T(8,128)(2,1)} %all-gather.3.cloned.1.call-done.w_ref.right_ref.refs_2_), custom_call_target="tpu_custom_call" | custom-call | flops 2952790016 | bytes 11534336 | tf_op jit(solution)/shard_map/pallas_call | solution.py:741
  149.6 17.6 %shard_map.213 = (bf16[512,4224]{1,0:T(8,128)(2,1)}, bf16[512,2048]{1,0:T(8,128)(2,1)}, bf16[512,1024]{1,0:T(8,128)(2,1)}, bf16[128,2048]{1,0:T(8,128)(2,1)}, bf...) custom-call(s32[1]{0:T(128)} %bitcast.at_ref.place_ref.core_ref.refs_0_, ...), custom_call_target="tpu_custom_call" | custom-call | flops 11811160064 | bytes 26214400 | tf_op jit(solution)/shard_map/pallas_call | solution.py:833
  167.8 3.6 %collective-permute-start.32 = (bf16[128,2048]{1,0:T(8,128)(2,1)}, bf16[128,2048]{1,0:T(8,128)(2,1)}, u32[]{:S(2)}, u32[]{:S(2)}) collective-permute-start(bf16[128,2048]{1,0:T(8,128)(2,1)} %get-tuple-element.237), channel_id=1, source_target_pairs={{0,96},{32,0},{64,32},{96,64},{1,97},{33,1},{65,33},{97,65},{2,98}... | collective-permute-start | bytes 1572872 | tf_op jit(solution)/shard_map/ppermute | solution.py:36
  172.9 7.2 %shard_map.214 = (bf16[128,2048]{1,0:T(8,128)(2,1)}, bf16[128,2048]{1,0:T(8,128)(2,1)}, bf16[128,2048]{1,0:T(8,128)(2,1)}, bf16[128,2048]{1,0:T(8,128)(2,1)}) custom-call(bf16[512,4224]{1,0:T(8,128)(2,1)} %get-tuple-element.226.left_ref.right_ref, bf16[2048,1920]{1,0:T(8,128)(2,1)} %all-gather.3.cloned.1.call-done.w_ref.right_ref.refs_2_), custom_call_target="tpu_custom_call" | custom-call | flops 2952790016 | bytes 9306112 | tf_op jit(solution)/shard_map/pallas_call | solution.py:932
  180.1 14.7 %shard_map.215 = bf16[1024,4224]{1,0:T(8,128)(2,1)} custom-call(s32[1]{0:T(128)} %bitcast.at_ref.place_ref.core_ref.refs_0_, bf16[512,2048]{1,0:T(8,128)(2,1)} %get-tuple-element.225.x_ref, bf16[512,1024]{1,0:T(8,128)(2,1)} %collective-permute-done.30.x2_ref, bf16[512,2048]{1,0:T(8,128)(2,1)} %get-tuple-element.222.left_ref.dy_ref, ...), custom_call_target="tpu_custom_call" | custom-call | flops 8858370048 | bytes 25165824 | tf_op jit(solution)/shard_map/pallas_call | solution.py:911
  196.0 4.2 %shard_map.216 = (f32[128,2048]{1,0:T(8,128)}, bf16[128,2048]{1,0:T(8,128)(2,1)}, f32[8,2048]{1,0:T(8,128)}) custom-call(f32[128,2048]{1,0:T(8,128)} %get-tuple-element.212.h_ref, bf16[128,2048]{1,0:T(8,128)(2,1)} %get-tuple-element.213.own_ref.dy_ref, f32[2,2048]{1,0:T(2,128)} %get-tuple-element.207.gain_ref.norm_ref, ...), custom_call_target="tpu_custom_call" | custom-call | flops 1576960 | bytes 7372800 | tf_op jit(solution)/shard_map/pallas_call | solution.py:185
  203.4 8.5 %shard_map.217 = (bf16[128,512]{1,0:T(8,128)(2,1)}, f32[1536,128]{1,0:T(8,128)}, f32[1536,128]{1,0:T(8,128)}) custom-call(s32[1]{0:T(128)} %bitcast.at_ref.place_ref.core_ref.refs_0_, bf16[512,512]{1,0:T(8,128)(2,1)} %get-tuple-element.202.q_ref.refs_1_, bf16[2048,1920]{1,0:T(8,128)(2,1)} %all-gather.3.cloned.1.call-done.w_ref.right_ref.refs_2_, ...), custom_call_target="tpu_custom_call" | custom-call | flops 1509949440 | bytes 6291456 | tf_op jit(solution)/shard_map/pallas_call | solution.py:700
  217.1 13.4 %shard_map.218 = (bf16[256,512]{1,0:T(8,128)(2,1)}, f32[1536,128]{1,0:T(8,128)}, f32[1536,128]{1,0:T(8,128)}) custom-call(s32[1]{0:T(128)} %bitcast.at_ref.place_ref.core_ref.refs_0_, bf16[512,512]{1,0:T(8,128)(2,1)} %get-tuple-element.202.q_ref.refs_1_, bf16[2048,1920]{1,0:T(8,128)(2,1)} %all-gather.3.cloned.1.call-done.w_ref.right_ref.refs_2_, ...), custom_call_target="tpu_custom_call" | custom-call | flops 3019898880 | bytes 6291456 | tf_op jit(solution)/shard_map/pallas_call | solution.py:700
  234.5 8.7 %shard_map.219 = (bf16[128,512]{1,0:T(8,128)(2,1)}, bf16[512,128]{1,0:T(8,128)(2,1)}, bf16[512,128]{1,0:T(8,128)(2,1)}, f32[512,128]{1,0:T(8,128)}) custom-call(s32[1]{0:T(128)} %bitcast.at_ref.place_ref.core_ref.refs_0_, bf16[512,512]{1,0:T(8,128)(2,1)} %get-tuple-element.202.q_ref.refs_1_, ...), custom_call_target="tpu_custom_call" | custom-call | flops 1509949440 | bytes 6291456 | tf_op jit(solution)/shard_map/pallas_call | solution.py:700
  245.8 7.6 %shard_map.220 = (bf16[1024,1024]{1,0:T(8,128)(2,1)}, bf16[1024,1024]{1,0:T(8,128)(2,1)}) custom-call(s32[1]{0:T(128)} %bitcast.at_ref.place_ref.core_ref.refs_0_, bf16[512,2048]{1,0:T(8,128)(2,1)} %get-tuple-element.189.x_ref, bf16[128,2048]{1,0:T(8,128)(2,1)} %get-tuple-element.260.refs_11_.dh0, bf16[128,2048]{1,0:T(8,128)(2,1)} %collective-permute-done.34.refs_11_.dh1, ...), custom_call_target="tpu_custom_call" | custom-call | flops 2147483648 | bytes 10485760 | tf_op jit(solution)/shard_map/pallas_call | solution.py:1007
  256.2 7.8 %shard_map.221 = (bf16[1024,128]{1,0:T(8,128)(2,1)}, bf16[1024,128]{1,0:T(8,128)(2,1)}, bf16[512,2048]{1,0:T(8,128)(2,1)}, f32[16,256]{1,0:T(8,128)}) custom-call(s32[1]{0:T(128)} %bitcast.at_ref.place_ref.core_ref.refs_0_, bf16[512,2048]{1,0:T(8,128)(2,1)} %get-tuple-element.189.x_ref, bf16[2048,640]{1,0:T(8,128)(2,1)} %get-tuple-element.190.w_ref, ...), custom_call_target="tpu_custom_call" | custom-call | flops 1610612736 | bytes 10485760 | tf_op jit(solution)/shard_map/pallas_call | solution.py:1093
  273.8 5.2 %shard_map.223 = (bf16[272,640]{1,0:T(8,128)(2,1)}, bf16[272,640]{1,0:T(8,128)(2,1)}, bf16[272,640]{1,0:T(8,128)(2,1)}, bf16[272,640]{1,0:T(8,128)(2,1)}, bf16[2...) custom-call(s32[1]{0:T(128)} %bitcast.at_ref.place_ref.core_ref.refs_0_, ...), custom_call_target="tpu_custom_call" | custom-call | flops 2359296 | bytes 7077888 | tf_op jit(solution)/shard_map/pallas_call | solution.py:294
  290.2 7.3 %collective-permute-start.49 = (bf16[272,640]{1,0:T(8,128)(2,1)}, bf16[272,640]{1,0:T(8,128)(2,1)}, u32[]{:S(2)}, u32[]{:S(2)}) collective-permute-start(bf16[272,640]{1,0:T(8,128)(2,1)} %get-tuple-element.299), channel_id=1, source_target_pairs={{0,6},{2,0},{4,2},{6,4},{1,7},{3,1},{5,3},{7,5},{8,14},{10,8},{12,... | collective-permute-start | bytes 1044488 | tf_op jit(solution)/shard_map/ppermute | solution.py:36
  (240 shorter events, 139.7 us)
Async XLA Ops:
  7.2 69.2 %all-gather.3.cloned.1.call-start = ((), (), s32[]{:S(2)}) async-start(), calls=%async_computation.2 | async-start | bytes 8110080 | tf_op jit(solution)/shard_map/all_gather | solution.py:1128
  9.0 139.9 %all-gather.5.cloned.1.call-start = ((), (), s32[]{:S(2)}) async-start(), calls=%async_computation.3 | async-start | bytes 11894784 | tf_op jit(solution)/shard_map/all_gather | solution.py:1131
  10.8 286.6 %reduce-scatter.3.cloned.1.call-start = ((), (), s32[]{:S(2)}) async-start(), calls=%async_computation.4 | async-start | bytes 9191424 | tf_op jit(solution)/shard_map/reduce_scatter | solution.py:1196
  21.6 15.3 %collective-permute-start.7 = (bf16[128,2048]{1,0:T(8,128)(2,1)}, bf16[128,2048]{1,0:T(8,128)(2,1)S(1)}, u32[]{:S(2)}, u32[]{:S(2)}) collective-permute-start(bf16[128,2048]{1,0:T(8,128)(2,1)} %get-tuple-element.177.refs_0_), channel_id=1, source_target_pairs={{0,32},{32,64},{64,96},{96,0},{1,33},{33,65},{65,97},{97,1},{2,34}... | collective-permute-start | bytes 1572872 | tf_op jit(solution)/shard_map/ppermute | solution.py:36
  29.1 18.5 %collective-permute-start.5 = (bf16[256,640]{1,0:T(8,128)(2,1)S(1)}, bf16[256,640]{1,0:T(8,128)(2,1)S(1)}, u32[]{:S(2)}, u32[]{:S(2)}) collective-permute-start(bf16[256,640]{1,0:T(8,128)(2,1)S(1)} %pad_maximum_fusion.1.refs_5_.refs_0_), channel_id=1, source_target_pairs={{0,16},{8,24},{16,0},{24,8},{1,17},{9,25},{17,1},{25,9},{2,18},{10... | collective-permute-start | bytes 983048 | tf_op jit(solution)/shard_map/ppermute | solution.py:36
  32.0 15.6 %collective-permute-start.4 = (bf16[256,640]{1,0:T(8,128)(2,1)S(1)}, bf16[256,640]{1,0:T(8,128)(2,1)S(1)}, u32[]{:S(2)}, u32[]{:S(2)}) collective-permute-start(bf16[256,640]{1,0:T(8,128)(2,1)S(1)} %pad_maximum_fusion.1.refs_5_.refs_0_), channel_id=1, source_target_pairs={{0,24},{8,0},{16,8},{24,16},{1,25},{9,1},{17,9},{25,17},{2,26},{10... | collective-permute-start | bytes 983048 | tf_op jit(solution)/shard_map/ppermute | solution.py:36
  57.1 25.3 %collective-permute-start.18 = (bf16[128,2048]{1,0:T(8,128)(2,1)}, bf16[128,2048]{1,0:T(8,128)(2,1)S(1)}, u32[]{:S(2)}, u32[]{:S(2)}) collective-permute-start(bf16[128,2048]{1,0:T(8,128)(2,1)} %bitcast.24), channel_id=1, source_target_pairs={{0,32},{32,64},{64,96},{96,0},{1,33},{33,65},{65,97},{97,1},{2,34}... | collective-permute-start | bytes 1572872 | tf_op jit(solution)/shard_map/ppermute | solution.py:36
  57.5 27.2 %collective-permute-start.17 = (bf16[128,2048]{1,0:T(8,128)(2,1)}, bf16[128,2048]{1,0:T(8,128)(2,1)}, u32[]{:S(2)}, u32[]{:S(2)}) collective-permute-start(bf16[128,2048]{1,0:T(8,128)(2,1)} %bitcast.25), channel_id=1, source_target_pairs={{0,64},{32,96},{64,0},{96,32},{1,65},{33,97},{65,1},{97,33},{2,66}... | collective-permute-start | bytes 1572872 | tf_op jit(solution)/shard_map/ppermute | solution.py:36
  61.2 23.5 %collective-permute-start.16 = (bf16[128,2048]{1,0:T(8,128)(2,1)}, bf16[128,2048]{1,0:T(8,128)(2,1)}, u32[]{:S(2)}, u32[]{:S(2)}) collective-permute-start(bf16[128,2048]{1,0:T(8,128)(2,1)} %bitcast.26), channel_id=1, source_target_pairs={{0,96},{32,0},{64,32},{96,64},{1,97},{33,1},{65,33},{97,65},{2,98}... | collective-permute-start | bytes 1572872 | tf_op jit(solution)/shard_map/ppermute | solution.py:36
  106.9 42.0 %collective-permute-start.28 = (bf16[512,1024]{1,0:T(8,128)(2,1)}, bf16[512,1024]{1,0:T(8,128)(2,1)}, u32[]{:S(2)}, u32[]{:S(2)}) collective-permute-start(bf16[512,1024]{1,0:T(8,128)(2,1)} %get-tuple-element.223), channel_id=1, source_target_pairs={{0,1},{1,0},{2,3},{3,2},{4,5},{5,4},{6,7},{7,6},{8,9},{9,8},{10,11... | collective-permute-start | bytes 3145736 | tf_op jit(solution)/shard_map/ppermute | solution.py:36
  121.8 27.1 %collective-permute-start.22 = (bf16[64,2048]{1,0:T(8,128)(2,1)}, bf16[64,2048]{1,0:T(8,128)(2,1)S(1)}, u32[]{:S(2)}, u32[]{:S(2)}) collective-permute-start(bf16[64,2048]{1,0:T(8,128)(2,1)} %get-tuple-element.214.refs_1_), channel_id=1, source_target_pairs={{0,96},{32,0},{64,32},{96,64},{1,97},{33,1},{65,33},{97,65},{2,98}... | collective-permute-start | bytes 786440 | tf_op jit(solution)/shard_map/ppermute | solution.py:36
  122.8 26.1 %collective-permute-start.27 = (bf16[64,2048]{1,0:T(8,128)(2,1)}, bf16[64,2048]{1,0:T(8,128)(2,1)}, u32[]{:S(2)}, u32[]{:S(2)}) collective-permute-start(bf16[64,2048]{1,0:T(8,128)(2,1)} %get-tuple-element.215.refs_2_), channel_id=1, source_target_pairs={{0,32},{32,64},{64,96},{96,0},{1,33},{33,65},{65,97},{97,1},{2,34}... | collective-permute-start | bytes 786440 | tf_op jit(solution)/shard_map/ppermute | solution.py:36
  129.2 19.7 %collective-permute-start.26 = (bf16[64,2048]{1,0:T(8,128)(2,1)S(1)}, bf16[64,2048]{1,0:T(8,128)(2,1)}, u32[]{:S(2)}, u32[]{:S(2)}) collective-permute-start(bf16[64,2048]{1,0:T(8,128)(2,1)S(1)} %collective-permute-done.24.refs_4_), channel_id=1, source_target_pairs={{0,96},{32,0},{64,32},{96,64},{1,97},{33,1},{65,33},{97,65},{2,98}... | collective-permute-start | bytes 786440 | tf_op jit(solution)/shard_map/ppermute | solution.py:36
  132.4 16.5 %collective-permute-start.25 = (bf16[64,2048]{1,0:T(8,128)(2,1)S(1)}, bf16[64,2048]{1,0:T(8,128)(2,1)}, u32[]{:S(2)}, u32[]{:S(2)}) collective-permute-start(bf16[64,2048]{1,0:T(8,128)(2,1)S(1)} %collective-permute-done.23.refs_7_), channel_id=1, source_target_pairs={{0,32},{32,64},{64,96},{96,0},{1,33},{33,65},{65,97},{97,1},{2,34}... | collective-permute-start | bytes 786440 | tf_op jit(solution)/shard_map/ppermute | solution.py:36
  167.8 27.1 %collective-permute-start.31 = (bf16[128,2048]{1,0:T(8,128)(2,1)}, bf16[128,2048]{1,0:T(8,128)(2,1)S(1)}, u32[]{:S(2)}, u32[]{:S(2)}) collective-permute-start(bf16[128,2048]{1,0:T(8,128)(2,1)} %get-tuple-element.236), channel_id=1, source_target_pairs={{0,32},{32,64},{64,96},{96,0},{1,33},{33,65},{65,97},{97,1},{2,34}... | collective-permute-start | bytes 1572872 | tf_op jit(solution)/shard_map/ppermute | solution.py:36
  167.8 27.1 %collective-permute-start.32 = (bf16[128,2048]{1,0:T(8,128)(2,1)}, bf16[128,2048]{1,0:T(8,128)(2,1)}, u32[]{:S(2)}, u32[]{:S(2)}) collective-permute-start(bf16[128,2048]{1,0:T(8,128)(2,1)} %get-tuple-element.237), channel_id=1, source_target_pairs={{0,96},{32,0},{64,32},{96,64},{1,97},{33,1},{65,33},{97,65},{2,98}... | collective-permute-start | bytes 1572872 | tf_op jit(solution)/shard_map/ppermute | solution.py:36
  171.4 24.5 %collective-permute-start.33 = (bf16[128,2048]{1,0:T(8,128)(2,1)}, bf16[128,2048]{1,0:T(8,128)(2,1)}, u32[]{:S(2)}, u32[]{:S(2)}) collective-permute-start(bf16[128,2048]{1,0:T(8,128)(2,1)} %get-tuple-element.238), channel_id=1, source_target_pairs={{0,64},{32,96},{64,0},{96,32},{1,65},{33,97},{65,1},{97,33},{2,66}... | collective-permute-start | bytes 1572872 | tf_op jit(solution)/shard_map/ppermute | solution.py:36
  195.9 119.1 %reduce-scatter.5.cloned.1.call-start = ((), (), s32[]{:S(2)}) async-start(), calls=%async_computation.5 | async-start | bytes 2621440 | tf_op jit(solution)/shard_map/reduce_scatter | solution.py:1234
  214.8 15.8 %collective-permute-start.36 = (bf16[128,2048]{1,0:T(8,128)(2,1)S(1)}, bf16[128,2048]{1,0:T(8,128)(2,1)}, u32[]{:S(2)}, u32[]{:S(2)}) collective-permute-start(bf16[128,2048]{1,0:T(8,128)(2,1)S(1)} %copy-done.11), channel_id=1, source_target_pairs={{0,64},{32,96},{64,0},{96,32},{1,65},{33,97},{65,1},{97,33},{2,66}... | collective-permute-start | bytes 1572872 | tf_op jit(solution)/shard_map/ppermute | solution.py:36
  230.6 25.0 %collective-permute-start.39 = (bf16[128,2048]{1,0:T(8,128)(2,1)}, bf16[128,2048]{1,0:T(8,128)(2,1)S(1)}, u32[]{:S(2)}, u32[]{:S(2)}) collective-permute-start(bf16[128,2048]{1,0:T(8,128)(2,1)} %get-tuple-element.276), channel_id=1, source_target_pairs={{0,32},{32,64},{64,96},{96,0},{1,33},{33,65},{65,97},{97,1},{2,34}... | collective-permute-start | bytes 1572872 | tf_op jit(solution)/shard_map/ppermute | solution.py:36
  232.4 23.2 %collective-permute-start.40 = (bf16[128,2048]{1,0:T(8,128)(2,1)}, bf16[128,2048]{1,0:T(8,128)(2,1)}, u32[]{:S(2)}, u32[]{:S(2)}) collective-permute-start(bf16[128,2048]{1,0:T(8,128)(2,1)} %get-tuple-element.277), channel_id=1, source_target_pairs={{0,96},{32,0},{64,32},{96,64},{1,97},{33,1},{65,33},{97,65},{2,98}... | collective-permute-start | bytes 1572872 | tf_op jit(solution)/shard_map/ppermute | solution.py:36
  233.9 21.7 %collective-permute-start.41 = (bf16[128,2048]{1,0:T(8,128)(2,1)}, bf16[128,2048]{1,0:T(8,128)(2,1)}, u32[]{:S(2)}, u32[]{:S(2)}) collective-permute-start(bf16[128,2048]{1,0:T(8,128)(2,1)} %get-tuple-element.278), channel_id=1, source_target_pairs={{0,64},{32,96},{64,0},{96,32},{1,65},{33,97},{65,1},{97,33},{2,66}... | collective-permute-start | bytes 1572872 | tf_op jit(solution)/shard_map/ppermute | solution.py:36
  281.6 17.9 %collective-permute-start.51 = (bf16[256,512]{1,0:T(8,128)(2,1)}, bf16[256,512]{1,0:T(8,128)(2,1)S(1)}, u32[]{:S(2)}, u32[]{:S(2)}) collective-permute-start(bf16[256,512]{1,0:T(8,128)(2,1)} %get-tuple-element.302), channel_id=1, source_target_pairs={{0,16},{8,24},{16,0},{24,8},{1,17},{9,25},{17,1},{25,9},{2,18},{10... | collective-permute-start | bytes 786440 | tf_op jit(solution)/shard_map/ppermute | solution.py:36
  287.4 15.7 %collective-permute-start.48 = (bf16[272,640]{1,0:T(8,128)(2,1)}, bf16[272,640]{1,0:T(8,128)(2,1)S(1)}, u32[]{:S(2)}, u32[]{:S(2)}) collective-permute-start(bf16[272,640]{1,0:T(8,128)(2,1)} %get-tuple-element.298), channel_id=1, source_target_pairs={{0,4},{2,6},{4,0},{6,2},{1,5},{3,7},{5,1},{7,3},{8,12},{10,14},{12... | collective-permute-start | bytes 1044488 | tf_op jit(solution)/shard_map/ppermute | solution.py:36
  (84 other events, 628.0 us)
Sparse Core Ops, SparseCore 0:
  10.3 66.1 all-gather.2
  79.3 60.1 all-gather.4
  196.0 86.3 reduce-scatter.2
  284.8 29.3 reduce-scatter.4

commit v4 on v3

--- a/solution.py
+++ b/solution.py
@@ -1246,9 +1246,12 @@
     )
     pieces, out_sums, grads = keep((exchange(pieces, "x"), exchange(out_sums, "y"), grads))
     pieces, out_sums = second_pieces(code, pieces, out_sums)
+    pieces, out_sums = exchange(pieces, "y"), exchange(out_sums, "x")
+    (gain_grads,) = small_call(gains_kernel, [((GAIN_ROWS, GAIN_COLUMNS), F32)], *pieces)
+    gain_grads, dnormed_one, out_sums = keep((gain_grads, dnormed_one, out_sums))
+    gain_grads_other = shift(gain_grads, "core", 1)
     (grad_inputs,) = small_call(input_grad_kernel, rows, dh1, x_rows, gains, dnormed_one)
-    pieces, out_sums, grad_inputs = keep((exchange(pieces, "y"), exchange(out_sums, "x"), grad_inputs))
-    (gain_grads,) = small_call(gains_kernel, [((GAIN_ROWS, GAIN_COLUMNS), F32)], *pieces)
+    gain_grads_other, grad_inputs = keep((gain_grads_other, grad_inputs))
     columns = (64, 512), (64, 512), (64, 64), (64, 64), (1, 2048), (1, 2048)
     grad_out, grad_query, grad_key, grad_value, grad_gain_one, grad_gain_two = small_call(
         attention_grads_kernel,
@@ -1256,7 +1259,7 @@
         *pieces,
         *out_sums,
         gain_grads,
-        shift(gain_grads, "core", 1),
+        gain_grads_other,
     )
 
     return (

time: 338 us -> 338 us (level)
  transfers between devices with their start and end apart: 64 -> 64, of which waited for: 21 -> 18; matrix products, arithmetic and copies ran while one was open for 3% -> 3% of each run, Pallas kernels for 42% -> 43%
where the time goes in v4:
time: 338 us; the launch traced here: 332 us
  Pallas kernels  162 us (48%)
  starting transfers between devices  103 us (30%)
  waiting for transfers between devices  35.4 us (10%)
  between operations  14.7 us (4%)
  other arithmetic  9.77 us (3%)
  local copies, waits for them, and re-layouts  7.68 us (2%)
    ppermute x56, starting transfers between devices, shift(): lax.ppermute(value, axis, [(i, (i + distance) % size) for i in range(size)])  95.9 us
    ppermute x56, waiting for transfers between devices, shift(): lax.ppermute(value, axis, [(i, (i + distance) % size) for i in range(size)])  33.3 us
    pallas_call x3, Pallas kernels, attend_back(): pl.pallas_call(functools.partial(attend_back_kernel, first, step, count),...  30.7 us
    pallas_call x3, Pallas kernels, attend(): pl.pallas_call(functools.partial(attend_kernel, first, step), grid_spec=g...  22.4 us
    pallas_call x1, Pallas kernels, ffn(): pl.pallas_call(ffn_kernel, out_shape=(jax.ShapeDtypeStruct((rows, 3 * HID...  17.6 us
    pallas_call x6, Pallas kernels, small_call(): pl.pallas_call(kernel, out_shape=tuple((jax.ShapeDtypeStruct(shape, dtype...  17.3 us
    pallas_call x1, Pallas kernels, weight_grads(): pl.pallas_call(weight_grads_kernel, grid_spec=grid, out_shape=jax.ShapeDt...  14.7 us
    pallas_call x1, Pallas kernels, finish(): pl.pallas_call(finish_kernel, grid_spec=grid, out_shape=(jax.ShapeDtypeSt...  7.78 us
  transfers between devices with their start and end apart: 64, of which 18 were waited for; matrix products, arithmetic and copies ran while one was open for 3% of the time, Pallas kernels for 43%

profile of v4, /device:TPU:0, one launch (start us, length us, event | category | flops | bytes accessed | tf_op | source)
XLA Modules:
  0.0 332.2 jit_solution(15719669571130946952)
XLA Ops:
  33.3 3.6 %collective-permute-done.7.refs_4_ = bf16[128,2048]{1,0:T(8,128)(2,1)S(1)} collective-permute-done((bf16[128,2048]{1,0:T(8,128)(2,1)}, bf16[128,2048]{1,0:T(8,128)(2,1)S(1)}, u32[]{:S(2)}, u32[]{:S(2)}) %collective-permute-start.7) | collective-permute-done | bytes 524320 | tf_op jit(solution)/shard_map/ppermute | solution.py:36
  42.2 5.4 %collective-permute-done.5.refs_7_.refs_2_ = bf16[256,640]{1,0:T(8,128)(2,1)S(1)} collective-permute-done((bf16[256,640]{1,0:T(8,128)(2,1)S(1)}, bf16[256,640]{1,0:T(8,128)(2,1)S(1)}, u32[]{:S(2)}, u32[]{:S(2)}) %collective-permute-start.5) | collective-permute-done | bytes 327712 | tf_op jit(solution)/shard_map/ppermute | solution.py:36
  51.8 5.3 %shard_map.204 = (bf16[512,128]{1,0:T(8,128)(2,1)}, bf16[512,2048]{1,0:T(8,128)(2,1)}) custom-call(s32[1]{0:T(128)} %bitcast.at_ref.place_ref.core_ref.refs_0_, bf16[128,2048]{1,0:T(8,128)(2,1)} %get-tuple-element.176.refs_0_, bf16[128,2048]{1,0:T(8,128)(2,1)} %copy-done.9, bf16[64,2048]{1,0:T(8,128)(2,1)} %copy-done.25, bf16[64,2048]{1,0:T(8,128)(2,1)} %copy-done.26, ...), custom_call_target="tpu_custom_call" | custom-call | flops 268435456 | bytes 5242880 | tf_op jit(solution)/shard_map/pallas_call | solution.py:393
  66.3 6.4 %shard_map.205 = (bf16[512,512]{1,0:T(8,128)(2,1)}, bf16[2048,640]{1,0:T(8,128)(2,1)}) custom-call(s32[1]{0:T(128)} %bitcast.at_ref.place_ref.core_ref.refs_0_, bf16[512,2048]{1,0:T(8,128)(2,1)} %get-tuple-element.188.x_ref, bf16[256,640]{1,0:T(8,128)(2,1)} %copy-done, bf16[256,640]{1,0:T(8,128)(2,1)} %copy-done.3, bf16[256,640]{1,0:T(8,128)(2,1)} %copy-done.2, ...), custom_call_target="tpu_custom_call" | custom-call | flops 1073741824 | bytes 7340032 | tf_op jit(solution)/shard_map/pallas_call | solution.py:429
  76.5 6.0 %shard_map.207 = (bf16[128,512]{1,0:T(8,128)(2,1)}, f32[1,4,1,256]{3,2,1,0:T(1,128)}, bf16[128,2048]{1,0:T(8,128)(2,1)}) custom-call(s32[1]{0:T(128)} %bitcast.at_ref.place_ref.core_ref.refs_0_, bf16[512,512]{1,0:T(8,128)(2,1)} %get-tuple-element.201.q_ref.refs_1_, bf16[1536,128]{1,0:T(8,128)(2,1)} %get-tuple-element.192.kk_ref.refs_4_, ...), custom_call_target="tpu_custom_call" | custom-call | flops 603979776 | bytes 3145728 | tf_op jit(solution)/shard_map/pallas_call | solution.py:568
  86.9 10.4 %shard_map.208 = (bf16[256,512]{1,0:T(8,128)(2,1)}, f32[2,4,1,256]{3,2,1,0:T(1,128)}, bf16[128,2048]{1,0:T(8,128)(2,1)}, bf16[128,2048]{1,0:T(8,128)(2,1)}) custom-call(s32[1]{0:T(128)} %bitcast.at_ref.place_ref.core_ref.refs_0_, bf16[512,512]{1,0:T(8,128)(2,1)} %get-tuple-element.201.q_ref.refs_1_, bf16[1536,128]{1,0:T(8,128)(2,1)} %get-tuple-element.192.kk_ref.refs_4_, ...), custom_call_target="tpu_custom_call" | custom-call | flops 1207959552 | bytes 3145728 | tf_op jit(solution)/shard_map/pallas_call | solution.py:568
  103.0 3.9 %shard_map.211 = (bf16[512,2048]{1,0:T(8,128)(2,1)}, bf16[512,1024]{1,0:T(8,128)(2,1)}) custom-call(s32[1]{0:T(128)} %bitcast.at_ref.place_ref.core_ref.refs_0_, bf16[128,2048]{1,0:T(8,128)(2,1)} %get-tuple-element.212.own_ref.dy_ref, bf16[128,2048]{1,0:T(8,128)(2,1)} %collective-permute-done.16.ahead_ref, ...), custom_call_target="tpu_custom_call" | custom-call | flops 4194304 | bytes 5242880 | tf_op jit(solution)/shard_map/pallas_call | solution.py:172
  106.9 6.0 %shard_map.209 = (bf16[128,512]{1,0:T(8,128)(2,1)}, f32[1,4,1,256]{3,2,1,0:T(1,128)}, bf16[128,2048]{1,0:T(8,128)(2,1)}) custom-call(s32[1]{0:T(128)} %bitcast.at_ref.place_ref.core_ref.refs_0_, bf16[512,512]{1,0:T(8,128)(2,1)} %get-tuple-element.201.q_ref.refs_1_, bf16[1536,128]{1,0:T(8,128)(2,1)} %get-tuple-element.192.kk_ref.refs_4_, ...), custom_call_target="tpu_custom_call" | custom-call | flops 603979776 | bytes 3145728 | tf_op jit(solution)/shard_map/pallas_call | solution.py:568
  123.8 5.4 %collective-permute-done.23.refs_7_ = bf16[64,2048]{1,0:T(8,128)(2,1)S(1)} collective-permute-done((bf16[64,2048]{1,0:T(8,128)(2,1)}, bf16[64,2048]{1,0:T(8,128)(2,1)S(1)}, u32[]{:S(2)}, u32[]{:S(2)}) %collective-permute-start.23) | collective-permute-done | bytes 262176 | tf_op jit(solution)/shard_map/ppermute | solution.py:36
  132.5 8.6 %collective-permute-start.25 = (bf16[64,2048]{1,0:T(8,128)(2,1)S(1)}, bf16[64,2048]{1,0:T(8,128)(2,1)}, u32[]{:S(2)}, u32[]{:S(2)}) collective-permute-start(bf16[64,2048]{1,0:T(8,128)(2,1)S(1)} %collective-permute-done.23.refs_7_), channel_id=1, source_target_pairs={{0,32},{32,64},{64,96},{96,0},{1,33},{33,65},{65,97},{97,1},{2,34}... | collective-permute-start | bytes 786440 | tf_op jit(solution)/shard_map/ppermute | solution.py:36
  141.1 7.8 %shard_map.212.refs_9_ = f32[512,1408]{1,0:T(8,128)} custom-call(bf16[512,2048]{1,0:T(8,128)(2,1)} %get-tuple-element.221.left_ref.dy_ref, bf16[2048,1920]{1,0:T(8,128)(2,1)} %all-gather.3.cloned.1.call-done.w_ref.right_ref.refs_2_), custom_call_target="tpu_custom_call" | custom-call | flops 2952790016 | bytes 11534336 | tf_op jit(solution)/shard_map/pallas_call | solution.py:741
  149.6 17.6 %shard_map.213 = (bf16[512,4224]{1,0:T(8,128)(2,1)}, bf16[512,2048]{1,0:T(8,128)(2,1)}, bf16[512,1024]{1,0:T(8,128)(2,1)}, bf16[128,2048]{1,0:T(8,128)(2,1)}, bf...) custom-call(s32[1]{0:T(128)} %bitcast.at_ref.place_ref.core_ref.refs_0_, ...), custom_call_target="tpu_custom_call" | custom-call | flops 11811160064 | bytes 26214400 | tf_op jit(solution)/shard_map/pallas_call | solution.py:833
  167.8 3.6 %collective-permute-start.32 = (bf16[128,2048]{1,0:T(8,128)(2,1)}, bf16[128,2048]{1,0:T(8,128)(2,1)}, u32[]{:S(2)}, u32[]{:S(2)}) collective-permute-start(bf16[128,2048]{1,0:T(8,128)(2,1)} %get-tuple-element.236), channel_id=1, source_target_pairs={{0,96},{32,0},{64,32},{96,64},{1,97},{33,1},{65,33},{97,65},{2,98}... | collective-permute-start | bytes 1572872 | tf_op jit(solution)/shard_map/ppermute | solution.py:36
  172.9 7.2 %shard_map.214 = (bf16[128,2048]{1,0:T(8,128)(2,1)}, bf16[128,2048]{1,0:T(8,128)(2,1)}, bf16[128,2048]{1,0:T(8,128)(2,1)}, bf16[128,2048]{1,0:T(8,128)(2,1)}) custom-call(bf16[512,4224]{1,0:T(8,128)(2,1)} %get-tuple-element.225.left_ref.right_ref, bf16[2048,1920]{1,0:T(8,128)(2,1)} %all-gather.3.cloned.1.call-done.w_ref.right_ref.refs_2_), custom_call_target="tpu_custom_call" | custom-call | flops 2952790016 | bytes 9306112 | tf_op jit(solution)/shard_map/pallas_call | solution.py:932
  180.2 14.7 %shard_map.215 = bf16[1024,4224]{1,0:T(8,128)(2,1)} custom-call(s32[1]{0:T(128)} %bitcast.at_ref.place_ref.core_ref.refs_0_, bf16[512,2048]{1,0:T(8,128)(2,1)} %get-tuple-element.224.x_ref, bf16[512,1024]{1,0:T(8,128)(2,1)} %collective-permute-done.30.x2_ref, bf16[512,2048]{1,0:T(8,128)(2,1)} %get-tuple-element.221.left_ref.dy_ref, ...), custom_call_target="tpu_custom_call" | custom-call | flops 8858370048 | bytes 25165824 | tf_op jit(solution)/shard_map/pallas_call | solution.py:911
  196.0 4.2 %shard_map.216 = (f32[128,2048]{1,0:T(8,128)}, bf16[128,2048]{1,0:T(8,128)(2,1)}, f32[8,2048]{1,0:T(8,128)}) custom-call(f32[128,2048]{1,0:T(8,128)} %get-tuple-element.211.h_ref, bf16[128,2048]{1,0:T(8,128)(2,1)} %get-tuple-element.212.own_ref.dy_ref, f32[2,2048]{1,0:T(2,128)} %get-tuple-element.206.gain_ref.norm_ref, ...), custom_call_target="tpu_custom_call" | custom-call | flops 1576960 | bytes 7372800 | tf_op jit(solution)/shard_map/pallas_call | solution.py:185
  203.4 8.6 %shard_map.217 = (bf16[128,512]{1,0:T(8,128)(2,1)}, f32[1536,128]{1,0:T(8,128)}, f32[1536,128]{1,0:T(8,128)}) custom-call(s32[1]{0:T(128)} %bitcast.at_ref.place_ref.core_ref.refs_0_, bf16[512,512]{1,0:T(8,128)(2,1)} %get-tuple-element.201.q_ref.refs_1_, bf16[2048,1920]{1,0:T(8,128)(2,1)} %all-gather.3.cloned.1.call-done.w_ref.right_ref.refs_2_, ...), custom_call_target="tpu_custom_call" | custom-call | flops 1509949440 | bytes 6291456 | tf_op jit(solution)/shard_map/pallas_call | solution.py:700
  217.2 13.4 %shard_map.218 = (bf16[256,512]{1,0:T(8,128)(2,1)}, f32[1536,128]{1,0:T(8,128)}, f32[1536,128]{1,0:T(8,128)}) custom-call(s32[1]{0:T(128)} %bitcast.at_ref.place_ref.core_ref.refs_0_, bf16[512,512]{1,0:T(8,128)(2,1)} %get-tuple-element.201.q_ref.refs_1_, bf16[2048,1920]{1,0:T(8,128)(2,1)} %all-gather.3.cloned.1.call-done.w_ref.right_ref.refs_2_, ...), custom_call_target="tpu_custom_call" | custom-call | flops 3019898880 | bytes 6291456 | tf_op jit(solution)/shard_map/pallas_call | solution.py:700
  234.7 8.7 %shard_map.219 = (bf16[128,512]{1,0:T(8,128)(2,1)}, bf16[512,128]{1,0:T(8,128)(2,1)}, bf16[512,128]{1,0:T(8,128)(2,1)}, f32[512,128]{1,0:T(8,128)}) custom-call(s32[1]{0:T(128)} %bitcast.at_ref.place_ref.core_ref.refs_0_, bf16[512,512]{1,0:T(8,128)(2,1)} %get-tuple-element.201.q_ref.refs_1_, ...), custom_call_target="tpu_custom_call" | custom-call | flops 1509949440 | bytes 6291456 | tf_op jit(solution)/shard_map/pallas_call | solution.py:700
  246.0 7.6 %shard_map.220 = (bf16[1024,1024]{1,0:T(8,128)(2,1)}, bf16[1024,1024]{1,0:T(8,128)(2,1)}) custom-call(s32[1]{0:T(128)} %bitcast.at_ref.place_ref.core_ref.refs_0_, bf16[512,2048]{1,0:T(8,128)(2,1)} %get-tuple-element.188.x_ref, bf16[128,2048]{1,0:T(8,128)(2,1)} %get-tuple-element.259.refs_11_.dh0, bf16[128,2048]{1,0:T(8,128)(2,1)} %collective-permute-done.34.refs_11_.dh1, ...), custom_call_target="tpu_custom_call" | custom-call | flops 2147483648 | bytes 10485760 | tf_op jit(solution)/shard_map/pallas_call | solution.py:1007
  256.3 7.8 %shard_map.221 = (bf16[1024,128]{1,0:T(8,128)(2,1)}, bf16[1024,128]{1,0:T(8,128)(2,1)}, bf16[512,2048]{1,0:T(8,128)(2,1)}, f32[16,256]{1,0:T(8,128)}) custom-call(s32[1]{0:T(128)} %bitcast.at_ref.place_ref.core_ref.refs_0_, bf16[512,2048]{1,0:T(8,128)(2,1)} %get-tuple-element.188.x_ref, bf16[2048,640]{1,0:T(8,128)(2,1)} %get-tuple-element.189.w_ref, ...), custom_call_target="tpu_custom_call" | custom-call | flops 1610612736 | bytes 10485760 | tf_op jit(solution)/shard_map/pallas_call | solution.py:1093
  273.9 5.2 %shard_map.223 = (bf16[272,640]{1,0:T(8,128)(2,1)}, bf16[272,640]{1,0:T(8,128)(2,1)}, bf16[272,640]{1,0:T(8,128)(2,1)}, bf16[272,640]{1,0:T(8,128)(2,1)}, bf16[2...) custom-call(s32[1]{0:T(128)} %bitcast.at_ref.place_ref.core_ref.refs_0_, ...), custom_call_target="tpu_custom_call" | custom-call | flops 2359296 | bytes 7077888 | tf_op jit(solution)/shard_map/pallas_call | solution.py:294
  290.2 7.0 %collective-permute-start.49 = (bf16[272,640]{1,0:T(8,128)(2,1)}, bf16[272,640]{1,0:T(8,128)(2,1)}, u32[]{:S(2)}, u32[]{:S(2)}) collective-permute-start(bf16[272,640]{1,0:T(8,128)(2,1)} %get-tuple-element.298), channel_id=1, source_target_pairs={{0,6},{2,0},{4,2},{6,4},{1,7},{3,1},{5,3},{7,5},{8,14},{10,8},{12,... | collective-permute-start | bytes 1044488 | tf_op jit(solution)/shard_map/ppermute | solution.py:36
  299.4 3.9 %collective-permute-done.48.refs_2_ = bf16[272,640]{1,0:T(8,128)(2,1)S(1)} collective-permute-done((bf16[272,640]{1,0:T(8,128)(2,1)}, bf16[272,640]{1,0:T(8,128)(2,1)S(1)}, u32[]{:S(2)}, u32[]{:S(2)}) %collective-permute-start.48) | collective-permute-done | bytes 348192 | tf_op jit(solution)/shard_map/ppermute | solution.py:36
  (240 shorter events, 139.3 us)
Async XLA Ops:
  7.2 69.2 %all-gather.3.cloned.1.call-start = ((), (), s32[]{:S(2)}) async-start(), calls=%async_computation.2 | async-start | bytes 8110080 | tf_op jit(solution)/shard_map/all_gather | solution.py:1128
  9.0 139.9 %all-gather.5.cloned.1.call-start = ((), (), s32[]{:S(2)}) async-start(), calls=%async_computation.3 | async-start | bytes 11894784 | tf_op jit(solution)/shard_map/all_gather | solution.py:1131
  10.9 286.3 %reduce-scatter.3.cloned.1.call-start = ((), (), s32[]{:S(2)}) async-start(), calls=%async_computation.4 | async-start | bytes 9191424 | tf_op jit(solution)/shard_map/reduce_scatter | solution.py:1196
  21.6 15.3 %collective-permute-start.7 = (bf16[128,2048]{1,0:T(8,128)(2,1)}, bf16[128,2048]{1,0:T(8,128)(2,1)S(1)}, u32[]{:S(2)}, u32[]{:S(2)}) collective-permute-start(bf16[128,2048]{1,0:T(8,128)(2,1)} %get-tuple-element.176.refs_0_), channel_id=1, source_target_pairs={{0,32},{32,64},{64,96},{96,0},{1,33},{33,65},{65,97},{97,1},{2,34}... | collective-permute-start | bytes 1572872 | tf_op jit(solution)/shard_map/ppermute | solution.py:36
  29.1 18.5 %collective-permute-start.5 = (bf16[256,640]{1,0:T(8,128)(2,1)S(1)}, bf16[256,640]{1,0:T(8,128)(2,1)S(1)}, u32[]{:S(2)}, u32[]{:S(2)}) collective-permute-start(bf16[256,640]{1,0:T(8,128)(2,1)S(1)} %pad_maximum_fusion.1.refs_5_.refs_0_), channel_id=1, source_target_pairs={{0,16},{8,24},{16,0},{24,8},{1,17},{9,25},{17,1},{25,9},{2,18},{10... | collective-permute-start | bytes 983048 | tf_op jit(solution)/shard_map/ppermute | solution.py:36
  32.0 15.6 %collective-permute-start.4 = (bf16[256,640]{1,0:T(8,128)(2,1)S(1)}, bf16[256,640]{1,0:T(8,128)(2,1)S(1)}, u32[]{:S(2)}, u32[]{:S(2)}) collective-permute-start(bf16[256,640]{1,0:T(8,128)(2,1)S(1)} %pad_maximum_fusion.1.refs_5_.refs_0_), channel_id=1, source_target_pairs={{0,24},{8,0},{16,8},{24,16},{1,25},{9,1},{17,9},{25,17},{2,26},{10... | collective-permute-start | bytes 983048 | tf_op jit(solution)/shard_map/ppermute | solution.py:36
  57.2 25.3 %collective-permute-start.18 = (bf16[128,2048]{1,0:T(8,128)(2,1)}, bf16[128,2048]{1,0:T(8,128)(2,1)S(1)}, u32[]{:S(2)}, u32[]{:S(2)}) collective-permute-start(bf16[128,2048]{1,0:T(8,128)(2,1)} %bitcast.24), channel_id=1, source_target_pairs={{0,32},{32,64},{64,96},{96,0},{1,33},{33,65},{65,97},{97,1},{2,34}... | collective-permute-start | bytes 1572872 | tf_op jit(solution)/shard_map/ppermute | solution.py:36
  57.6 27.1 %collective-permute-start.17 = (bf16[128,2048]{1,0:T(8,128)(2,1)}, bf16[128,2048]{1,0:T(8,128)(2,1)}, u32[]{:S(2)}, u32[]{:S(2)}) collective-permute-start(bf16[128,2048]{1,0:T(8,128)(2,1)} %bitcast.25), channel_id=1, source_target_pairs={{0,64},{32,96},{64,0},{96,32},{1,65},{33,97},{65,1},{97,33},{2,66}... | collective-permute-start | bytes 1572872 | tf_op jit(solution)/shard_map/ppermute | solution.py:36
  61.2 23.5 %collective-permute-start.16 = (bf16[128,2048]{1,0:T(8,128)(2,1)}, bf16[128,2048]{1,0:T(8,128)(2,1)}, u32[]{:S(2)}, u32[]{:S(2)}) collective-permute-start(bf16[128,2048]{1,0:T(8,128)(2,1)} %bitcast.26), channel_id=1, source_target_pairs={{0,96},{32,0},{64,32},{96,64},{1,97},{33,1},{65,33},{97,65},{2,98}... | collective-permute-start | bytes 1572872 | tf_op jit(solution)/shard_map/ppermute | solution.py:36
  106.9 41.9 %collective-permute-start.28 = (bf16[512,1024]{1,0:T(8,128)(2,1)}, bf16[512,1024]{1,0:T(8,128)(2,1)}, u32[]{:S(2)}, u32[]{:S(2)}) collective-permute-start(bf16[512,1024]{1,0:T(8,128)(2,1)} %get-tuple-element.222), channel_id=1, source_target_pairs={{0,1},{1,0},{2,3},{3,2},{4,5},{5,4},{6,7},{7,6},{8,9},{9,8},{10,11... | collective-permute-start | bytes 3145736 | tf_op jit(solution)/shard_map/ppermute | solution.py:36
  121.8 27.1 %collective-permute-start.22 = (bf16[64,2048]{1,0:T(8,128)(2,1)}, bf16[64,2048]{1,0:T(8,128)(2,1)S(1)}, u32[]{:S(2)}, u32[]{:S(2)}) collective-permute-start(bf16[64,2048]{1,0:T(8,128)(2,1)} %get-tuple-element.213.refs_1_), channel_id=1, source_target_pairs={{0,96},{32,0},{64,32},{96,64},{1,97},{33,1},{65,33},{97,65},{2,98}... | collective-permute-start | bytes 786440 | tf_op jit(solution)/shard_map/ppermute | solution.py:36
  122.8 26.0 %collective-permute-start.27 = (bf16[64,2048]{1,0:T(8,128)(2,1)}, bf16[64,2048]{1,0:T(8,128)(2,1)}, u32[]{:S(2)}, u32[]{:S(2)}) collective-permute-start(bf16[64,2048]{1,0:T(8,128)(2,1)} %get-tuple-element.214.refs_2_), channel_id=1, source_target_pairs={{0,32},{32,64},{64,96},{96,0},{1,33},{33,65},{65,97},{97,1},{2,34}... | collective-permute-start | bytes 786440 | tf_op jit(solution)/shard_map/ppermute | solution.py:36
  129.2 19.7 %collective-permute-start.26 = (bf16[64,2048]{1,0:T(8,128)(2,1)S(1)}, bf16[64,2048]{1,0:T(8,128)(2,1)}, u32[]{:S(2)}, u32[]{:S(2)}) collective-permute-start(bf16[64,2048]{1,0:T(8,128)(2,1)S(1)} %collective-permute-done.24.refs_4_), channel_id=1, source_target_pairs={{0,96},{32,0},{64,32},{96,64},{1,97},{33,1},{65,33},{97,65},{2,98}... | collective-permute-start | bytes 786440 | tf_op jit(solution)/shard_map/ppermute | solution.py:36
  132.5 16.4 %collective-permute-start.25 = (bf16[64,2048]{1,0:T(8,128)(2,1)S(1)}, bf16[64,2048]{1,0:T(8,128)(2,1)}, u32[]{:S(2)}, u32[]{:S(2)}) collective-permute-start(bf16[64,2048]{1,0:T(8,128)(2,1)S(1)} %collective-permute-done.23.refs_7_), channel_id=1, source_target_pairs={{0,32},{32,64},{64,96},{96,0},{1,33},{33,65},{65,97},{97,1},{2,34}... | collective-permute-start | bytes 786440 | tf_op jit(solution)/shard_map/ppermute | solution.py:36
  167.8 27.1 %collective-permute-start.31 = (bf16[128,2048]{1,0:T(8,128)(2,1)}, bf16[128,2048]{1,0:T(8,128)(2,1)S(1)}, u32[]{:S(2)}, u32[]{:S(2)}) collective-permute-start(bf16[128,2048]{1,0:T(8,128)(2,1)} %get-tuple-element.235), channel_id=1, source_target_pairs={{0,32},{32,64},{64,96},{96,0},{1,33},{33,65},{65,97},{97,1},{2,34}... | collective-permute-start | bytes 1572872 | tf_op jit(solution)/shard_map/ppermute | solution.py:36
  167.8 27.2 %collective-permute-start.32 = (bf16[128,2048]{1,0:T(8,128)(2,1)}, bf16[128,2048]{1,0:T(8,128)(2,1)}, u32[]{:S(2)}, u32[]{:S(2)}) collective-permute-start(bf16[128,2048]{1,0:T(8,128)(2,1)} %get-tuple-element.236), channel_id=1, source_target_pairs={{0,96},{32,0},{64,32},{96,64},{1,97},{33,1},{65,33},{97,65},{2,98}... | collective-permute-start | bytes 1572872 | tf_op jit(solution)/shard_map/ppermute | solution.py:36
  171.4 24.5 %collective-permute-start.33 = (bf16[128,2048]{1,0:T(8,128)(2,1)}, bf16[128,2048]{1,0:T(8,128)(2,1)}, u32[]{:S(2)}, u32[]{:S(2)}) collective-permute-start(bf16[128,2048]{1,0:T(8,128)(2,1)} %get-tuple-element.237), channel_id=1, source_target_pairs={{0,64},{32,96},{64,0},{96,32},{1,65},{33,97},{65,1},{97,33},{2,66}... | collective-permute-start | bytes 1572872 | tf_op jit(solution)/shard_map/ppermute | solution.py:36
  196.0 123.8 %reduce-scatter.5.cloned.1.call-start = ((), (), s32[]{:S(2)}) async-start(), calls=%async_computation.5 | async-start | bytes 2621440 | tf_op jit(solution)/shard_map/reduce_scatter | solution.py:1234
  215.0 15.6 %collective-permute-start.36 = (bf16[128,2048]{1,0:T(8,128)(2,1)S(1)}, bf16[128,2048]{1,0:T(8,128)(2,1)}, u32[]{:S(2)}, u32[]{:S(2)}) collective-permute-start(bf16[128,2048]{1,0:T(8,128)(2,1)S(1)} %copy-done.11), channel_id=1, source_target_pairs={{0,64},{32,96},{64,0},{96,32},{1,65},{33,97},{65,1},{97,33},{2,66}... | collective-permute-start | bytes 1572872 | tf_op jit(solution)/shard_map/ppermute | solution.py:36
  230.6 25.0 %collective-permute-start.39 = (bf16[128,2048]{1,0:T(8,128)(2,1)}, bf16[128,2048]{1,0:T(8,128)(2,1)S(1)}, u32[]{:S(2)}, u32[]{:S(2)}) collective-permute-start(bf16[128,2048]{1,0:T(8,128)(2,1)} %get-tuple-element.275), channel_id=1, source_target_pairs={{0,32},{32,64},{64,96},{96,0},{1,33},{33,65},{65,97},{97,1},{2,34}... | collective-permute-start | bytes 1572872 | tf_op jit(solution)/shard_map/ppermute | solution.py:36
  232.6 23.0 %collective-permute-start.40 = (bf16[128,2048]{1,0:T(8,128)(2,1)}, bf16[128,2048]{1,0:T(8,128)(2,1)}, u32[]{:S(2)}, u32[]{:S(2)}) collective-permute-start(bf16[128,2048]{1,0:T(8,128)(2,1)} %get-tuple-element.276), channel_id=1, source_target_pairs={{0,96},{32,0},{64,32},{96,64},{1,97},{33,1},{65,33},{97,65},{2,98}... | collective-permute-start | bytes 1572872 | tf_op jit(solution)/shard_map/ppermute | solution.py:36
  233.9 21.7 %collective-permute-start.41 = (bf16[128,2048]{1,0:T(8,128)(2,1)}, bf16[128,2048]{1,0:T(8,128)(2,1)}, u32[]{:S(2)}, u32[]{:S(2)}) collective-permute-start(bf16[128,2048]{1,0:T(8,128)(2,1)} %get-tuple-element.277), channel_id=1, source_target_pairs={{0,64},{32,96},{64,0},{96,32},{1,65},{33,97},{65,1},{97,33},{2,66}... | collective-permute-start | bytes 1572872 | tf_op jit(solution)/shard_map/ppermute | solution.py:36
  281.7 17.6 %collective-permute-start.51 = (bf16[256,512]{1,0:T(8,128)(2,1)}, bf16[256,512]{1,0:T(8,128)(2,1)S(1)}, u32[]{:S(2)}, u32[]{:S(2)}) collective-permute-start(bf16[256,512]{1,0:T(8,128)(2,1)} %get-tuple-element.301), channel_id=1, source_target_pairs={{0,16},{8,24},{16,0},{24,8},{1,17},{9,25},{17,1},{25,9},{2,18},{10... | collective-permute-start | bytes 786440 | tf_op jit(solution)/shard_map/ppermute | solution.py:36
  287.5 15.7 %collective-permute-start.48 = (bf16[272,640]{1,0:T(8,128)(2,1)}, bf16[272,640]{1,0:T(8,128)(2,1)S(1)}, u32[]{:S(2)}, u32[]{:S(2)}) collective-permute-start(bf16[272,640]{1,0:T(8,128)(2,1)} %get-tuple-element.297), channel_id=1, source_target_pairs={{0,4},{2,6},{4,0},{6,2},{1,5},{3,7},{5,1},{7,3},{8,12},{10,14},{12... | collective-permute-start | bytes 1044488 | tf_op jit(solution)/shard_map/ppermute | solution.py:36
  (84 other events, 621.3 us)
Sparse Core Ops, SparseCore 0:
  10.3 66.0 all-gather.2
  79.3 60.1 all-gather.4
  196.1 86.6 reduce-scatter.2
  285.1 29.2 reduce-scatter.4
